TPU v7x, 32 devices: a whole 2x2x4 slice. The times are simulated.
32 devices in a mesh: groups: 2 (over x), wide: 16 (over z, y, core).
Axes of the slice: x: 2, y: 2, z: 4, core: 2. Of those that a mesh axis runs over, the one named last changes fastest.
Arguments:
- key_mant: bfloat16 [32768, 128], P(('groups', 'wide')), parts along dimension 0, may hold values from -8 to 8
- scale_exp: int32 [1024], P(('groups', 'wide')), parts along dimension 0, may hold values from -1 to 1
- values: bfloat16 [32768, 128], P(('groups', 'wide')), parts along dimension 0, may hold values from -6 to 6
- queries: bfloat16 [2048, 128], P('groups'), parts along dimension 0, may hold values from -8 to 8
- compact_index: int32 [1024], P('groups'), parts along dimension 0, may hold values from 0 to 15615, as said below
- shard_lengths: int32 [32], P('groups'), parts along dimension 0, may hold values from 256 to 1024, as said below
Outputs:
- key_weights: float32 [1024], P('groups'), parts along dimension 0
- compact_values: float32 [1024, 128], P('groups'), parts along dimension 0
There are 2 independent parts, one for each index of `groups`. A program takes and returns all parts, laid end to end along the dimension named above; each array names one. Nothing has to cross between parts.
Inputs may be any that keep to these rules, and one draw needn't show every extreme that they name: `compact_index`: distinct; each lies among the first 256 positions of its shard of 1024 tokens. `shard_lengths`: some shard is full in every draw.
All inputs are finite; a program needn't handle non-finite values. Where the computation divides by a largest or mean magnitude, that divisor is 1e-20 or more.
Results may differ from a plain program's by a relative error of at most 0.0003.
Values may be sent and summed in bfloat16 or wider, within the bound.
No kernel may reach another device: no remote copies, remote signals or barrier semaphores. Data moves between devices by JAX's collectives and lax.ppermute only.
A program may use at most 256 MiB of HBM per device.

v0:
```python
import jax
import jax.numpy as jnp
from jax import lax
from jax.sharding import PartitionSpec as P

DH = 128
NQ = 1024
CTX_DEV = 1024
M = 512
KBLK = 256
QB = 32
NNLS_STEPS = 8
NS_ITERS = 9


ridge_weight = 4.0
nnls_ridge = 0.1
floor_value = -1e30


def merged(value, axis, join):
    pieces = jax.tree.map(lambda part: lax.all_gather(part, axis), value)
    head = jax.tree.map(lambda part: part[0], pieces)
    tail = jax.tree.map(lambda part: part[1:], pieces)
    total, _ = lax.scan(lambda total, section: (join(total, section), None), head, tail)
    return total


def dequantize(key_mant, scale_exp):
    factor = jnp.repeat(jnp.exp2(scale_exp.astype(jnp.float32)), QB)
    return (key_mant.astype(jnp.float32) * factor[:, None]).astype(jnp.bfloat16)


def across(left, right):
    return lax.dot_general(left, right, (((0,), (0,)), ((), ())), precision=lax.Precision.HIGHEST)


def attend_blocks(
    queries, keys_cat, values_cat, block_first, block_last, low_blocks, low_len, high_len
):
    score_scale = DH ** (-0.5)
    offsets = jnp.arange(KBLK, dtype=jnp.int32)

    def block_step(number, state):
        row_max, row_mass, numerator = state
        in_low = number < low_blocks
        within = jnp.where(in_low, number, number - low_blocks) * KBLK
        row_start = jnp.where(in_low, within, CTX_DEV + within)
        length = jnp.where(in_low, low_len, high_len)
        key_block = lax.dynamic_slice_in_dim(keys_cat, row_start, KBLK, 0)
        value_block = lax.dynamic_slice_in_dim(values_cat, row_start, KBLK, 0)
        scores = (
            lax.dot_general(
                queries, key_block, (((1,), (1,)), ((), ())), preferred_element_type=jnp.float32
            )
            * score_scale
        )
        live_mask = within + offsets < length
        scores = jnp.where(live_mask[None, :], scores, floor_value)
        new_max = jnp.maximum(row_max, jnp.max(scores, axis=1))
        rescale = jnp.exp(row_max - new_max)
        attn = jnp.where(live_mask[None, :], jnp.exp(scores - new_max[:, None]), 0.0)
        row_mass = row_mass * rescale + jnp.sum(attn, axis=1)
        numerator = numerator * rescale[:, None] + jnp.dot(
            attn.astype(jnp.bfloat16), value_block, preferred_element_type=jnp.float32
        )
        return (new_max, row_mass, numerator)

    initial = (
        jnp.full((NQ,), floor_value, jnp.float32),
        jnp.zeros((NQ,), jnp.float32),
        jnp.zeros((NQ, DH), jnp.float32),
    )
    return lax.fori_loop(block_first, block_last, block_step, initial)


def combine_partials(first_part, second_part):
    max_first, mass_first, numer_first = first_part
    max_second, mass_second, numer_second = second_part
    joint_max = jnp.maximum(max_first, max_second)
    scale_first = jnp.exp(max_first - joint_max)
    scale_second = jnp.exp(max_second - joint_max)
    joint_mass = mass_first * scale_first + mass_second * scale_second
    joint_numer = numer_first * scale_first[:, None] + numer_second * scale_second[:, None]
    return (joint_max, joint_mass, joint_numer)


def per_device(key_mant, scale_exp, values, queries, compact_index, shard_lengths):
    highest = lax.Precision.HIGHEST
    wide_count = lax.axis_size("wide")
    my_index = lax.axis_index("wide")
    keys = dequantize(key_mant, scale_exp)
    own_len = lax.dynamic_index_in_dim(shard_lengths, my_index, 0, keepdims=False)
    local_pos = compact_index - my_index * CTX_DEV
    inside = (local_pos >= 0) & (local_pos < CTX_DEV)
    clipped = jnp.clip(local_pos, 0, CTX_DEV - 1)
    picked_keys = jnp.where(inside[:, None], keys[clipped].astype(jnp.float32), 0.0)
    picked_values = jnp.where(inside[:, None], values[clipped].astype(jnp.float32), 0.0)
    compact_keys, prior_values = lax.psum((picked_keys, picked_values), "wide")
    compact_keys = compact_keys.astype(jnp.bfloat16)
    own_blocks = (own_len + KBLK - 1) // KBLK
    keys_cat, values_cat = (keys, values)
    low_len, high_len, low_blocks = (own_len, own_len, own_blocks)
    block_first = jnp.int32(0)
    row_max, row_mass, numerator = attend_blocks(
        queries, keys_cat, values_cat, block_first, own_blocks, low_blocks, low_len, high_len
    )
    row_count = NQ // wide_count
    row_begin = my_index * row_count
    row_max, row_mass, numerator = merged((row_max, row_mass, numerator), "wide", combine_partials)
    own_max = lax.dynamic_slice_in_dim(row_max, row_begin, row_count, 0)
    own_mass = lax.dynamic_slice_in_dim(row_mass, row_begin, row_count, 0)
    own_numer = lax.dynamic_slice_in_dim(numerator, row_begin, row_count, 0)
    own_queries = lax.dynamic_slice_in_dim(queries, row_begin, row_count, 0)
    outputs = own_numer / own_mass[:, None]
    score_scale = DH ** (-0.5)
    features = jnp.exp(
        lax.dot_general(
            own_queries, compact_keys, (((1,), (1,)), ((), ())), preferred_element_type=jnp.float32
        )
        * score_scale
        - own_max[:, None]
    )
    live_total = jnp.sum(shard_lengths).astype(jnp.float32)
    target = own_mass * (M / live_total)
    key_weights = jnp.ones((M,), jnp.float32)

    def local_gradient(weights_now):
        return across(features, jnp.dot(features, weights_now, precision=highest) - target)

    gradient, frobenius = lax.psum(
        (local_gradient(key_weights), jnp.sum(features * features)), "wide"
    )
    damping = nnls_ridge * (frobenius / M + 1e-06)
    stepsize = 1.0 / (frobenius + damping)
    key_weights = jnp.maximum(key_weights - stepsize * (gradient + damping * key_weights), 0.0)
    for number in range(NNLS_STEPS - 1):
        gradient = lax.psum(local_gradient(key_weights), "wide")
        key_weights = jnp.maximum(key_weights - stepsize * (gradient + damping * key_weights), 0.0)
    attend = features * key_weights[None, :] / target[:, None]
    attend_gram, attend_out = lax.psum((across(attend, attend), across(attend, outputs)), "wide")
    ridge = ridge_weight * (jnp.trace(attend_gram) / M + 1e-06)
    identity = jnp.eye(M, dtype=jnp.float32)
    system = attend_gram + ridge * identity
    right_side = attend_out + ridge * prior_values
    start_inverse = identity / jnp.max(jnp.sum(jnp.abs(system), axis=1))

    def newton_step(number, inverse):
        return 2.0 * inverse - jnp.dot(
            jnp.dot(inverse, system, precision=highest), inverse, precision=highest
        )

    inverse = lax.fori_loop(0, NS_ITERS, newton_step, start_inverse)
    compact_values = jnp.dot(inverse, right_side, precision=highest)
    return (key_weights, compact_values)


def solution(mesh):
    placed = (
        P(("groups", "wide"), None),
        P(("groups", "wide")),
        P(("groups", "wide"), None),
        P("groups", None),
        P("groups"),
        P("groups"),
    )
    return jax.shard_map(
        per_device,
        mesh=mesh,
        in_specs=placed,
        out_specs=(P("groups"), P("groups", None)),
        check_vma=False,
    )
```

profile of v0, /device:TPU:0, one launch (start us, length us, event | category | flops | bytes accessed | tf_op | source)
XLA Modules:
  0.0 550.3 jit_solution(11949710310065845343)
XLA Ops:
  7.2 1.2 dynamic_slice.34
  9.9 1.2 multiply_convert_fusion
  11.2 7.3 %while.41 = (s32[]{:T(128)}, f32[1024]{0:T(1024)S(1)}, f32[1024]{0:T(1024)S(1)}, f32[1024,128]{1,0:T(8,128)S(1)}, s32[]{:T(128)}, /*index=5*/s32[]{:T(128)}, bf1...) while((s32[]{:T(128)}, f32[1024]{0:T(1024)S(1)}, ...), condition=%wide.region_4.5_spmd.clone, body=%wide.region_1.4_spmd.clone.sunk | while | flops 136841728 | bytes 4654582 | solution.py:74
  11.9 1.3 fusion.120
  13.4 1.4 convolution_add_fusion.2
  15.5 1.3 fusion.120
  17.0 1.4 convolution_add_fusion.2
  19.4 24.5 %all-gather = f32[16384]{0:T(1024)S(1)} all-gather(f32[1024]{0:T(1024)S(1)} %get-tuple-element.113), channel_id=2, replica_groups=mesh['groups'=2,'wide'=16] {'wide'}, dimensions={0}, use_global_device_ids=true | all-gather | bytes 69632 | tf_op jit(solution)/shard_map/all_gather | solution.py:22
  43.9 19.4 %all-gather.1 = f32[16384]{0:T(1024)S(1)} all-gather(f32[1024]{0:T(1024)S(1)} %get-tuple-element.114), channel_id=3, replica_groups=mesh['groups'=2,'wide'=16] {'wide'}, dimensions={0}, use_global_device_ids=true | all-gather | bytes 69632 | tf_op jit(solution)/shard_map/all_gather | solution.py:22
  63.4 1.3 gather_fusion
  64.7 2.0 gather_fusion.1
  67.5 0.8 convert_select_fusion
  69.0 62.5 %all-reduce.6 = bf16[512,128]{1,0:T(8,128)(2,1)S(1)} all-reduce(f32[512,128]{1,0:T(8,128)S(1)} %get-tuple-element.199), channel_id=1, replica_groups=mesh['groups'=2,'wide'=16] {'wide'}, use_global_device_ids=true, to_apply=%region_0.1 | all-reduce | flops 65536 | bytes 393216 | tf_op jit(solution)/shard_map/psum | solution.py:99
  131.6 5.5 %slice.39 = f32[15360,128]{1,0:T(8,128)} slice(f32[16384,128]{1,0:T(8,128)} %all-gather.5.cloned.1.call-done), slice={[1024:16384], [0:128]} | slice | bytes 15728640 | tf_op jit(solution)/shard_map/slice | solution.py:24
  137.1 23.4 %while.39 = (s32[]{:T(128)}, f32[1024]{0:T(1024)S(1)}, f32[1024]{0:T(1024)S(1)}, f32[1024,128]{1,0:T(8,128)S(1)}, f32[15,1024]{1,0:T(8,128)S(1)}, /*index=5*/f32...) while((s32[]{:T(128)}, f32[1024]{0:T(1024)S(1)}, f32[1024]{0:T(1024)S(1)}, f32[1024,128]{1,0:T(8,128)S(1)}, ...), condition=%wide.region_6.7_spmd, body=%wide.region_5.6_spmd.sunk | while | flops 399362 | bytes 1630301 | solution.py:25
  137.1 1.5 fusion.110
  138.7 1.5 fusion.110
  140.3 1.5 fusion.110
  141.8 1.5 fusion.110
  143.4 1.5 fusion.110
  144.9 1.5 fusion.110
  146.5 1.5 fusion.110
  148.1 1.5 fusion.110
  149.6 1.5 fusion.110
  151.2 1.5 fusion.110
  152.7 1.5 fusion.110
  154.3 1.5 fusion.110
  155.8 1.5 fusion.110
  157.4 1.5 fusion.110
  159.0 1.5 fusion.110
  160.6 1.5 multiply_reduce_fusion
  162.6 30.1 %all-reduce = (f32[512]{0:T(512)S(1)}, f32[]{:T(128)}) all-reduce(f32[512]{0:T(512)S(1)} %bitcast.150, f32[]{:T(128)} %get-tuple-element.200), channel_id=1, replica_groups=mesh['groups'=2,'wide'=16] {'wide'}, use_global_device_ids=true, to_apply=%region_10.11 | all-reduce | flops 513 | bytes 4104 | tf_op jit(solution)/shard_map/psum | solution.py:131
  194.4 29.5 %psum.94 = f32[512]{0:T(512)S(1)} all-reduce(f32[512]{0:T(512)S(1)} %bitcast.151), channel_id=1, replica_groups=mesh['groups'=2,'wide'=16] {'wide'}, use_global_device_ids=true, to_apply=%region_11.12 | all-reduce | flops 512 | bytes 4096 | tf_op jit(solution)/shard_map/psum | solution.py:138
  224.4 29.5 %psum.95 = f32[512]{0:T(512)S(1)} all-reduce(f32[512]{0:T(512)S(1)} %bitcast.152), channel_id=1, replica_groups=mesh['groups'=2,'wide'=16] {'wide'}, use_global_device_ids=true, to_apply=%region_12.13 | all-reduce | flops 512 | bytes 4096 | tf_op jit(solution)/shard_map/psum | solution.py:138
  254.3 29.5 %psum.96 = f32[512]{0:T(512)S(1)} all-reduce(f32[512]{0:T(512)S(1)} %bitcast.153), channel_id=1, replica_groups=mesh['groups'=2,'wide'=16] {'wide'}, use_global_device_ids=true, to_apply=%region_13.14 | all-reduce | flops 512 | bytes 4096 | tf_op jit(solution)/shard_map/psum | solution.py:138
  284.2 29.5 %psum.97 = f32[512]{0:T(512)S(1)} all-reduce(f32[512]{0:T(512)S(1)} %bitcast.154), channel_id=1, replica_groups=mesh['groups'=2,'wide'=16] {'wide'}, use_global_device_ids=true, to_apply=%region_14.15 | all-reduce | flops 512 | bytes 4096 | tf_op jit(solution)/shard_map/psum | solution.py:138
  314.1 29.5 %psum.98 = f32[512]{0:T(512)S(1)} all-reduce(f32[512]{0:T(512)S(1)} %bitcast.155), channel_id=1, replica_groups=mesh['groups'=2,'wide'=16] {'wide'}, use_global_device_ids=true, to_apply=%region_15.16 | all-reduce | flops 512 | bytes 4096 | tf_op jit(solution)/shard_map/psum | solution.py:138
  344.0 29.5 %psum.99 = f32[512]{0:T(512)S(1)} all-reduce(f32[512]{0:T(512)S(1)} %bitcast.156), channel_id=1, replica_groups=mesh['groups'=2,'wide'=16] {'wide'}, use_global_device_ids=true, to_apply=%region_16.17 | all-reduce | flops 512 | bytes 4096 | tf_op jit(solution)/shard_map/psum | solution.py:138
  373.9 29.7 %psum.100 = f32[512]{0:T(512)S(1)} all-reduce(f32[512]{0:T(512)S(1)} %bitcast.157), channel_id=1, replica_groups=mesh['groups'=2,'wide'=16] {'wide'}, use_global_device_ids=true, to_apply=%region_17.18 | all-reduce | flops 512 | bytes 4096 | tf_op jit(solution)/shard_map/psum | solution.py:138
  403.5 2.1 fusion.45
  405.7 1.4 fusion.40
  407.1 95.0 %all-reduce.5.cloned.1.call-done = (f32[512,512]{1,0:T(8,128)}, f32[512,128]{1,0:T(8,128)}, f32[512,128]{1,0:T(8,128)}) async-done(((f32[512,512]{1,0:T(8,128)}, f32[512,128]{1,0:T(8,128)}, f32[512,128]{1,0:T(8,128)}), (f32[512,512]{1,0:T(8,128)}, f32[512,128]{1,0:T(8,128)}, f32[512,128]{1,0:T(8,128)})) %all-reduce.5.cloned.1.call-update) | async-done | bytes 1572880 | tf_op jit(solution)/shard_map/psum | solution.py:141
  502.1 1.9 select_reduce_fusion
  504.7 1.4 abs_reduce_fusion
  507.5 34.2 %while.40 = (s32[]{:T(128)}, f32[512,512]{1,0:T(8,128)S(1)}, f32[512,512]{1,0:T(8,128)S(1)}, s32[]{:T(128)}) while((s32[]{:T(128)}, f32[512,512]{1,0:T(8,128)S(1)}, f32[512,512]{1,0:T(8,128)S(1)}, s32[]{:T(128)}) %tuple.75), condition=%wide.region_23.24_spmd, body=%wide.region_22.23_spmd.sunk | while | flops 3221749760 | bytes 8388661 | solution.py:153
  507.6 1.8 fusion.115
  509.5 1.8 convolution_subtract_fusion.2
  511.4 1.8 fusion.115
  513.3 1.8 convolution_subtract_fusion.2
  515.2 1.8 fusion.115
  517.1 1.8 convolution_subtract_fusion.2
  519.0 1.8 fusion.115
  520.9 1.8 convolution_subtract_fusion.2
  522.8 1.8 fusion.115
  524.7 1.8 convolution_subtract_fusion.2
  526.6 1.8 fusion.115
  528.5 1.8 convolution_subtract_fusion.2
  530.4 1.8 fusion.115
  532.3 1.8 convolution_subtract_fusion.2
  534.3 1.8 fusion.115
  536.1 1.8 convolution_subtract_fusion.2
  538.1 1.8 fusion.115
  539.9 1.8 convolution_subtract_fusion.2
  541.8 1.7 fusion.35
  (112 shorter events, 9.5 us)
Async XLA Ops:
  7.2 124.4 %all-gather.5.cloned.1.call-start = ((), (), s32[]{:S(2)}) async-start(), calls=%async_computation | async-start | bytes 8912896 | tf_op jit(solution)/shard_map/all_gather | solution.py:22
  11.2 52.2 %copy-start.4 = (s32[512]{0:T(512)S(1)}, s32[512]{0:T(512)}, u32[]{:S(2)}) copy-start(s32[512]{0:T(512)} %param.16) | copy-start | bytes 6148
  11.2 55.6 %copy-start.5 = (s32[16]{0:T(128)S(1)}, s32[16]{0:T(128)}, u32[]{:S(2)}) copy-start(s32[16]{0:T(128)} %param.17) | copy-start | bytes 196
  18.5 0.8 copy-start
  19.3 482.8 %all-reduce.5.cloned.1.call-start = ((), (), s32[]{:S(2)}) async-start(), calls=%async_computation.1 | async-start | bytes 3145728 | tf_op jit(solution)/shard_map/psum | solution.py:141
  131.6 5.6 %slice-start = ((f32[16384,128]{1,0:T(8,128)}), f32[1024,128]{1,0:T(8,128)S(1)}, s32[]{:S(2)}) async-start(f32[16384,128]{1,0:T(8,128)} %all-gather.5.cloned.1.call-done), calls=%async_computation.2 | async-start | bytes 1048576 | tf_op jit(solution)/shard_map/slice | solution.py:23
  403.5 104.0 %copy-start.3 = (f32[512]{0:T(512)}, f32[512]{0:T(512)S(1)}, u32[]{:S(2)}) copy-start(f32[512]{0:T(512)S(1)} %subtract_maximum_fusion) | copy-start | bytes 6148
  507.5 34.3 %copy-start.1 = (f32[512,128]{1,0:T(8,128)S(1)}, f32[512,128]{1,0:T(8,128)}, u32[]{:S(2)}) copy-start(f32[512,128]{1,0:T(8,128)} %get-tuple-element.182) | copy-start | bytes 786436
  507.5 34.3 %copy-start.2 = (f32[512,128]{1,0:T(8,128)S(1)}, f32[512,128]{1,0:T(8,128)}, u32[]{:S(2)}) copy-start(f32[512,128]{1,0:T(8,128)} %get-tuple-element.183) | copy-start | bytes 786436
Sparse Core Ops, SparseCore 0:
  19.5 84.2 all-gather.4
  407.2 94.8 all-reduce.4
where the time goes:
time: 553 us; the launch traced here: 550 us
  blocking collectives  343 us (62%)
  waiting for transfers between devices  95.1 us (17%)
  matrix products  48.6 us (9%)
  other arithmetic  32 us (6%)
  between operations  18.3 us (3%)
  local copies, waits for them, and re-layouts  12.2 us (2%)
    psum x7, blocking collectives, per_device(): gradient = lax.psum(local_gradient(key_weights), 'wide')  207 us
    psum x1, waiting for transfers between devices, per_device(): lax.psum((across(attend, attend), across(attend, outputs)), 'wide')  95 us
    psum x1, blocking collectives, per_device(): compact_keys, prior_values = lax.psum((picked_keys, picked_values), 'wide')  62.5 us
    all_gather x2, blocking collectives, merged(): pieces = jax.tree.map(lambda part: lax.all_gather(part, axis), value)  43.9 us
    psum x1, blocking collectives, per_device(): lax.psum((local_gradient(key_weights), jnp.sum(features * features)), 'wi...  30.1 us
    add x15, other arithmetic, combine_partials(): numer_first * scale_first[:, None] + numer_second * scale_second[:, None]  22.5 us
    dot_general x9, matrix products, newton_step(): jnp.dot(jnp.dot(inverse, system, precision=highest), inverse, precision=h...  16.6 us
    dot_general x9, matrix products, newton_step(): jnp.dot(inverse, system, precision=highest)  16.6 us
  transfers between devices with their start and end apart: 2, of which 1 were waited for; matrix products, arithmetic and copies ran while one was open for 1% of the time, Pallas kernels for 0%

commit v1 on v0

v1 whole, which is shorter than its diff:
```python
import jax
import jax.numpy as jnp
from jax import lax
from jax.experimental import pallas as pl
from jax.experimental.pallas import tpu as pltpu
from jax.sharding import PartitionSpec as P

DH = 128
NQ = 1024
M = 512
QB = 32
SELECT_FROM = 256
NNLS_STEPS = 8
NS_ITERS = 9
STAT_ROWS = 8

ridge_weight = 4.0
nnls_ridge = 0.1
floor_value = -1e30
EXP2_SCALE = DH ** (-0.5) * 1.4426950408889634

f32 = jnp.float32
bf16 = jnp.bfloat16
NN = (((1,), (0,)), ((), ()))
NT = (((1,), (1,)), ((), ()))
TN = (((0,), (0,)), ((), ()))


def params():
    return pltpu.CompilerParams(vmem_limit_bytes=48 * 1024 * 1024)


def vmem(count):
    return [pl.BlockSpec(memory_space=pltpu.VMEM)] * count


def smem(count):
    return [pl.BlockSpec(memory_space=pltpu.SMEM)] * count


def mm(left, right, dims):
    return lax.dot_general(left, right, dims, preferred_element_type=f32)


def split(x):
    high = x.astype(bf16)
    return high, (x - high.astype(f32)).astype(bf16)


def mm3(left, right, dims):
    return mm(left[0], right[0], dims) + (mm(left[0], right[1], dims) + mm(left[1], right[0], dims))


def stat_tile(row_max, row_mass):
    row = lax.broadcasted_iota(jnp.int32, (STAT_ROWS, row_max.shape[1]), 0)
    return jnp.where(row == 0, row_max, jnp.where(row == 1, row_mass, 0.0))


def attention_kernel(
    len_ref, exp_ref, index_ref, mant_ref, value_ref, query_ref,
    send_ref, keep_ref, send_rows_ref, keep_rows_ref, key_ref,
):
    ctx = mant_ref.shape[0]
    me = lax.axis_index("wide")
    core = lax.rem(me, 2)
    own_len = len_ref[me]
    for b in range(ctx // QB):
        exponent = exp_ref[b]
        factor = jnp.where(exponent > 0, 2.0, jnp.where(exponent < 0, 0.5, 1.0)).astype(f32)
        rows = pl.ds(b * QB, QB)
        key_ref[rows, :] = (mant_ref[rows, :].astype(f32) * factor).astype(bf16)
    half_m = M // 2
    position = lax.broadcasted_iota(jnp.int32, (SELECT_FROM, half_m), 0)
    for half, out in ((1 - core, send_rows_ref), (core, keep_rows_ref)):
        columns = pl.ds(pl.multiple_of(half * half_m, half_m), half_m)
        wanted = index_ref[:, columns] - me * ctx
        chosen = jnp.where(position == wanted, 1.0, 0.0).astype(bf16)
        out[:, :DH] = mm(chosen, key_ref[:SELECT_FROM, :], TN).astype(bf16)
        out[:, DH:] = mm(chosen, value_ref[:SELECT_FROM, :], TN).astype(bf16)
    chunk = 256
    half_q = NQ // 2
    dead = lax.broadcasted_iota(jnp.int32, (ctx, chunk), 0) >= own_len
    for half, out in ((1 - core, send_ref), (core, keep_ref)):
        for c in range(half_q // chunk):
            begin = pl.multiple_of(half * half_q + c * chunk, chunk)
            scores = mm(key_ref[...], query_ref[pl.ds(begin, chunk), :], NT)
            scores = jnp.where(dead, floor_value, scores)
            row_max = jnp.max(scores, axis=0, keepdims=True)
            attn = jnp.exp2((scores - row_max) * EXP2_SCALE)
            row_mass = jnp.sum(attn, axis=0, keepdims=True)
            out[:DH, pl.ds(c * chunk, chunk)] = mm(value_ref[...], attn.astype(bf16), TN)
            out[DH:, pl.ds(c * chunk, chunk)] = stat_tile(row_max, row_mass)


def joined(first, second):
    max_first, max_second = first[DH : DH + 1], second[DH : DH + 1]
    joint = jnp.maximum(max_first, max_second)
    scale_first = jnp.exp2((max_first - joint) * EXP2_SCALE)
    scale_second = jnp.exp2((max_second - joint) * EXP2_SCALE)
    mass = first[DH + 1 : DH + 2] * scale_first + second[DH + 1 : DH + 2] * scale_second
    return first[:DH] * scale_first + second[:DH] * scale_second, stat_tile(joint, mass)


def halve_kernel(first_ref, second_ref, first_rows_ref, second_rows_ref,
                 send_ref, keep_ref, send_rows_ref, keep_rows_ref):
    me = lax.axis_index("wide")
    bit = lax.rem(lax.div(me, 2), 2)
    width = send_ref.shape[1]
    height = send_rows_ref.shape[0]
    for half, out, out_rows in ((1 - bit, send_ref, send_rows_ref), (bit, keep_ref, keep_rows_ref)):
        columns = pl.ds(pl.multiple_of(half * width, width), width)
        numer, stats = joined(first_ref[:, columns], second_ref[:, columns])
        out[:DH, :] = numer
        out[DH:, :] = stats
        rows = pl.ds(pl.multiple_of(half * height, height), height)
        out_rows[...] = first_rows_ref[rows, :] + second_rows_ref[rows, :]


def join_kernel(first_ref, second_ref, first_rows_ref, second_rows_ref, out_ref, out_rows_ref):
    numer, stats = joined(first_ref[...], second_ref[...])
    out_ref[:DH, :] = numer
    out_ref[DH:, :] = stats
    out_rows_ref[...] = first_rows_ref[...] + second_rows_ref[...]


def refit_kernel(
    len_ref, query_ref, part0, part1, part2, part3, rows0, rows1, rows2, rows3,
    weight_out, value_out,
    key_ref, prior_ref, feat_hi, feat_lo, scaled_hi, scaled_lo, out_hi, out_lo,
    gram_hi, gram_lo, power_ref, refit_ref,
):
    me = lax.axis_index("wide")
    core = lax.rem(me, 2)
    bit = lax.rem(lax.div(me, 2), 2)
    total = len_ref[0]
    for i in range(1, len_ref.shape[0]):
        total = total + len_ref[i]
    live_total = jnp.full((1, 1), total, jnp.int32).astype(f32)
    places = ((core, bit), (core, 1 - bit), (1 - core, bit), (1 - core, 1 - bit))
    parts = (part0, part1, part2, part3)
    quarter = NQ // 4
    quarter_m = M // 4
    for (hi_bit, lo_bit), rows_ref in zip(places, (rows0, rows1, rows2, rows3)):
        rows = pl.ds(pl.multiple_of((hi_bit * 2 + lo_bit) * quarter_m, quarter_m), quarter_m)
        key_ref[rows, :] = rows_ref[:, :DH]
        prior_ref[rows, :] = rows_ref[:, DH:].astype(f32)
    frobenius = jnp.zeros((1, 1), f32)
    linear = jnp.zeros((16, M), f32)
    for p, ((hi_bit, lo_bit), part) in enumerate(zip(places, parts)):
        begin = pl.multiple_of((hi_bit * 2 + lo_bit) * quarter, quarter)
        columns = pl.ds(p * quarter, quarter)
        row_max, row_mass = part[DH : DH + 1, :], part[DH + 1 : DH + 2, :]
        scores = mm(key_ref[...], query_ref[pl.ds(begin, quarter), :], NT)
        features = jnp.exp2((scores - row_max) * EXP2_SCALE)
        target = row_mass * (M / live_total)
        high, low = split(features)
        feat_hi[:, columns] = high
        feat_lo[:, columns] = low
        frobenius = frobenius + jnp.sum(
            jnp.sum(features * features, axis=0, keepdims=True), axis=1, keepdims=True
        )
        target_pair = split(jnp.broadcast_to(target, (16, quarter)))
        linear = linear + mm3(target_pair, (high, low), NT)
        high, low = split(features * (1.0 / target))
        scaled_hi[:, columns] = high
        scaled_lo[:, columns] = low
        high, low = split(part[:DH, :] / row_mass)
        out_hi[:, columns] = high
        out_lo[:, columns] = low
    feat = (feat_hi[...], feat_lo[...])
    high, low = split(mm3(feat, feat, NT))
    gram_hi[...] = high
    gram_lo[...] = low
    damping = nnls_ridge * (frobenius / M + 1e-6)
    stepsize = 1.0 / (frobenius + damping)

    def nnls_step(number, weights):
        gradient = mm3(split(weights), (gram_hi[...], gram_lo[...]), NN) - linear + damping * weights
        return jnp.maximum(weights - stepsize * gradient, 0.0)

    weights = lax.fori_loop(0, NNLS_STEPS, nnls_step, jnp.ones((16, M), f32))
    weight_row = weights[:1]
    weight_out[...] = weight_row
    weight_column = jnp.broadcast_to(weight_row, (DH, M)).T
    scaled = (scaled_hi[...], scaled_lo[...])
    gram = mm3(scaled, scaled, NT) * weight_row
    gram = gram * jnp.concatenate([weight_column] * (M // DH), axis=1)
    diagonal = lax.broadcasted_iota(jnp.int32, (M, M), 0) == lax.broadcasted_iota(
        jnp.int32, (M, M), 1
    )
    trace = jnp.sum(
        jnp.sum(jnp.where(diagonal, gram, 0.0), axis=0, keepdims=True), axis=1, keepdims=True
    )
    ridge = ridge_weight * (trace / M + 1e-6)
    system = gram + jnp.where(diagonal, ridge, 0.0)
    right_side = weight_column * mm3(scaled, (out_hi[...], out_lo[...]), NT)
    right_side = right_side + ridge * prior_ref[...]
    bound = jnp.max(jnp.sum(jnp.abs(system), axis=0, keepdims=True), axis=1, keepdims=True)
    power_ref[...] = system / bound
    refit_ref[...] = right_side / bound

    def newton_step(number, carry):
        power = power_ref[...]
        refit = refit_ref[...]
        pair = split(power)
        refit_ref[...] = 2.0 * refit - mm3(pair, split(refit), NN)
        power_ref[...] = 2.0 * power - mm3(pair, pair, NN)
        return carry

    lax.fori_loop(0, NS_ITERS - 1, newton_step, 0)
    refit = refit_ref[...]
    value_out[...] = 2.0 * refit - mm3(split(power_ref[...]), split(refit), NN)


def shape(rows, columns, dtype):
    return jax.ShapeDtypeStruct((rows, columns), dtype)


def per_device(key_mant, scale_exp, values, queries, compact_index, shard_lengths):
    wide_count = lax.axis_size("wide")
    ctx = key_mant.shape[0]
    rows_num = DH + STAT_ROWS

    def exchanged(arrays, mask):
        pairs = [(i, i ^ mask) for i in range(wide_count)]
        return tuple(lax.ppermute(array, "wide", pairs) for array in arrays)

    send, keep, send_rows, keep_rows = pl.pallas_call(
        attention_kernel,
        out_shape=(shape(rows_num, NQ // 2, f32),) * 2 + (shape(M // 2, 2 * DH, bf16),) * 2,
        in_specs=smem(2) + vmem(4),
        out_specs=tuple(vmem(4)),
        scratch_shapes=[pltpu.VMEM((ctx, DH), bf16)],
        compiler_params=params(),
    )(shard_lengths, scale_exp, compact_index.reshape(1, M), key_mant, values, queries)
    got, got_rows = exchanged((send, send_rows), 1)
    send, keep, send_rows, keep_rows = pl.pallas_call(
        halve_kernel,
        out_shape=(shape(rows_num, NQ // 4, f32),) * 2 + (shape(M // 4, 2 * DH, bf16),) * 2,
        in_specs=vmem(4),
        out_specs=tuple(vmem(4)),
        compiler_params=params(),
    )(keep, got, keep_rows, got_rows)
    got, got_rows = exchanged((send, send_rows), 2)
    mask = 4
    while True:
        keep, keep_rows = pl.pallas_call(
            join_kernel,
            out_shape=(shape(rows_num, NQ // 4, f32), shape(M // 4, 2 * DH, bf16)),
            in_specs=vmem(4),
            out_specs=tuple(vmem(2)),
            compiler_params=params(),
        )(keep, got, keep_rows, got_rows)
        if mask >= wide_count:
            break
        got, got_rows = exchanged((keep, keep_rows), mask)
        mask *= 2
    side, side_rows = exchanged((keep, keep_rows), 2)
    core, core_rows, both, both_rows = exchanged((keep, keep_rows, side, side_rows), 1)
    weights, compact_values = pl.pallas_call(
        refit_kernel,
        out_shape=(shape(1, M, f32), shape(M, DH, f32)),
        in_specs=smem(1) + vmem(9),
        out_specs=tuple(vmem(2)),
        scratch_shapes=[
            pltpu.VMEM((M, DH), bf16),
            pltpu.VMEM((M, DH), f32),
            pltpu.VMEM((M, NQ), bf16),
            pltpu.VMEM((M, NQ), bf16),
            pltpu.VMEM((M, NQ), bf16),
            pltpu.VMEM((M, NQ), bf16),
            pltpu.VMEM((DH, NQ), bf16),
            pltpu.VMEM((DH, NQ), bf16),
            pltpu.VMEM((M, M), bf16),
            pltpu.VMEM((M, M), bf16),
            pltpu.VMEM((M, M), f32),
            pltpu.VMEM((M, DH), f32),
        ],
        compiler_params=params(),
    )(shard_lengths, queries, keep, side, core, both, keep_rows, side_rows, core_rows, both_rows)
    return weights.reshape(M), compact_values


def solution(mesh):
    placed = (
        P(("groups", "wide"), None),
        P(("groups", "wide")),
        P(("groups", "wide"), None),
        P("groups", None),
        P("groups"),
        P("groups"),
    )
    return jax.shard_map(
        per_device,
        mesh=mesh,
        in_specs=placed,
        out_specs=(P("groups"), P("groups", None)),
        check_vma=False,
    )
```

time: 553 us -> 71.4 us (0.13)
  blocking collectives: 343 us -> 0 us
  waiting for transfers between devices: 95.1 us -> 27.7 us
  matrix products: 48.6 us -> 0 us
  other arithmetic: 32 us -> 0 us
  Pallas kernels: 0 us -> 27.4 us
  between operations: 18.3 us -> 0.71 us
  starting transfers between devices: 0.08 us -> 11.2 us
  local copies, waits for them, and re-layouts: 12.2 us -> 4.19 us
    psum x9 -> x0, blocking collectives: 299 us -> none  [the longest x7 207 us: per_device(): gradient = lax.psum(local_gradient(key_weights), 'wide')]
    psum x1 -> x0, waiting for transfers between devices: 95 us -> none  [per_device(): lax.psum((across(attend, attend), across(attend, outputs)), 'wide')]
    dot_general x42 -> x0, matrix products: 48.6 us -> none  [the longest x9 16.6 us: newton_step(): jnp.dot(jnp.dot(inverse, system, precision=highest), inverse, precision=h...]
    all_gather x2 -> x0, blocking collectives: 43.9 us -> none  [merged(): pieces = jax.tree.map(lambda part: lax.all_gather(part, axis), value)]
    ppermute x0 -> x14, waiting for transfers between devices: none -> 27.7 us  [exchanged(): return tuple((lax.ppermute(array, 'wide', pairs) for array in arrays))]
    pallas_call x0 -> x6, Pallas kernels: none -> 27.4 us  [the longest x1 23.4 us: per_device(): pl.pallas_call(refit_kernel, out_shape=(shape(1, M, f32), shape(M, DH, f3...]
    add x32 -> x0, other arithmetic: 22.7 us -> none  [the longest x15 22.5 us: combine_partials(): numer_first * scale_first[:, None] + numer_second * scale_second[:, None]]
    ppermute x0 -> x14, starting transfers between devices: none -> 11.2 us  [exchanged(): return tuple((lax.ppermute(array, 'wide', pairs) for array in arrays))]
  transfers between devices with their start and end apart: 2 -> 14, of which waited for: 1 -> 7; matrix products, arithmetic and copies ran while one was open for 1% -> 0% of each run, Pallas kernels for 0% -> 0%
where the time goes in v1:
time: 71.4 us; the launch traced here: 71.1 us
  waiting for transfers between devices  27.7 us (39%)
  Pallas kernels  27.4 us (38%)
  starting transfers between devices  11.2 us (16%)
  local copies, waits for them, and re-layouts  4.19 us (6%)
    ppermute x14, waiting for transfers between devices, exchanged(): return tuple((lax.ppermute(array, 'wide', pairs) for array in arrays))  27.7 us
    pallas_call x1, Pallas kernels, per_device(): pl.pallas_call(refit_kernel, out_shape=(shape(1, M, f32), shape(M, DH, f3...  23.4 us
    ppermute x14, starting transfers between devices, exchanged(): return tuple((lax.ppermute(array, 'wide', pairs) for array in arrays))  11.2 us
    unnamed x14, local copies, waits for them, and re-layouts  4.19 us
    pallas_call x1, Pallas kernels, per_device(): pl.pallas_call(attention_kernel, out_shape=(shape(rows_num, NQ // 2, f32)...  3.77 us
  transfers between devices with their start and end apart: 14, of which 7 were waited for; matrix products, arithmetic and copies ran while one was open for 0% of the time, Pallas kernels for 0%

profile of v1, /device:TPU:0, one launch (start us, length us, event | category | flops | bytes accessed | tf_op | source)
XLA Modules:
  0.0 71.1 jit_solution(3090867745707314835)
XLA Ops:
  0.6 0.0 copy-start.5
  0.6 0.0 copy-start.6
  0.7 0.6 copy-done.5
  1.3 0.0 copy-done.6
  1.3 0.0 copy-start
  1.3 0.9 %copy-done = bf16[1024,128]{1,0:T(8,128)(2,1)S(1)} copy-done((bf16[1024,128]{1,0:T(8,128)(2,1)S(1)}, bf16[1024,128]{1,0:T(8,128)(2,1)}, u32[]{:S(2)}) %copy-start) | copy-done | bytes 262168
  2.3 0.0 copy-start.2
  2.3 0.9 %copy-done.2 = bf16[1024,128]{1,0:T(8,128)(2,1)S(1)} copy-done((bf16[1024,128]{1,0:T(8,128)(2,1)S(1)}, bf16[1024,128]{1,0:T(8,128)(2,1)}, u32[]{:S(2)}) %copy-start.2) | copy-done | bytes 262168
  3.2 0.0 copy-start.3
  3.2 0.9 %copy-done.3 = bf16[1024,128]{1,0:T(8,128)(2,1)S(1)} copy-done((bf16[1024,128]{1,0:T(8,128)(2,1)S(1)}, bf16[1024,128]{1,0:T(8,128)(2,1)}, u32[]{:S(2)}) %copy-start.3) | copy-done | bytes 262168
  4.2 0.0 copy-start.4
  4.2 0.7 copy-done.4
  4.8 3.8 %shard_map.77 = (f32[136,512]{1,0:T(8,128)S(1)}, f32[136,512]{1,0:T(8,128)S(1)}, bf16[256,256]{1,0:T(8,128)(2,1)S(1)}, bf16[256,256]{1,0:T(8,128)(2,1)S(1)}) custom-call(s32[16]{0:T(128)S(1)} %copy-done.5, s32[32]{0:T(128)S(1)} %copy-done.6, s32[1,512]{1,0:T(1,128)S(1)} %bitcast.2, bf16[1024,128]{1,0:T(8,128)(2,1)S(1)} %copy-done.2, ...), custom_call_target="tpu_custom_call" | custom-call | tf_op jit(solution)/shard_map/pallas_call | solution.py:228
  8.6 0.5 collective-permute-start
  9.1 0.1 collective-permute-start.1
  9.2 1.3 %collective-permute-done.1.second_rows_ref = bf16[256,256]{1,0:T(8,128)(2,1)S(1)} collective-permute-done((bf16[256,256]{1,0:T(8,128)(2,1)S(1)}, bf16[256,256]{1,0:T(8,128)(2,1)S(1)}, u32[]{:S(2)}, u32[]{:S(2)}) %collective-permute-start.1) | collective-permute-done | bytes 131104 | tf_op jit(solution)/shard_map/ppermute | solution.py:226
  10.5 0.0 collective-permute-done.second_ref
  10.5 0.1 shard_map.78
  10.6 3.0 %collective-permute-start.2 = (f32[136,256]{1,0:T(8,128)S(1)}, f32[136,256]{1,0:T(8,128)S(1)}, u32[]{:S(2)}, u32[]{:S(2)}) collective-permute-start(f32[136,256]{1,0:T(8,128)S(1)} %get-tuple-element.23), channel_id=1, source_target_pairs={{0,2},{1,3},{2,0},{3,1},{4,6},{5,7},{6,4},{7,5},{8,10},{9,11},{10,... | collective-permute-start | bytes 417800 | tf_op jit(solution)/shard_map/ppermute | solution.py:226
  13.5 0.1 collective-permute-start.3
  13.6 5.3 %collective-permute-done.3.second_rows_ref = bf16[128,256]{1,0:T(8,128)(2,1)S(1)} collective-permute-done((bf16[128,256]{1,0:T(8,128)(2,1)S(1)}, bf16[128,256]{1,0:T(8,128)(2,1)S(1)}, u32[]{:S(2)}, u32[]{:S(2)}) %collective-permute-start.3) | collective-permute-done | bytes 65568 | tf_op jit(solution)/shard_map/ppermute | solution.py:226
  18.9 0.0 collective-permute-done.2.second_ref
  19.0 1.9 %collective-permute-start.4 = (f32[136,256]{1,0:T(8,128)S(1)}, f32[136,256]{1,0:T(8,128)S(1)}, u32[]{:S(2)}, u32[]{:S(2)}) collective-permute-start(f32[136,256]{1,0:T(8,128)S(1)} %get-tuple-element.26.first_ref), channel_id=1, source_target_pairs={{0,4},{1,5},{2,6},{3,7},{4,0},{5,1},{6,2},{7,3},{8,12},{9,13},{10,... | collective-permute-start | bytes 417800 | tf_op jit(solution)/shard_map/ppermute | solution.py:226
  20.8 0.2 collective-permute-start.5
  21.1 4.6 %collective-permute-done.5.second_rows_ref = bf16[128,256]{1,0:T(8,128)(2,1)S(1)} collective-permute-done((bf16[128,256]{1,0:T(8,128)(2,1)S(1)}, bf16[128,256]{1,0:T(8,128)(2,1)S(1)}, u32[]{:S(2)}, u32[]{:S(2)}) %collective-permute-start.5) | collective-permute-done | bytes 65568 | tf_op jit(solution)/shard_map/ppermute | solution.py:226
  25.6 0.0 collective-permute-done.4.second_ref
  25.7 0.0 copy-start.1
  25.7 2.6 %collective-permute-start.6 = (f32[136,256]{1,0:T(8,128)S(1)}, f32[136,256]{1,0:T(8,128)S(1)}, u32[]{:S(2)}, u32[]{:S(2)}) collective-permute-start(f32[136,256]{1,0:T(8,128)S(1)} %get-tuple-element.28.first_ref), channel_id=1, source_target_pairs={{0,8},{1,9},{2,10},{3,11},{4,12},{5,13},{6,14},{7,15},{8,0},{9,1},... | collective-permute-start | bytes 417800 | tf_op jit(solution)/shard_map/ppermute | solution.py:226
  28.3 0.4 collective-permute-start.7
  28.7 8.1 %collective-permute-done.7.second_rows_ref = bf16[128,256]{1,0:T(8,128)(2,1)S(1)} collective-permute-done((bf16[128,256]{1,0:T(8,128)(2,1)S(1)}, bf16[128,256]{1,0:T(8,128)(2,1)S(1)}, u32[]{:S(2)}, u32[]{:S(2)}) %collective-permute-start.7) | collective-permute-done | bytes 65568 | tf_op jit(solution)/shard_map/ppermute | solution.py:226
  36.8 0.0 collective-permute-done.6.second_ref
  36.8 1.1 %collective-permute-start.8 = (f32[136,256]{1,0:T(8,128)S(1)}, f32[136,256]{1,0:T(8,128)S(1)}, u32[]{:S(2)}, u32[]{:S(2)}) collective-permute-start(f32[136,256]{1,0:T(8,128)S(1)} %get-tuple-element.30.part0), channel_id=1, source_target_pairs={{0,2},{1,3},{2,0},{3,1},{4,6},{5,7},{6,4},{7,5},{8,10},{9,11},{10,... | collective-permute-start | bytes 417800 | tf_op jit(solution)/shard_map/ppermute | solution.py:226
  38.0 0.0 collective-permute-start.9
  38.0 4.0 %collective-permute-done.8.part1 = f32[136,256]{1,0:T(8,128)S(1)} collective-permute-done((f32[136,256]{1,0:T(8,128)S(1)}, f32[136,256]{1,0:T(8,128)S(1)}, u32[]{:S(2)}, u32[]{:S(2)}) %collective-permute-start.8) | collective-permute-done | bytes 139296 | tf_op jit(solution)/shard_map/ppermute | solution.py:226
  41.9 0.0 collective-permute-start.10
  41.9 1.1 %collective-permute-start.11 = (bf16[128,256]{1,0:T(8,128)(2,1)S(1)}, bf16[128,256]{1,0:T(8,128)(2,1)S(1)}, u32[]{:S(2)}, u32[]{:S(2)}) collective-permute-start(bf16[128,256]{1,0:T(8,128)(2,1)S(1)} %get-tuple-element.31.rows0), channel_id=1, source_target_pairs={{0,2},{1,3},{2,0},{3,1},{4,6},{5,7},{6,4},{7,5},{8,10},{9,11},{10,... | collective-permute-start | bytes 196616 | tf_op jit(solution)/shard_map/ppermute | solution.py:226
  43.0 0.2 collective-permute-start.12
  43.2 3.2 %collective-permute-done.11.rows1 = bf16[128,256]{1,0:T(8,128)(2,1)S(1)} collective-permute-done((bf16[128,256]{1,0:T(8,128)(2,1)S(1)}, bf16[128,256]{1,0:T(8,128)(2,1)S(1)}, u32[]{:S(2)}, u32[]{:S(2)}) %collective-permute-start.11) | collective-permute-done | bytes 65568 | tf_op jit(solution)/shard_map/ppermute | solution.py:226
  46.4 0.0 collective-permute-start.13
  46.4 0.0 collective-permute-done.12.rows2
  46.4 1.2 %collective-permute-done.13.rows3 = bf16[128,256]{1,0:T(8,128)(2,1)S(1)} collective-permute-done((bf16[128,256]{1,0:T(8,128)(2,1)S(1)}, bf16[128,256]{1,0:T(8,128)(2,1)S(1)}, u32[]{:S(2)}, u32[]{:S(2)}) %collective-permute-start.13) | collective-permute-done | bytes 65568 | tf_op jit(solution)/shard_map/ppermute | solution.py:226
  47.7 0.0 collective-permute-done.9.part2
  47.7 0.0 collective-permute-done.10.part3
  47.7 0.0 copy-done.1
  47.7 23.4 %shard_map.82 = (f32[1,512]{1,0:T(1,128)}, f32[512,128]{1,0:T(8,128)}) custom-call(s32[16]{0:T(128)S(1)} %copy-done.5, bf16[1024,128]{1,0:T(8,128)(2,1)S(1)} %copy-done.1, f32[136,256]{1,0:T(8,128)S(1)} %get-tuple-element.30.part0, f32[136,256]{1,0:T(8,128)S(1)} %collective-permute-done.8.part1, f32[136,256]{1,0:T(8,128)S(1)} %collective-permute-done.9.part2, ...), custom_call_target="tpu_custom_call" | custom-call | tf_op jit(solution)/shard_map/pallas_call | solution.py:260
  (3 shorter events, 0.1 us)
Async XLA Ops:
  0.6 0.7 copy-start.5
  0.6 0.7 copy-start.6
  1.3 0.9 %copy-start = (bf16[1024,128]{1,0:T(8,128)(2,1)S(1)}, bf16[1024,128]{1,0:T(8,128)(2,1)}, u32[]{:S(2)}) copy-start(bf16[1024,128]{1,0:T(8,128)(2,1)} %query_ref.3) | copy-start | bytes 786436
  2.3 0.9 %copy-start.2 = (bf16[1024,128]{1,0:T(8,128)(2,1)S(1)}, bf16[1024,128]{1,0:T(8,128)(2,1)}, u32[]{:S(2)}) copy-start(bf16[1024,128]{1,0:T(8,128)(2,1)} %mant_ref.1) | copy-start | bytes 786436
  3.2 0.9 %copy-start.3 = (bf16[1024,128]{1,0:T(8,128)(2,1)S(1)}, bf16[1024,128]{1,0:T(8,128)(2,1)}, u32[]{:S(2)}) copy-start(bf16[1024,128]{1,0:T(8,128)(2,1)} %value_ref.1) | copy-start | bytes 786436
  4.2 0.7 copy-start.4
  8.6 1.9 %collective-permute-start = (f32[136,512]{1,0:T(8,128)S(1)}, f32[136,512]{1,0:T(8,128)S(1)}, u32[]{:S(2)}, u32[]{:S(2)}) collective-permute-start(f32[136,512]{1,0:T(8,128)S(1)} %get-tuple-element.19), channel_id=1, source_target_pairs={{0,1},{1,0},{2,3},{3,2},{4,5},{5,4},{6,7},{7,6},{8,9},{9,8},{10,11... | collective-permute-start | bytes 835592 | tf_op jit(solution)/shard_map/ppermute | solution.py:226
  9.1 1.4 %collective-permute-start.1 = (bf16[256,256]{1,0:T(8,128)(2,1)S(1)}, bf16[256,256]{1,0:T(8,128)(2,1)S(1)}, u32[]{:S(2)}, u32[]{:S(2)}) collective-permute-start(bf16[256,256]{1,0:T(8,128)(2,1)S(1)} %get-tuple-element.21), channel_id=1, source_target_pairs={{0,1},{1,0},{2,3},{3,2},{4,5},{5,4},{6,7},{7,6},{8,9},{9,8},{10,11... | collective-permute-start | bytes 393224 | tf_op jit(solution)/shard_map/ppermute | solution.py:226
  10.6 8.3 %collective-permute-start.2 = (f32[136,256]{1,0:T(8,128)S(1)}, f32[136,256]{1,0:T(8,128)S(1)}, u32[]{:S(2)}, u32[]{:S(2)}) collective-permute-start(f32[136,256]{1,0:T(8,128)S(1)} %get-tuple-element.23), channel_id=1, source_target_pairs={{0,2},{1,3},{2,0},{3,1},{4,6},{5,7},{6,4},{7,5},{8,10},{9,11},{10,... | collective-permute-start | bytes 417800 | tf_op jit(solution)/shard_map/ppermute | solution.py:226
  13.5 5.4 %collective-permute-start.3 = (bf16[128,256]{1,0:T(8,128)(2,1)S(1)}, bf16[128,256]{1,0:T(8,128)(2,1)S(1)}, u32[]{:S(2)}, u32[]{:S(2)}) collective-permute-start(bf16[128,256]{1,0:T(8,128)(2,1)S(1)} %get-tuple-element.25), channel_id=1, source_target_pairs={{0,2},{1,3},{2,0},{3,1},{4,6},{5,7},{6,4},{7,5},{8,10},{9,11},{10,... | collective-permute-start | bytes 196616 | tf_op jit(solution)/shard_map/ppermute | solution.py:226
  19.0 6.7 %collective-permute-start.4 = (f32[136,256]{1,0:T(8,128)S(1)}, f32[136,256]{1,0:T(8,128)S(1)}, u32[]{:S(2)}, u32[]{:S(2)}) collective-permute-start(f32[136,256]{1,0:T(8,128)S(1)} %get-tuple-element.26.first_ref), channel_id=1, source_target_pairs={{0,4},{1,5},{2,6},{3,7},{4,0},{5,1},{6,2},{7,3},{8,12},{9,13},{10,... | collective-permute-start | bytes 417800 | tf_op jit(solution)/shard_map/ppermute | solution.py:226
  20.8 4.8 %collective-permute-start.5 = (bf16[128,256]{1,0:T(8,128)(2,1)S(1)}, bf16[128,256]{1,0:T(8,128)(2,1)S(1)}, u32[]{:S(2)}, u32[]{:S(2)}) collective-permute-start(bf16[128,256]{1,0:T(8,128)(2,1)S(1)} %get-tuple-element.27.first_rows_ref), channel_id=1, source_target_pairs={{0,4},{1,5},{2,6},{3,7},{4,0},{5,1},{6,2},{7,3},{8,12},{9,13},{10,... | collective-permute-start | bytes 196616 | tf_op jit(solution)/shard_map/ppermute | solution.py:226
  25.7 22.0 %copy-start.1 = (bf16[1024,128]{1,0:T(8,128)(2,1)S(1)}, bf16[1024,128]{1,0:T(8,128)(2,1)}, u32[]{:S(2)}) copy-start(bf16[1024,128]{1,0:T(8,128)(2,1)} %query_ref.3) | copy-start | bytes 786436
  25.7 11.1 %collective-permute-start.6 = (f32[136,256]{1,0:T(8,128)S(1)}, f32[136,256]{1,0:T(8,128)S(1)}, u32[]{:S(2)}, u32[]{:S(2)}) collective-permute-start(f32[136,256]{1,0:T(8,128)S(1)} %get-tuple-element.28.first_ref), channel_id=1, source_target_pairs={{0,8},{1,9},{2,10},{3,11},{4,12},{5,13},{6,14},{7,15},{8,0},{9,1},... | collective-permute-start | bytes 417800 | tf_op jit(solution)/shard_map/ppermute | solution.py:226
  28.3 8.5 %collective-permute-start.7 = (bf16[128,256]{1,0:T(8,128)(2,1)S(1)}, bf16[128,256]{1,0:T(8,128)(2,1)S(1)}, u32[]{:S(2)}, u32[]{:S(2)}) collective-permute-start(bf16[128,256]{1,0:T(8,128)(2,1)S(1)} %get-tuple-element.29.first_rows_ref), channel_id=1, source_target_pairs={{0,8},{1,9},{2,10},{3,11},{4,12},{5,13},{6,14},{7,15},{8,0},{9,1},... | collective-permute-start | bytes 196616 | tf_op jit(solution)/shard_map/ppermute | solution.py:226
  36.8 5.1 %collective-permute-start.8 = (f32[136,256]{1,0:T(8,128)S(1)}, f32[136,256]{1,0:T(8,128)S(1)}, u32[]{:S(2)}, u32[]{:S(2)}) collective-permute-start(f32[136,256]{1,0:T(8,128)S(1)} %get-tuple-element.30.part0), channel_id=1, source_target_pairs={{0,2},{1,3},{2,0},{3,1},{4,6},{5,7},{6,4},{7,5},{8,10},{9,11},{10,... | collective-permute-start | bytes 417800 | tf_op jit(solution)/shard_map/ppermute | solution.py:226
  38.0 9.7 %collective-permute-start.9 = (f32[136,256]{1,0:T(8,128)S(1)}, f32[136,256]{1,0:T(8,128)S(1)}, u32[]{:S(2)}, u32[]{:S(2)}) collective-permute-start(f32[136,256]{1,0:T(8,128)S(1)} %get-tuple-element.30.part0), channel_id=1, source_target_pairs={{0,1},{1,0},{2,3},{3,2},{4,5},{5,4},{6,7},{7,6},{8,9},{9,8},{10,11... | collective-permute-start | bytes 417800 | tf_op jit(solution)/shard_map/ppermute | solution.py:226
  41.9 5.8 %collective-permute-start.10 = (f32[136,256]{1,0:T(8,128)S(1)}, f32[136,256]{1,0:T(8,128)S(1)}, u32[]{:S(2)}, u32[]{:S(2)}) collective-permute-start(f32[136,256]{1,0:T(8,128)S(1)} %collective-permute-done.8.part1), channel_id=1, source_target_pairs={{0,1},{1,0},{2,3},{3,2},{4,5},{5,4},{6,7},{7,6},{8,9},{9,8},{10,11... | collective-permute-start | bytes 417800 | tf_op jit(solution)/shard_map/ppermute | solution.py:226
  41.9 4.5 %collective-permute-start.11 = (bf16[128,256]{1,0:T(8,128)(2,1)S(1)}, bf16[128,256]{1,0:T(8,128)(2,1)S(1)}, u32[]{:S(2)}, u32[]{:S(2)}) collective-permute-start(bf16[128,256]{1,0:T(8,128)(2,1)S(1)} %get-tuple-element.31.rows0), channel_id=1, source_target_pairs={{0,2},{1,3},{2,0},{3,1},{4,6},{5,7},{6,4},{7,5},{8,10},{9,11},{10,... | collective-permute-start | bytes 196616 | tf_op jit(solution)/shard_map/ppermute | solution.py:226
  43.0 3.4 %collective-permute-start.12 = (bf16[128,256]{1,0:T(8,128)(2,1)S(1)}, bf16[128,256]{1,0:T(8,128)(2,1)S(1)}, u32[]{:S(2)}, u32[]{:S(2)}) collective-permute-start(bf16[128,256]{1,0:T(8,128)(2,1)S(1)} %get-tuple-element.31.rows0), channel_id=1, source_target_pairs={{0,1},{1,0},{2,3},{3,2},{4,5},{5,4},{6,7},{7,6},{8,9},{9,8},{10,11... | collective-permute-start | bytes 196616 | tf_op jit(solution)/shard_map/ppermute | solution.py:226
  46.4 1.3 %collective-permute-start.13 = (bf16[128,256]{1,0:T(8,128)(2,1)S(1)}, bf16[128,256]{1,0:T(8,128)(2,1)S(1)}, u32[]{:S(2)}, u32[]{:S(2)}) collective-permute-start(bf16[128,256]{1,0:T(8,128)(2,1)S(1)} %collective-permute-done.11.rows1), channel_id=1, source_target_pairs={{0,1},{1,0},{2,3},{3,2},{4,5},{5,4},{6,7},{7,6},{8,9},{9,8},{10,11... | collective-permute-start | bytes 196616 | tf_op jit(solution)/shard_map/ppermute | solution.py:226

commit v2 on v1

v2 whole, which is shorter than its diff:
```python
import jax
import jax.numpy as jnp
from jax import lax
from jax.experimental import pallas as pl
from jax.experimental.pallas import tpu as pltpu
from jax.sharding import PartitionSpec as P

DH = 128
NQ = 1024
M = 512
QB = 32
SELECT_FROM = 256
NNLS_STEPS = 8
NS_ITERS = 9
CHUNKS = 4
CHUNK = NQ // CHUNKS
QUARTER_M = M // CHUNKS
SUM_ROWS = 2 * DH + QUARTER_M // 2

ridge_weight = 4.0
nnls_ridge = 0.1
floor_value = -1e30
EXP2_SCALE = DH ** (-0.5) * 1.4426950408889634

f32 = jnp.float32
bf16 = jnp.bfloat16
NN = (((1,), (0,)), ((), ()))
NT = (((1,), (1,)), ((), ()))
TN = (((0,), (0,)), ((), ()))


def mm(left, right, dims):
    return lax.dot_general(left, right, dims, preferred_element_type=f32)


def split(x):
    high = x.astype(bf16)
    return high, (x - high.astype(f32)).astype(bf16)


def mm3(left, right, dims):
    return mm(left[0], right[0], dims) + (mm(left[0], right[1], dims) + mm(left[1], right[0], dims))


def total_of(x):
    return jnp.sum(jnp.sum(x, axis=0, keepdims=True), axis=1, keepdims=True)


def place(number, size):
    return pl.ds(pl.multiple_of(number * size, size), size)


def bits():
    me = lax.axis_index("wide")
    return me, lax.rem(me, 2), lax.rem(lax.div(me, 2), 2)


def put_sums(out_ref, columns, sums):
    high, low = split(sums)
    out_ref[:DH, columns] = high
    out_ref[DH : 2 * DH, columns] = low


def get_sums(ref, columns):
    return ref[:DH, columns].astype(f32) + ref[DH : 2 * DH, columns].astype(f32)


def attention_kernel(
    len_hbm, exp_hbm, index_hbm, mant_hbm, value_hbm, query_hbm,
    stat_ref, send_key_ref, keep_key_ref, send_ref, keep_ref,
    len_ref, exp_ref, index_ref, mant_ref, value_ref, query_ref, key_ref, sems,
):
    copies = [
        pltpu.make_async_copy(source, target, sems.at[i])
        for i, (source, target) in enumerate(
            (
                (exp_hbm, exp_ref),
                (mant_hbm, mant_ref),
                (query_hbm, query_ref),
                (len_hbm, len_ref),
                (index_hbm, index_ref),
                (value_hbm, value_ref),
            )
        )
    ]
    for copy in copies:
        copy.start()
    ctx = mant_ref.shape[0]
    me, core, bit = bits()
    for copy in copies:
        copy.wait()
    own_len = len_ref[me]
    for b in range(ctx // QB):
        exponent = exp_ref[b]
        factor = jnp.where(exponent > 0, 2.0, jnp.where(exponent < 0, 0.5, 1.0)).astype(f32)
        rows = pl.ds(b * QB, QB)
        key_ref[rows, :] = (mant_ref[rows, :].astype(f32) * factor).astype(bf16)
    half_m = M // 2
    position = lax.broadcasted_iota(jnp.int32, (SELECT_FROM, half_m), 0)
    for half, key_out, out in ((1 - core, send_key_ref, send_ref), (core, keep_key_ref, keep_ref)):
        wanted = index_ref[:, place(half, half_m)] - me * ctx
        chosen = jnp.where(position == wanted, 1.0, 0.0).astype(bf16)
        key_out[...] = mm(chosen, key_ref[:SELECT_FROM, :], TN).astype(bf16)
        prior = mm(value_ref[:SELECT_FROM, :], chosen, TN).astype(bf16)
        for piece in range(2):
            for part in range(2):
                begin = piece * CHUNK + part * QUARTER_M
                out[2 * DH :, begin : begin + QUARTER_M] = prior[
                    part * (DH // 2) : (part + 1) * (DH // 2), piece * QUARTER_M : (piece + 1) * QUARTER_M
                ]
    dead = lax.broadcasted_iota(jnp.int32, (ctx, CHUNK), 0) >= own_len
    for half, out in ((1 - core, send_ref), (core, keep_ref)):
        for c in range(2):
            number = half * 2 + c
            scores = mm(key_ref[...], query_ref[place(number, CHUNK), :], NT)
            scores = jnp.where(dead, floor_value, scores)
            row_max = jnp.max(scores, axis=0, keepdims=True)
            attn = jnp.exp2((scores - row_max) * EXP2_SCALE)
            stat_ref[pl.ds(number, 1), :] = row_max
            stat_ref[pl.ds(CHUNKS + number, 1), :] = jnp.sum(attn, axis=0, keepdims=True)
            sums = mm(value_ref[...], attn.astype(bf16), TN)
            put_sums(out, pl.ds(c * CHUNK, CHUNK), sums)


def joined_stats(first_ref, second_ref, out_ref, scale_ref):
    max_first, max_second = first_ref[:CHUNKS, :], second_ref[:CHUNKS, :]
    joint = jnp.maximum(max_first, max_second)
    scale_first = jnp.exp2((max_first - joint) * EXP2_SCALE)
    scale_second = jnp.exp2((max_second - joint) * EXP2_SCALE)
    out_ref[:CHUNKS, :] = joint
    out_ref[CHUNKS:, :] = first_ref[CHUNKS:, :] * scale_first + second_ref[CHUNKS:, :] * scale_second
    scale_ref[...] = scale_first


def core_kernel(stat_a, stat_b, key_a, key_b, send_in, keep_in,
                stat_out, key_out, send_out, keep_out, scale_ref):
    me, core, bit = bits()
    joined_stats(stat_a, stat_b, stat_out, scale_ref)
    key_out[...] = key_a[...] + key_b[...]
    for half, source, out in ((1 - core, send_in, send_out), (core, keep_in, keep_out)):
        for c in range(2):
            columns = pl.ds(c * CHUNK, CHUNK)
            factor = scale_ref[pl.ds(half * 2 + c, 1), :]
            put_sums(out, columns, get_sums(source, columns) * factor)
        out[2 * DH :, :] = source[2 * DH :, :]


def halve_kernel(stat_a, stat_b, key_a, key_b, sum_a, sum_b,
                 stat_out, key_out, send_out, keep_out, scale_ref):
    me, core, bit = bits()
    joined_stats(stat_a, stat_b, stat_out, scale_ref)
    key_out[...] = key_a[...] + key_b[...]
    everything = pl.ds(0, CHUNK)
    for half, out in ((1 - bit, send_out), (bit, keep_out)):
        columns = place(half, CHUNK)
        factor = scale_ref[pl.ds(core * 2 + half, 1), :]
        put_sums(out, everything, (get_sums(sum_a, columns) + get_sums(sum_b, columns)) * factor)
        out[2 * DH :, :] = sum_a[2 * DH :, columns] + sum_b[2 * DH :, columns]


def join_kernel(stat_a, stat_b, key_a, key_b, sum_a, sum_b, stat_out, key_out, sum_out, scale_ref):
    me, core, bit = bits()
    joined_stats(stat_a, stat_b, stat_out, scale_ref)
    key_out[...] = key_a[...] + key_b[...]
    everything = pl.ds(0, CHUNK)
    factor = scale_ref[pl.ds(core * 2 + bit, 1), :]
    put_sums(sum_out, everything, (get_sums(sum_a, everything) + get_sums(sum_b, everything)) * factor)
    sum_out[2 * DH :, :] = sum_a[2 * DH :, :] + sum_b[2 * DH :, :]


def outputs_kernel(stat_ref, sum_a, sum_b, after_ref, out_ref):
    me, core, bit = bits()
    everything = pl.ds(0, CHUNK)
    row_mass = stat_ref[pl.ds(CHUNKS + core * 2 + bit, 1), :]
    put_sums(out_ref, everything, (get_sums(sum_a, everything) + get_sums(sum_b, everything)) / row_mass)
    out_ref[2 * DH :, :] = sum_a[2 * DH :, :] + sum_b[2 * DH :, :]


def feature_kernel(
    len_ref, query_ref, stat_ref, own_key_ref, other_key_ref,
    gram_hi, gram_lo, linear_ref, norm_ref, scaled_hi, scaled_lo,
    key_ref, feat_hi, feat_lo,
):
    me, core, bit = bits()
    total = len_ref[0]
    for i in range(1, len_ref.shape[0]):
        total = total + len_ref[i]
    live_total = jnp.full((1, 1), total, jnp.int32).astype(f32)
    key_ref[place(core, M // 2), :] = own_key_ref[...]
    key_ref[place(1 - core, M // 2), :] = other_key_ref[...]
    frobenius = jnp.zeros((1, 1), f32)
    linear = jnp.zeros((16, M), f32)
    for c in range(CHUNKS):
        columns = pl.ds(c * CHUNK, CHUNK)
        row_max, row_mass = stat_ref[c : c + 1, :], stat_ref[CHUNKS + c : CHUNKS + c + 1, :]
        scores = mm(key_ref[...], query_ref[columns, :], NT)
        features = jnp.exp2((scores - row_max) * EXP2_SCALE)
        target = row_mass * (M / live_total)
        high, low = split(features)
        feat_hi[:, columns] = high
        feat_lo[:, columns] = low
        frobenius = frobenius + total_of(features * features)
        linear = linear + mm3(split(jnp.broadcast_to(target, (16, CHUNK))), (high, low), NT)
        high, low = split(features * (1.0 / target))
        scaled_hi[:, columns] = high
        scaled_lo[:, columns] = low
    feat = (feat_hi[...], feat_lo[...])
    high, low = split(mm3(feat, feat, NT))
    gram_hi[...] = high
    gram_lo[...] = low
    linear_ref[...] = linear
    norm_ref[...] = jnp.broadcast_to(frobenius, norm_ref.shape)


def weight_kernel(
    gram_hi, gram_lo, linear_ref, norm_ref, scaled_hi, scaled_lo,
    weight_out, factor_out, power_out, attend_ref,
):
    linear = linear_ref[...]
    frobenius = norm_ref[:1, :1]
    damping = nnls_ridge * (frobenius / M + 1e-6)
    stepsize = 1.0 / (frobenius + damping)
    weights = jnp.ones((16, M), f32)
    for number in range(NNLS_STEPS):
        gradient = mm3(split(weights), (gram_hi[...], gram_lo[...]), NN) - linear + damping * weights
        weights = jnp.maximum(weights - stepsize * gradient, 0.0)
        if number % 2 == 0 and number // 2 < CHUNKS:
            columns = pl.ds(number // 2 * CHUNK, CHUNK)
            scaled = (scaled_hi[:, columns], scaled_lo[:, columns])
            part = mm3(scaled, scaled, NT)
            attend_ref[...] = part if number == 0 else attend_ref[...] + part
    weight_row = weights[:1]
    weight_out[...] = weight_row
    weight_column = jnp.broadcast_to(weight_row, (DH, M)).T
    gram = attend_ref[...] * weight_row
    gram = gram * jnp.concatenate([weight_column] * (M // DH), axis=1)
    diagonal = lax.broadcasted_iota(jnp.int32, (M, M), 0) == lax.broadcasted_iota(
        jnp.int32, (M, M), 1
    )
    ridge = ridge_weight * (total_of(jnp.where(diagonal, gram, 0.0)) / M + 1e-6)
    system = gram + jnp.where(diagonal, ridge, 0.0)
    bound = jnp.max(jnp.sum(jnp.abs(system), axis=0, keepdims=True), axis=1, keepdims=True)
    row = lax.broadcasted_iota(jnp.int32, factor_out.shape, 0)
    factor_out[...] = jnp.where(row == 0, ridge, bound)
    power_out[...] = system * (1.0 / bound)


def forward_kernel(sum_ref, after_ref, out_ref):
    out_ref[...] = sum_ref[...]


def refit_kernel(
    power_in, weight_ref, factor_ref, scaled_hi, scaled_lo, part0, part1, part2, part3,
    value_out, both_ref, left_ref, right_ref, prior_ref,
):
    me, core, bit = bits()
    places = ((core, bit), (core, 1 - bit), (1 - core, bit), (1 - core, 1 - bit))
    product = jnp.zeros((DH, M), f32)
    for (hi_bit, lo_bit), part in zip(places, (part0, part1, part2, part3)):
        number = hi_bit * 2 + lo_bit
        columns = place(number, CHUNK)
        lanes = place(number, QUARTER_M)
        prior_ref[: DH // 2, lanes] = part[2 * DH :, :QUARTER_M].astype(f32)
        prior_ref[DH // 2 :, lanes] = part[2 * DH :, QUARTER_M:].astype(f32)
        high = mm(part[: 2 * DH, :], scaled_hi[:, columns], NT)
        product = product + (high[:DH] + high[DH:] + mm(part[:DH, :], scaled_lo[:, columns], NT))
    ridge, bound = factor_ref[0:1, :1], factor_ref[1:2, :1]
    both_ref[:M, :] = power_in[...]
    both_ref[M:, :] = (weight_ref[...] * product + ridge * prior_ref[...]) * (1.0 / bound)

    def newton_step(number, carry):
        both = both_ref[...]
        high, low = split(both)
        both_ref[...] = 2.0 * both - mm3((high, low), (high[:M], low[:M]), NN)
        return carry

    lax.fori_loop(0, NS_ITERS - 1, newton_step, 0)
    refit = both_ref[M:, :]
    refit = 2.0 * refit - mm3(split(refit), split(both_ref[:M, :]), NN)
    value_out[...] = refit.T


def shape(rows, columns, dtype):
    return jax.ShapeDtypeStruct((rows, columns), dtype)


def call(kernel, outs, arrays, scalars=0, scratch=(), in_specs=None, flops=None, limit=48):
    return pl.pallas_call(
        kernel,
        out_shape=tuple(outs),
        in_specs=in_specs
        or [pl.BlockSpec(memory_space=pltpu.SMEM)] * scalars
        + [pl.BlockSpec(memory_space=pltpu.VMEM)] * (len(arrays) - scalars),
        out_specs=tuple([pl.BlockSpec(memory_space=pltpu.VMEM)] * len(outs)),
        scratch_shapes=list(scratch),
        compiler_params=pltpu.CompilerParams(vmem_limit_bytes=limit * 1024 * 1024),
        cost_estimate=None
        if flops is None
        else pl.CostEstimate(flops=flops, bytes_accessed=1024, transcendentals=0),
    )(*arrays)


def per_device(key_mant, scale_exp, values, queries, compact_index, shard_lengths):
    wide_count = lax.axis_size("wide")
    ctx = key_mant.shape[0]

    def exchanged(array, mask):
        return lax.ppermute(array, "wide", [(i, i ^ mask) for i in range(wide_count)])

    stat_shape = shape(2 * CHUNKS, CHUNK, f32)
    key_shape = shape(M // 2, DH, bf16)
    half_sum = shape(SUM_ROWS, 2 * CHUNK, bf16)
    quarter_sum = shape(SUM_ROWS, CHUNK, bf16)
    factors = [pltpu.VMEM((CHUNKS, CHUNK), f32)]

    stats, send_keys, keys, send, keep = call(
        attention_kernel,
        (stat_shape, key_shape, key_shape, half_sum, half_sum),
        (shard_lengths, scale_exp, compact_index.reshape(1, M), key_mant, values, queries),
        in_specs=[pl.BlockSpec(memory_space=pltpu.HBM)] * 6,
        flops=10**9,
        limit=48,
        scratch=[
            pltpu.SMEM(shard_lengths.shape, jnp.int32),
            pltpu.SMEM(scale_exp.shape, jnp.int32),
            pltpu.VMEM((1, M), jnp.int32),
            pltpu.VMEM((ctx, DH), bf16),
            pltpu.VMEM((ctx, DH), bf16),
            pltpu.VMEM((NQ, DH), bf16),
            pltpu.VMEM((ctx, DH), bf16),
            pltpu.SemaphoreType.DMA((6,)),
        ],
    )
    stats, keys, send, keep = call(
        core_kernel,
        (stat_shape, key_shape, half_sum, half_sum),
        (stats, exchanged(stats, 1), keys, exchanged(send_keys, 1), send, keep),
        scratch=factors,
    )
    stats, keys, send, keep = call(
        halve_kernel,
        (stat_shape, key_shape, quarter_sum, quarter_sum),
        (stats, exchanged(stats, 2), keys, exchanged(keys, 2), keep, exchanged(send, 1)),
        scratch=factors,
    )
    sums, got = keep, exchanged(send, 2)
    mask = 4
    while mask < wide_count:
        stats, keys, sums = call(
            join_kernel,
            (stat_shape, key_shape, quarter_sum),
            (stats, exchanged(stats, mask), keys, exchanged(keys, mask), sums, got),
            scratch=factors,
        )
        got = exchanged(sums, mask)
        mask *= 2
    gram_hi, gram_lo, linear, norm, scaled_hi, scaled_lo = call(
        feature_kernel,
        (shape(M, M, bf16),) * 2 + (shape(16, M, f32), shape(8, DH, f32)) + (shape(M, NQ, bf16),) * 2,
        (shard_lengths, queries, stats, keys, exchanged(keys, 1)),
        scalars=1,
        flops=4 * 10**9,
        scratch=[pltpu.VMEM((M, DH), bf16), pltpu.VMEM((M, NQ), bf16), pltpu.VMEM((M, NQ), bf16)],
    )
    (outputs,) = call(outputs_kernel, (quarter_sum,), (stats, sums, got, norm))
    side = exchanged(outputs, 2)
    core = exchanged(outputs, 1)
    weights, factor, power = call(
        weight_kernel,
        (shape(1, M, f32), shape(8, DH, f32), shape(M, M, f32)),
        (gram_hi, gram_lo, linear, norm, scaled_hi, scaled_lo),
        flops=5 * 10**9,
        scratch=[pltpu.VMEM((M, M), f32)],
    )
    (side,) = call(forward_kernel, (quarter_sum,), (side, factor))
    (compact_values,) = call(
        refit_kernel,
        (shape(M, DH, f32),),
        (power, weights, factor, scaled_hi, scaled_lo, outputs, side, core, exchanged(side, 1)),
        scratch=[
            pltpu.VMEM((M + DH, M), f32),
            pltpu.VMEM((M + DH, 3 * M), bf16),
            pltpu.VMEM((3 * M, M), bf16),
            pltpu.VMEM((DH, M), f32),
        ],
    )
    return weights.reshape(M), compact_values


def solution(mesh):
    placed = (
        P(("groups", "wide"), None),
        P(("groups", "wide")),
        P(("groups", "wide"), None),
        P("groups", None),
        P("groups"),
        P("groups"),
    )
    return jax.shard_map(
        per_device,
        mesh=mesh,
        in_specs=placed,
        out_specs=(P("groups"), P("groups", None)),
        check_vma=False,
    )
```

time: 71.4 us -> 62.1 us (0.87)
  waiting for transfers between devices: 27.7 us -> 18.3 us
  starting transfers between devices: 11.2 us -> 13.3 us
  Pallas kernels: 27.4 us -> 25.4 us
    ppermute x14 -> x16, waiting for transfers between devices: 27.7 us -> 18.3 us  [exchanged(): lax.ppermute(array, 'wide', [(i, i ^ mask) for i in range(wide_count)])]
    ppermute x14 -> x16, starting transfers between devices: 11.2 us -> 13.3 us  [exchanged(): lax.ppermute(array, 'wide', [(i, i ^ mask) for i in range(wide_count)])]
    pallas_call x6 -> x10, Pallas kernels: 27.4 us -> 25.4 us  [call(): pl.pallas_call(kernel, out_shape=tuple(outs), in_specs=in_specs or [pl.Bl...]
    unnamed x14 -> x16, local copies, waits for them, and re-layouts: 4.19 us -> 4.2 us
  transfers between devices with their start and end apart: 14 -> 16, of which waited for: 7 -> 8; matrix products, arithmetic and copies ran while one was open for 0% -> 0% of each run, Pallas kernels for 0% -> 16%
where the time goes in v2:
time: 62.1 us; the launch traced here: 61.9 us
  Pallas kernels  25.4 us (41%)
  waiting for transfers between devices  18.3 us (29%)
  starting transfers between devices  13.3 us (21%)
  local copies, waits for them, and re-layouts  4.2 us (7%)
  between operations  0.74 us (1%)
    pallas_call x10, Pallas kernels, call(): pl.pallas_call(kernel, out_shape=tuple(outs), in_specs=in_specs or [pl.Bl...  25.4 us
    ppermute x16, waiting for transfers between devices, exchanged(): lax.ppermute(array, 'wide', [(i, i ^ mask) for i in range(wide_count)])  18.3 us
    ppermute x16, starting transfers between devices, exchanged(): lax.ppermute(array, 'wide', [(i, i ^ mask) for i in range(wide_count)])  13.3 us
    unnamed x16, local copies, waits for them, and re-layouts  4.2 us
  transfers between devices with their start and end apart: 16, of which 8 were waited for; matrix products, arithmetic and copies ran while one was open for 0% of the time, Pallas kernels for 16%

profile of v2, /device:TPU:0, one launch (start us, length us, event | category | flops | bytes accessed | tf_op | source)
XLA Modules:
  0.0 61.9 jit_solution(15670407537987966354)
XLA Ops:
  0.6 0.0 copy-start.7
  0.6 0.0 copy-start.6
  0.7 0.6 %copy-done.7 = s32[16]{0:T(128)S(1)} copy-done((s32[16]{0:T(128)S(1)}, s32[16]{0:T(128)}, u32[]{:S(2)}) %copy-start.7) | copy-done | bytes 88
  1.3 0.0 copy-done.6
  1.3 0.0 copy-start.1
  1.3 0.9 %copy-done.1 = bf16[1024,128]{1,0:T(8,128)(2,1)S(1)} copy-done((bf16[1024,128]{1,0:T(8,128)(2,1)S(1)}, bf16[1024,128]{1,0:T(8,128)(2,1)}, u32[]{:S(2)}) %copy-start.1) | copy-done | bytes 262168
  2.3 0.0 copy-start.2
  2.3 0.9 %copy-done.2 = bf16[1024,128]{1,0:T(8,128)(2,1)S(1)} copy-done((bf16[1024,128]{1,0:T(8,128)(2,1)S(1)}, bf16[1024,128]{1,0:T(8,128)(2,1)}, u32[]{:S(2)}) %copy-start.2) | copy-done | bytes 262168
  3.2 0.0 copy-start.3
  3.2 0.9 %copy-done.3 = bf16[1024,128]{1,0:T(8,128)(2,1)S(1)} copy-done((bf16[1024,128]{1,0:T(8,128)(2,1)S(1)}, bf16[1024,128]{1,0:T(8,128)(2,1)}, u32[]{:S(2)}) %copy-start.3) | copy-done | bytes 262168
  4.2 0.0 copy-start.5
  4.2 0.7 %copy-done.5 = s32[512]{0:T(512)S(1)} copy-done((s32[512]{0:T(512)S(1)}, s32[512]{0:T(512)}, u32[]{:S(2)}) %copy-start.5) | copy-done | bytes 2072
  4.8 3.7 %shard_map.77 = (f32[8,256]{1,0:T(8,128)S(1)}, bf16[256,128]{1,0:T(8,128)(2,1)S(1)}, bf16[256,128]{1,0:T(8,128)(2,1)S(1)}, bf16[320,512]{1,0:T(8,128)(2,1)S(1)}, bf16[320,512]{1,0:T(8,128)(2,1)S(1)}) custom-call(s32[16]{0:T(128)S(1)} %copy-done.7, s32[32]{0:T(128)S(1)} %copy-done.6, s32[1,512]{1,0:T(1,128)S(1)} %bitcast.3, bf16[1024,128]{1,0:T(8,128)(2,1)S(1)} %copy-done.1, ...), custom_call_target="tpu_custom_call" | custom-call | flops 1000000000 | bytes 1024 | tf_op jit(solution)/shard_map/pallas_call | solution.py:288
  8.5 0.5 collective-permute-start.1
  9.1 0.1 collective-permute-start
  9.1 1.1 %collective-permute-done.stat_b = f32[8,256]{1,0:T(8,128)S(1)} collective-permute-done((f32[8,256]{1,0:T(8,128)S(1)}, f32[8,256]{1,0:T(8,128)S(1)}, u32[]{:S(2)}, u32[]{:S(2)}) %collective-permute-start) | collective-permute-done | bytes 8224 | tf_op jit(solution)/shard_map/ppermute | solution.py:308
  10.2 0.0 collective-permute-done.1.key_b
  10.2 0.2 shard_map.78
  10.4 0.2 collective-permute-start.4
  10.6 2.9 %collective-permute-start.3 = (bf16[256,128]{1,0:T(8,128)(2,1)S(1)}, bf16[256,128]{1,0:T(8,128)(2,1)S(1)}, u32[]{:S(2)}, u32[]{:S(2)}) collective-permute-start(bf16[256,128]{1,0:T(8,128)(2,1)S(1)} %get-tuple-element.36.key_a), channel_id=1, source_target_pairs={{0,2},{1,3},{2,0},{3,1},{4,6},{5,7},{6,4},{7,5},{8,10},{9,11},{10,... | collective-permute-start | bytes 196616 | tf_op jit(solution)/shard_map/ppermute | solution.py:308
  13.5 0.0 collective-permute-start.2
  13.5 3.6 %collective-permute-done.2.stat_b = f32[8,256]{1,0:T(8,128)S(1)} collective-permute-done((f32[8,256]{1,0:T(8,128)S(1)}, f32[8,256]{1,0:T(8,128)S(1)}, u32[]{:S(2)}, u32[]{:S(2)}) %collective-permute-start.2) | collective-permute-done | bytes 8224 | tf_op jit(solution)/shard_map/ppermute | solution.py:308
  17.1 0.0 collective-permute-done.3.key_b
  17.1 0.0 collective-permute-done.4.sum_b
  17.2 0.1 shard_map.79
  17.3 0.8 %collective-permute-start.7 = (bf16[320,256]{1,0:T(8,128)(2,1)S(1)}, bf16[320,256]{1,0:T(8,128)(2,1)S(1)}, u32[]{:S(2)}, u32[]{:S(2)}) collective-permute-start(bf16[320,256]{1,0:T(8,128)(2,1)S(1)} %get-tuple-element.42), channel_id=1, source_target_pairs={{0,2},{1,3},{2,0},{3,1},{4,6},{5,7},{6,4},{7,5},{8,10},{9,11},{10,... | collective-permute-start | bytes 491528 | tf_op jit(solution)/shard_map/ppermute | solution.py:308
  18.1 1.6 %collective-permute-start.6 = (bf16[256,128]{1,0:T(8,128)(2,1)S(1)}, bf16[256,128]{1,0:T(8,128)(2,1)S(1)}, u32[]{:S(2)}, u32[]{:S(2)}) collective-permute-start(bf16[256,128]{1,0:T(8,128)(2,1)S(1)} %get-tuple-element.40.key_a), channel_id=1, source_target_pairs={{0,4},{1,5},{2,6},{3,7},{4,0},{5,1},{6,2},{7,3},{8,12},{9,13},{10,... | collective-permute-start | bytes 196616 | tf_op jit(solution)/shard_map/ppermute | solution.py:308
  19.7 0.4 collective-permute-start.5
  20.1 3.2 %collective-permute-done.5.stat_b = f32[8,256]{1,0:T(8,128)S(1)} collective-permute-done((f32[8,256]{1,0:T(8,128)S(1)}, f32[8,256]{1,0:T(8,128)S(1)}, u32[]{:S(2)}, u32[]{:S(2)}) %collective-permute-start.5) | collective-permute-done | bytes 8224 | tf_op jit(solution)/shard_map/ppermute | solution.py:308
  23.3 0.0 collective-permute-done.6.key_b
  23.3 0.0 collective-permute-done.7.sum_b
  23.3 0.1 shard_map.80
  23.4 0.0 copy-start.4
  23.4 1.0 %collective-permute-start.10 = (bf16[320,256]{1,0:T(8,128)(2,1)S(1)}, bf16[320,256]{1,0:T(8,128)(2,1)S(1)}, u32[]{:S(2)}, u32[]{:S(2)}) collective-permute-start(bf16[320,256]{1,0:T(8,128)(2,1)S(1)} %get-tuple-element.45.sum_a), channel_id=1, source_target_pairs={{0,4},{1,5},{2,6},{3,7},{4,0},{5,1},{6,2},{7,3},{8,12},{9,13},{10,... | collective-permute-start | bytes 491528 | tf_op jit(solution)/shard_map/ppermute | solution.py:308
  24.4 2.6 %collective-permute-start.9 = (bf16[256,128]{1,0:T(8,128)(2,1)S(1)}, bf16[256,128]{1,0:T(8,128)(2,1)S(1)}, u32[]{:S(2)}, u32[]{:S(2)}) collective-permute-start(bf16[256,128]{1,0:T(8,128)(2,1)S(1)} %get-tuple-element.44.key_a), channel_id=1, source_target_pairs={{0,8},{1,9},{2,10},{3,11},{4,12},{5,13},{6,14},{7,15},{8,0},{9,1},... | collective-permute-start | bytes 196616 | tf_op jit(solution)/shard_map/ppermute | solution.py:308
  27.0 0.3 collective-permute-start.8
  27.4 4.3 %collective-permute-done.8.stat_b = f32[8,256]{1,0:T(8,128)S(1)} collective-permute-done((f32[8,256]{1,0:T(8,128)S(1)}, f32[8,256]{1,0:T(8,128)S(1)}, u32[]{:S(2)}, u32[]{:S(2)}) %collective-permute-start.8) | collective-permute-done | bytes 8224 | tf_op jit(solution)/shard_map/ppermute | solution.py:308
  31.6 0.0 collective-permute-done.9.key_b
  31.6 0.0 collective-permute-done.10.sum_b
  31.6 0.1 shard_map.81
  31.7 0.1 collective-permute-start.11
  31.8 0.8 %collective-permute-start.12 = (bf16[320,256]{1,0:T(8,128)(2,1)S(1)}, bf16[320,256]{1,0:T(8,128)(2,1)S(1)}, u32[]{:S(2)}, u32[]{:S(2)}) collective-permute-start(bf16[320,256]{1,0:T(8,128)(2,1)S(1)} %get-tuple-element.57.sum_a), channel_id=1, source_target_pairs={{0,8},{1,9},{2,10},{3,11},{4,12},{5,13},{6,14},{7,15},{8,0},{9,1},... | collective-permute-start | bytes 491528 | tf_op jit(solution)/shard_map/ppermute | solution.py:308
  32.6 0.4 collective-permute-done.11.other_key_ref
  33.0 0.0 copy-done.4
  33.0 5.2 %shard_map.82 = (bf16[512,512]{1,0:T(8,128)(2,1)S(1)}, bf16[512,512]{1,0:T(8,128)(2,1)S(1)}, f32[16,512]{1,0:T(8,128)S(1)}, f32[8,128]{1,0:T(8,128)S(1)}, bf16[5...) custom-call(s32[16]{0:T(128)S(1)} %copy-done.7, bf16[1024,128]{1,0:T(8,128)(2,1)S(1)} %copy-done.4, ...), custom_call_target="tpu_custom_call" | custom-call | flops 4000000000 | bytes 1024 | tf_op jit(solution)/shard_map/pallas_call | solution.py:288
  38.2 4.6 %collective-permute-done.12.sum_b = bf16[320,256]{1,0:T(8,128)(2,1)S(1)} collective-permute-done((bf16[320,256]{1,0:T(8,128)(2,1)S(1)}, bf16[320,256]{1,0:T(8,128)(2,1)S(1)}, u32[]{:S(2)}, u32[]{:S(2)}) %collective-permute-start.12) | collective-permute-done | bytes 163872 | tf_op jit(solution)/shard_map/ppermute | solution.py:308
  42.8 0.1 shard_map.84.part0
  42.9 1.4 %collective-permute-start.13 = (bf16[320,256]{1,0:T(8,128)(2,1)S(1)}, bf16[320,256]{1,0:T(8,128)(2,1)S(1)}, u32[]{:S(2)}, u32[]{:S(2)}) collective-permute-start(bf16[320,256]{1,0:T(8,128)(2,1)S(1)} %shard_map.84.part0), channel_id=1, source_target_pairs={{0,2},{1,3},{2,0},{3,1},{4,6},{5,7},{6,4},{7,5},{8,10},{9,11},{10,... | collective-permute-start | bytes 491528 | tf_op jit(solution)/shard_map/ppermute | solution.py:308
  44.3 4.5 %shard_map.83 = (f32[1,512]{1,0:T(1,128)}, f32[8,128]{1,0:T(8,128)S(1)}, f32[512,512]{1,0:T(8,128)S(1)}) custom-call(bf16[512,512]{1,0:T(8,128)(2,1)S(1)} %get-tuple-element.48.gram_hi, bf16[512,512]{1,0:T(8,128)(2,1)S(1)} %get-tuple-element.49.gram_lo, f32[16,512]{1,0:T(8,128)S(1)} %get-tuple-element.50.linear_ref, ...), custom_call_target="tpu_custom_call" | custom-call | flops 5000000000 | bytes 1024 | tf_op jit(solution)/shard_map/pallas_call | solution.py:288
  48.8 0.0 collective-permute-start.14
  48.8 0.0 collective-permute-done.13.sum_ref
  48.8 0.0 copy-start
  48.8 0.6 collective-permute-start.15
  49.4 0.8 %collective-permute-done.14.part2 = bf16[320,256]{1,0:T(8,128)(2,1)S(1)} collective-permute-done((bf16[320,256]{1,0:T(8,128)(2,1)S(1)}, bf16[320,256]{1,0:T(8,128)(2,1)S(1)}, u32[]{:S(2)}, u32[]{:S(2)}) %collective-permute-start.14) | collective-permute-done | bytes 163872 | tf_op jit(solution)/shard_map/ppermute | solution.py:308
  50.2 0.2 collective-permute-done.15.part3
  50.4 0.0 copy-done
  50.4 11.5 %shard_map.86 = f32[512,128]{1,0:T(8,128)} custom-call(f32[512,512]{1,0:T(8,128)S(1)} %get-tuple-element.55.power_in, f32[1,512]{1,0:T(1,128)S(1)} %copy-done, f32[8,128]{1,0:T(8,128)S(1)} %get-tuple-element.56.after_ref.factor_ref, bf16[512,1024]{1,0:T(8,128)(2,1)S(1)} %get-tuple-element.52.scaled_hi, bf16[512,1024]{1,0:T(8,128)(2,1)S(1)} %get-tuple-element.53.scaled_lo, ...), custom_call_target="tpu_custom_call" | custom-call | tf_op jit(solution)/shard_map/pallas_call | solution.py:288
  (1 shorter events, 0.0 us)
Async XLA Ops:
  0.6 0.7 %copy-start.7 = (s32[16]{0:T(128)S(1)}, s32[16]{0:T(128)}, u32[]{:S(2)}) copy-start(s32[16]{0:T(128)} %len_ref.1) | copy-start | bytes 196
  0.6 0.7 %copy-start.6 = (s32[32]{0:T(128)S(1)}, s32[32]{0:T(128)}, u32[]{:S(2)}) copy-start(s32[32]{0:T(128)} %exp_hbm.1) | copy-start | bytes 388
  1.3 0.9 %copy-start.1 = (bf16[1024,128]{1,0:T(8,128)(2,1)S(1)}, bf16[1024,128]{1,0:T(8,128)(2,1)}, u32[]{:S(2)}) copy-start(bf16[1024,128]{1,0:T(8,128)(2,1)} %mant_hbm.1) | copy-start | bytes 786436
  2.3 0.9 %copy-start.2 = (bf16[1024,128]{1,0:T(8,128)(2,1)S(1)}, bf16[1024,128]{1,0:T(8,128)(2,1)}, u32[]{:S(2)}) copy-start(bf16[1024,128]{1,0:T(8,128)(2,1)} %value_hbm.1) | copy-start | bytes 786436
  3.2 0.9 %copy-start.3 = (bf16[1024,128]{1,0:T(8,128)(2,1)S(1)}, bf16[1024,128]{1,0:T(8,128)(2,1)}, u32[]{:S(2)}) copy-start(bf16[1024,128]{1,0:T(8,128)(2,1)} %query_ref.1) | copy-start | bytes 786436
  4.2 0.7 %copy-start.5 = (s32[512]{0:T(512)S(1)}, s32[512]{0:T(512)}, u32[]{:S(2)}) copy-start(s32[512]{0:T(512)} %param.10) | copy-start | bytes 6148
  8.5 1.7 %collective-permute-start.1 = (bf16[256,128]{1,0:T(8,128)(2,1)S(1)}, bf16[256,128]{1,0:T(8,128)(2,1)S(1)}, u32[]{:S(2)}, u32[]{:S(2)}) collective-permute-start(bf16[256,128]{1,0:T(8,128)(2,1)S(1)} %get-tuple-element.32), channel_id=1, source_target_pairs={{0,1},{1,0},{2,3},{3,2},{4,5},{5,4},{6,7},{7,6},{8,9},{9,8},{10,11... | collective-permute-start | bytes 196616 | tf_op jit(solution)/shard_map/ppermute | solution.py:308
  9.1 1.2 %collective-permute-start = (f32[8,256]{1,0:T(8,128)S(1)}, f32[8,256]{1,0:T(8,128)S(1)}, u32[]{:S(2)}, u32[]{:S(2)}) collective-permute-start(f32[8,256]{1,0:T(8,128)S(1)} %get-tuple-element.30.stat_a), channel_id=1, source_target_pairs={{0,1},{1,0},{2,3},{3,2},{4,5},{5,4},{6,7},{7,6},{8,9},{9,8},{10,11... | collective-permute-start | bytes 24584 | tf_op jit(solution)/shard_map/ppermute | solution.py:308
  10.4 6.7 %collective-permute-start.4 = (bf16[320,512]{1,0:T(8,128)(2,1)S(1)}, bf16[320,512]{1,0:T(8,128)(2,1)S(1)}, u32[]{:S(2)}, u32[]{:S(2)}) collective-permute-start(bf16[320,512]{1,0:T(8,128)(2,1)S(1)} %get-tuple-element.38), channel_id=1, source_target_pairs={{0,1},{1,0},{2,3},{3,2},{4,5},{5,4},{6,7},{7,6},{8,9},{9,8},{10,11... | collective-permute-start | bytes 983048 | tf_op jit(solution)/shard_map/ppermute | solution.py:308
  10.6 6.5 %collective-permute-start.3 = (bf16[256,128]{1,0:T(8,128)(2,1)S(1)}, bf16[256,128]{1,0:T(8,128)(2,1)S(1)}, u32[]{:S(2)}, u32[]{:S(2)}) collective-permute-start(bf16[256,128]{1,0:T(8,128)(2,1)S(1)} %get-tuple-element.36.key_a), channel_id=1, source_target_pairs={{0,2},{1,3},{2,0},{3,1},{4,6},{5,7},{6,4},{7,5},{8,10},{9,11},{10,... | collective-permute-start | bytes 196616 | tf_op jit(solution)/shard_map/ppermute | solution.py:308
  13.5 3.7 %collective-permute-start.2 = (f32[8,256]{1,0:T(8,128)S(1)}, f32[8,256]{1,0:T(8,128)S(1)}, u32[]{:S(2)}, u32[]{:S(2)}) collective-permute-start(f32[8,256]{1,0:T(8,128)S(1)} %get-tuple-element.35.stat_a), channel_id=1, source_target_pairs={{0,2},{1,3},{2,0},{3,1},{4,6},{5,7},{6,4},{7,5},{8,10},{9,11},{10,... | collective-permute-start | bytes 24584 | tf_op jit(solution)/shard_map/ppermute | solution.py:308
  17.3 6.0 %collective-permute-start.7 = (bf16[320,256]{1,0:T(8,128)(2,1)S(1)}, bf16[320,256]{1,0:T(8,128)(2,1)S(1)}, u32[]{:S(2)}, u32[]{:S(2)}) collective-permute-start(bf16[320,256]{1,0:T(8,128)(2,1)S(1)} %get-tuple-element.42), channel_id=1, source_target_pairs={{0,2},{1,3},{2,0},{3,1},{4,6},{5,7},{6,4},{7,5},{8,10},{9,11},{10,... | collective-permute-start | bytes 491528 | tf_op jit(solution)/shard_map/ppermute | solution.py:308
  18.1 5.3 %collective-permute-start.6 = (bf16[256,128]{1,0:T(8,128)(2,1)S(1)}, bf16[256,128]{1,0:T(8,128)(2,1)S(1)}, u32[]{:S(2)}, u32[]{:S(2)}) collective-permute-start(bf16[256,128]{1,0:T(8,128)(2,1)S(1)} %get-tuple-element.40.key_a), channel_id=1, source_target_pairs={{0,4},{1,5},{2,6},{3,7},{4,0},{5,1},{6,2},{7,3},{8,12},{9,13},{10,... | collective-permute-start | bytes 196616 | tf_op jit(solution)/shard_map/ppermute | solution.py:308
  19.7 3.7 %collective-permute-start.5 = (f32[8,256]{1,0:T(8,128)S(1)}, f32[8,256]{1,0:T(8,128)S(1)}, u32[]{:S(2)}, u32[]{:S(2)}) collective-permute-start(f32[8,256]{1,0:T(8,128)S(1)} %get-tuple-element.39.stat_a), channel_id=1, source_target_pairs={{0,4},{1,5},{2,6},{3,7},{4,0},{5,1},{6,2},{7,3},{8,12},{9,13},{10,... | collective-permute-start | bytes 24584 | tf_op jit(solution)/shard_map/ppermute | solution.py:308
  23.4 9.6 %copy-start.4 = (bf16[1024,128]{1,0:T(8,128)(2,1)S(1)}, bf16[1024,128]{1,0:T(8,128)(2,1)}, u32[]{:S(2)}) copy-start(bf16[1024,128]{1,0:T(8,128)(2,1)} %query_ref.1) | copy-start | bytes 786436
  23.4 8.2 %collective-permute-start.10 = (bf16[320,256]{1,0:T(8,128)(2,1)S(1)}, bf16[320,256]{1,0:T(8,128)(2,1)S(1)}, u32[]{:S(2)}, u32[]{:S(2)}) collective-permute-start(bf16[320,256]{1,0:T(8,128)(2,1)S(1)} %get-tuple-element.45.sum_a), channel_id=1, source_target_pairs={{0,4},{1,5},{2,6},{3,7},{4,0},{5,1},{6,2},{7,3},{8,12},{9,13},{10,... | collective-permute-start | bytes 491528 | tf_op jit(solution)/shard_map/ppermute | solution.py:308
  24.4 7.2 %collective-permute-start.9 = (bf16[256,128]{1,0:T(8,128)(2,1)S(1)}, bf16[256,128]{1,0:T(8,128)(2,1)S(1)}, u32[]{:S(2)}, u32[]{:S(2)}) collective-permute-start(bf16[256,128]{1,0:T(8,128)(2,1)S(1)} %get-tuple-element.44.key_a), channel_id=1, source_target_pairs={{0,8},{1,9},{2,10},{3,11},{4,12},{5,13},{6,14},{7,15},{8,0},{9,1},... | collective-permute-start | bytes 196616 | tf_op jit(solution)/shard_map/ppermute | solution.py:308
  27.0 4.6 %collective-permute-start.8 = (f32[8,256]{1,0:T(8,128)S(1)}, f32[8,256]{1,0:T(8,128)S(1)}, u32[]{:S(2)}, u32[]{:S(2)}) collective-permute-start(f32[8,256]{1,0:T(8,128)S(1)} %get-tuple-element.43.stat_a), channel_id=1, source_target_pairs={{0,8},{1,9},{2,10},{3,11},{4,12},{5,13},{6,14},{7,15},{8,0},{9,1},... | collective-permute-start | bytes 24584 | tf_op jit(solution)/shard_map/ppermute | solution.py:308
  31.7 1.3 %collective-permute-start.11 = (bf16[256,128]{1,0:T(8,128)(2,1)S(1)}, bf16[256,128]{1,0:T(8,128)(2,1)S(1)}, u32[]{:S(2)}, u32[]{:S(2)}) collective-permute-start(bf16[256,128]{1,0:T(8,128)(2,1)S(1)} %get-tuple-element.47.own_key_ref), channel_id=1, source_target_pairs={{0,1},{1,0},{2,3},{3,2},{4,5},{5,4},{6,7},{7,6},{8,9},{9,8},{10,11... | collective-permute-start | bytes 196616 | tf_op jit(solution)/shard_map/ppermute | solution.py:308
  31.8 11.0 %collective-permute-start.12 = (bf16[320,256]{1,0:T(8,128)(2,1)S(1)}, bf16[320,256]{1,0:T(8,128)(2,1)S(1)}, u32[]{:S(2)}, u32[]{:S(2)}) collective-permute-start(bf16[320,256]{1,0:T(8,128)(2,1)S(1)} %get-tuple-element.57.sum_a), channel_id=1, source_target_pairs={{0,8},{1,9},{2,10},{3,11},{4,12},{5,13},{6,14},{7,15},{8,0},{9,1},... | collective-permute-start | bytes 491528 | tf_op jit(solution)/shard_map/ppermute | solution.py:308
  42.9 5.9 %collective-permute-start.13 = (bf16[320,256]{1,0:T(8,128)(2,1)S(1)}, bf16[320,256]{1,0:T(8,128)(2,1)S(1)}, u32[]{:S(2)}, u32[]{:S(2)}) collective-permute-start(bf16[320,256]{1,0:T(8,128)(2,1)S(1)} %shard_map.84.part0), channel_id=1, source_target_pairs={{0,2},{1,3},{2,0},{3,1},{4,6},{5,7},{6,4},{7,5},{8,10},{9,11},{10,... | collective-permute-start | bytes 491528 | tf_op jit(solution)/shard_map/ppermute | solution.py:308
  48.8 1.4 %collective-permute-start.14 = (bf16[320,256]{1,0:T(8,128)(2,1)S(1)}, bf16[320,256]{1,0:T(8,128)(2,1)S(1)}, u32[]{:S(2)}, u32[]{:S(2)}) collective-permute-start(bf16[320,256]{1,0:T(8,128)(2,1)S(1)} %shard_map.84.part0), channel_id=1, source_target_pairs={{0,1},{1,0},{2,3},{3,2},{4,5},{5,4},{6,7},{7,6},{8,9},{9,8},{10,11... | collective-permute-start | bytes 491528 | tf_op jit(solution)/shard_map/ppermute | solution.py:308
  48.8 1.6 %copy-start = (f32[1,512]{1,0:T(1,128)S(1)}, f32[1,512]{1,0:T(1,128)}, u32[]{:S(2)}) copy-start(f32[1,512]{1,0:T(1,128)} %get-tuple-element.54.weight_ref) | copy-start | bytes 6148
  48.8 1.6 %collective-permute-start.15 = (bf16[320,256]{1,0:T(8,128)(2,1)S(1)}, bf16[320,256]{1,0:T(8,128)(2,1)S(1)}, u32[]{:S(2)}, u32[]{:S(2)}) collective-permute-start(bf16[320,256]{1,0:T(8,128)(2,1)S(1)} %shard_map.85.part1), channel_id=1, source_target_pairs={{0,1},{1,0},{2,3},{3,2},{4,5},{5,4},{6,7},{7,6},{8,9},{9,8},{10,11... | collective-permute-start | bytes 491528 | tf_op jit(solution)/shard_map/ppermute | solution.py:308

commit v3 on v2

--- a/solution.py
+++ b/solution.py
@@ -15,7 +15,7 @@
 CHUNKS = 4
 CHUNK = NQ // CHUNKS
 QUARTER_M = M // CHUNKS
-SUM_ROWS = 2 * DH + QUARTER_M // 2
+SUM_ROWS = DH + QUARTER_M // 2
 
 ridge_weight = 4.0
 nnls_ridge = 0.1
@@ -56,13 +56,11 @@
 
 
 def put_sums(out_ref, columns, sums):
-    high, low = split(sums)
-    out_ref[:DH, columns] = high
-    out_ref[DH : 2 * DH, columns] = low
+    out_ref[:DH, columns] = sums.astype(bf16)
 
 
 def get_sums(ref, columns):
-    return ref[:DH, columns].astype(f32) + ref[DH : 2 * DH, columns].astype(f32)
+    return ref[:DH, columns].astype(f32)
 
 
 def attention_kernel(
@@ -105,7 +103,7 @@
         for piece in range(2):
             for part in range(2):
                 begin = piece * CHUNK + part * QUARTER_M
-                out[2 * DH :, begin : begin + QUARTER_M] = prior[
+                out[DH :, begin : begin + QUARTER_M] = prior[
                     part * (DH // 2) : (part + 1) * (DH // 2), piece * QUARTER_M : (piece + 1) * QUARTER_M
                 ]
     dead = lax.broadcasted_iota(jnp.int32, (ctx, CHUNK), 0) >= own_len
@@ -142,7 +140,7 @@
             columns = pl.ds(c * CHUNK, CHUNK)
             factor = scale_ref[pl.ds(half * 2 + c, 1), :]
             put_sums(out, columns, get_sums(source, columns) * factor)
-        out[2 * DH :, :] = source[2 * DH :, :]
+        out[DH :, :] = source[DH :, :]
 
 
 def halve_kernel(stat_a, stat_b, key_a, key_b, sum_a, sum_b,
@@ -155,7 +153,7 @@
         columns = place(half, CHUNK)
         factor = scale_ref[pl.ds(core * 2 + half, 1), :]
         put_sums(out, everything, (get_sums(sum_a, columns) + get_sums(sum_b, columns)) * factor)
-        out[2 * DH :, :] = sum_a[2 * DH :, columns] + sum_b[2 * DH :, columns]
+        out[DH :, :] = sum_a[DH :, columns] + sum_b[DH :, columns]
 
 
 def join_kernel(stat_a, stat_b, key_a, key_b, sum_a, sum_b, stat_out, key_out, sum_out, scale_ref):
@@ -165,7 +163,7 @@
     everything = pl.ds(0, CHUNK)
     factor = scale_ref[pl.ds(core * 2 + bit, 1), :]
     put_sums(sum_out, everything, (get_sums(sum_a, everything) + get_sums(sum_b, everything)) * factor)
-    sum_out[2 * DH :, :] = sum_a[2 * DH :, :] + sum_b[2 * DH :, :]
+    sum_out[DH :, :] = sum_a[DH :, :] + sum_b[DH :, :]
 
 
 def outputs_kernel(stat_ref, sum_a, sum_b, after_ref, out_ref):
@@ -173,7 +171,7 @@
     everything = pl.ds(0, CHUNK)
     row_mass = stat_ref[pl.ds(CHUNKS + core * 2 + bit, 1), :]
     put_sums(out_ref, everything, (get_sums(sum_a, everything) + get_sums(sum_b, everything)) / row_mass)
-    out_ref[2 * DH :, :] = sum_a[2 * DH :, :] + sum_b[2 * DH :, :]
+    out_ref[DH :, :] = sum_a[DH :, :] + sum_b[DH :, :]
 
 
 def feature_kernel(
@@ -260,10 +258,11 @@
         number = hi_bit * 2 + lo_bit
         columns = place(number, CHUNK)
         lanes = place(number, QUARTER_M)
-        prior_ref[: DH // 2, lanes] = part[2 * DH :, :QUARTER_M].astype(f32)
-        prior_ref[DH // 2 :, lanes] = part[2 * DH :, QUARTER_M:].astype(f32)
-        high = mm(part[: 2 * DH, :], scaled_hi[:, columns], NT)
-        product = product + (high[:DH] + high[DH:] + mm(part[:DH, :], scaled_lo[:, columns], NT))
+        prior_ref[: DH // 2, lanes] = part[DH :, :QUARTER_M].astype(f32)
+        prior_ref[DH // 2 :, lanes] = part[DH :, QUARTER_M:].astype(f32)
+        product = product + (
+            mm(part[:DH, :], scaled_hi[:, columns], NT) + mm(part[:DH, :], scaled_lo[:, columns], NT)
+        )
     ridge, bound = factor_ref[0:1, :1], factor_ref[1:2, :1]
     both_ref[:M, :] = power_in[...]
     both_ref[M:, :] = (weight_ref[...] * product + ridge * prior_ref[...]) * (1.0 / bound)
@@ -293,7 +292,7 @@
         + [pl.BlockSpec(memory_space=pltpu.VMEM)] * (len(arrays) - scalars),
         out_specs=tuple([pl.BlockSpec(memory_space=pltpu.VMEM)] * len(outs)),
         scratch_shapes=list(scratch),
-        compiler_params=pltpu.CompilerParams(vmem_limit_bytes=limit * 1024 * 1024),
+        compiler_params=pltpu.CompilerParams(vmem_limit_bytes=int(limit * 1024 * 1024)),
         cost_estimate=None
         if flops is None
         else pl.CostEstimate(flops=flops, bytes_accessed=1024, transcendentals=0),
@@ -316,10 +315,14 @@
     stats, send_keys, keys, send, keep = call(
         attention_kernel,
         (stat_shape, key_shape, key_shape, half_sum, half_sum),
-        (shard_lengths, scale_exp, compact_index.reshape(1, M), key_mant, values, queries),
+        [
+            pltpu.with_memory_space_constraint(array, pltpu.HBM)
+            for array in (
+                shard_lengths, scale_exp, compact_index.reshape(1, M), key_mant, values, queries
+            )
+        ],
         in_specs=[pl.BlockSpec(memory_space=pltpu.HBM)] * 6,
         flops=10**9,
-        limit=48,
         scratch=[
             pltpu.SMEM(shard_lengths.shape, jnp.int32),
             pltpu.SMEM(scale_exp.shape, jnp.int32),

time: 62.1 us -> 55 us (0.89)
  local copies, waits for them, and re-layouts: 4.2 us -> 0.02 us
  waiting for transfers between devices: 18.3 us -> 15.3 us
    unnamed x16 -> x6, local copies, waits for them, and re-layouts: 4.2 us -> 0.02 us
    ppermute x16, waiting for transfers between devices: 18.3 us -> 15.3 us  [exchanged(): lax.ppermute(array, 'wide', [(i, i ^ mask) for i in range(wide_count)])]
  transfers between devices with their start and end apart: 16 -> 16, of which waited for: 8 -> 8; matrix products, arithmetic and copies ran while one was open for 0% -> 0% of each run, Pallas kernels for 16% -> 18%
where the time goes in v3:
time: 55 us; the launch traced here: 54.8 us
  Pallas kernels  25.7 us (47%)
  waiting for transfers between devices  15.3 us (28%)
  starting transfers between devices  13.1 us (24%)
  between operations  0.73 us (1%)
    pallas_call x10, Pallas kernels, call(): pl.pallas_call(kernel, out_shape=tuple(outs), in_specs=in_specs or [pl.Bl...  25.7 us
    ppermute x16, waiting for transfers between devices, exchanged(): lax.ppermute(array, 'wide', [(i, i ^ mask) for i in range(wide_count)])  15.3 us
    ppermute x16, starting transfers between devices, exchanged(): lax.ppermute(array, 'wide', [(i, i ^ mask) for i in range(wide_count)])  13.1 us
  transfers between devices with their start and end apart: 16, of which 8 were waited for; matrix products, arithmetic and copies ran while one was open for 0% of the time, Pallas kernels for 18%

profile of v3, /device:TPU:0, one launch (start us, length us, event | category | flops | bytes accessed | tf_op | source)
XLA Modules:
  0.0 54.8 jit_solution(4917426714176731723)
XLA Ops:
  0.6 4.2 %shard_map.77 = (f32[8,256]{1,0:T(8,128)S(1)}, bf16[256,128]{1,0:T(8,128)(2,1)S(1)}, bf16[256,128]{1,0:T(8,128)(2,1)S(1)}, bf16[192,512]{1,0:T(8,128)(2,1)S(1)}, bf16[192,512]{1,0:T(8,128)(2,1)S(1)}) custom-call(s32[16]{0:T(128)} %len_ref.1, s32[32]{0:T(128)} %exp_hbm.1, s32[1,512]{1,0:T(1,128)} %bitcast.3, bf16[1024,128]{1,0:T(8,128)(2,1)} %mant_hbm.1, ...), custom_call_target="tpu_custom_call" | custom-call | flops 1000000000 | bytes 1024 | tf_op jit(solution)/shard_map/pallas_call | solution.py:287
  4.9 0.5 collective-permute-start.1
  5.4 0.1 collective-permute-start
  5.5 1.1 %collective-permute-done.stat_b = f32[8,256]{1,0:T(8,128)S(1)} collective-permute-done((f32[8,256]{1,0:T(8,128)S(1)}, f32[8,256]{1,0:T(8,128)S(1)}, u32[]{:S(2)}, u32[]{:S(2)}) %collective-permute-start) | collective-permute-done | bytes 8224 | tf_op jit(solution)/shard_map/ppermute | solution.py:307
  6.6 0.0 collective-permute-done.1.key_b
  6.6 0.1 shard_map.78
  6.6 0.2 collective-permute-start.4
  6.9 2.9 %collective-permute-start.3 = (bf16[256,128]{1,0:T(8,128)(2,1)S(1)}, bf16[256,128]{1,0:T(8,128)(2,1)S(1)}, u32[]{:S(2)}, u32[]{:S(2)}) collective-permute-start(bf16[256,128]{1,0:T(8,128)(2,1)S(1)} %get-tuple-element.36.key_a), channel_id=1, source_target_pairs={{0,2},{1,3},{2,0},{3,1},{4,6},{5,7},{6,4},{7,5},{8,10},{9,11},{10,... | collective-permute-start | bytes 196616 | tf_op jit(solution)/shard_map/ppermute | solution.py:307
  9.7 0.0 collective-permute-start.2
  9.8 3.6 %collective-permute-done.2.stat_b = f32[8,256]{1,0:T(8,128)S(1)} collective-permute-done((f32[8,256]{1,0:T(8,128)S(1)}, f32[8,256]{1,0:T(8,128)S(1)}, u32[]{:S(2)}, u32[]{:S(2)}) %collective-permute-start.2) | collective-permute-done | bytes 8224 | tf_op jit(solution)/shard_map/ppermute | solution.py:307
  13.4 0.0 collective-permute-done.3.key_b
  13.4 0.0 collective-permute-done.4.sum_b
  13.4 0.1 shard_map.79
  13.5 0.8 %collective-permute-start.7 = (bf16[192,256]{1,0:T(8,128)(2,1)S(1)}, bf16[192,256]{1,0:T(8,128)(2,1)S(1)}, u32[]{:S(2)}, u32[]{:S(2)}) collective-permute-start(bf16[192,256]{1,0:T(8,128)(2,1)S(1)} %get-tuple-element.42), channel_id=1, source_target_pairs={{0,2},{1,3},{2,0},{3,1},{4,6},{5,7},{6,4},{7,5},{8,10},{9,11},{10,... | collective-permute-start | bytes 294920 | tf_op jit(solution)/shard_map/ppermute | solution.py:307
  14.2 1.6 %collective-permute-start.6 = (bf16[256,128]{1,0:T(8,128)(2,1)S(1)}, bf16[256,128]{1,0:T(8,128)(2,1)S(1)}, u32[]{:S(2)}, u32[]{:S(2)}) collective-permute-start(bf16[256,128]{1,0:T(8,128)(2,1)S(1)} %get-tuple-element.40.key_a), channel_id=1, source_target_pairs={{0,4},{1,5},{2,6},{3,7},{4,0},{5,1},{6,2},{7,3},{8,12},{9,13},{10,... | collective-permute-start | bytes 196616 | tf_op jit(solution)/shard_map/ppermute | solution.py:307
  15.8 0.4 collective-permute-start.5
  16.3 3.2 %collective-permute-done.5.stat_b = f32[8,256]{1,0:T(8,128)S(1)} collective-permute-done((f32[8,256]{1,0:T(8,128)S(1)}, f32[8,256]{1,0:T(8,128)S(1)}, u32[]{:S(2)}, u32[]{:S(2)}) %collective-permute-start.5) | collective-permute-done | bytes 8224 | tf_op jit(solution)/shard_map/ppermute | solution.py:307
  19.5 0.0 collective-permute-done.6.key_b
  19.5 0.0 collective-permute-done.7.sum_b
  19.6 0.0 copy-start.1
  19.6 0.8 %collective-permute-start.10 = (bf16[192,256]{1,0:T(8,128)(2,1)S(1)}, bf16[192,256]{1,0:T(8,128)(2,1)S(1)}, u32[]{:S(2)}, u32[]{:S(2)}) collective-permute-start(bf16[192,256]{1,0:T(8,128)(2,1)S(1)} %get-tuple-element.45.sum_a), channel_id=1, source_target_pairs={{0,4},{1,5},{2,6},{3,7},{4,0},{5,1},{6,2},{7,3},{8,12},{9,13},{10,... | collective-permute-start | bytes 294920 | tf_op jit(solution)/shard_map/ppermute | solution.py:307
  20.3 2.6 %collective-permute-start.9 = (bf16[256,128]{1,0:T(8,128)(2,1)S(1)}, bf16[256,128]{1,0:T(8,128)(2,1)S(1)}, u32[]{:S(2)}, u32[]{:S(2)}) collective-permute-start(bf16[256,128]{1,0:T(8,128)(2,1)S(1)} %get-tuple-element.44.key_a), channel_id=1, source_target_pairs={{0,8},{1,9},{2,10},{3,11},{4,12},{5,13},{6,14},{7,15},{8,0},{9,1},... | collective-permute-start | bytes 196616 | tf_op jit(solution)/shard_map/ppermute | solution.py:307
  22.9 0.3 collective-permute-start.8
  23.3 4.2 %collective-permute-done.8.stat_b = f32[8,256]{1,0:T(8,128)S(1)} collective-permute-done((f32[8,256]{1,0:T(8,128)S(1)}, f32[8,256]{1,0:T(8,128)S(1)}, u32[]{:S(2)}, u32[]{:S(2)}) %collective-permute-start.8) | collective-permute-done | bytes 8224 | tf_op jit(solution)/shard_map/ppermute | solution.py:307
  27.5 0.0 collective-permute-done.9.key_b
  27.5 0.0 collective-permute-done.10.sum_b
  27.5 0.1 collective-permute-start.11
  27.6 0.0 copy-start.2
  27.6 0.9 %collective-permute-start.12 = (bf16[192,256]{1,0:T(8,128)(2,1)S(1)}, bf16[192,256]{1,0:T(8,128)(2,1)S(1)}, u32[]{:S(2)}, u32[]{:S(2)}) collective-permute-start(bf16[192,256]{1,0:T(8,128)(2,1)S(1)} %get-tuple-element.57.sum_a), channel_id=1, source_target_pairs={{0,8},{1,9},{2,10},{3,11},{4,12},{5,13},{6,14},{7,15},{8,0},{9,1},... | collective-permute-start | bytes 294920 | tf_op jit(solution)/shard_map/ppermute | solution.py:307
  28.5 0.4 collective-permute-done.11.other_key_ref
  28.8 0.0 copy-done.1
  28.8 0.0 copy-done.2
  28.9 5.2 %shard_map.82 = (bf16[512,512]{1,0:T(8,128)(2,1)S(1)}, bf16[512,512]{1,0:T(8,128)(2,1)S(1)}, f32[16,512]{1,0:T(8,128)S(1)}, f32[8,128]{1,0:T(8,128)S(1)}, bf16[5...) custom-call(s32[16]{0:T(128)S(1)} %copy-done.2, bf16[1024,128]{1,0:T(8,128)(2,1)S(1)} %copy-done.1, ...), custom_call_target="tpu_custom_call" | custom-call | flops 4000000000 | bytes 1024 | tf_op jit(solution)/shard_map/pallas_call | solution.py:287
  34.0 1.8 %collective-permute-done.12.sum_b = bf16[192,256]{1,0:T(8,128)(2,1)S(1)} collective-permute-done((bf16[192,256]{1,0:T(8,128)(2,1)S(1)}, bf16[192,256]{1,0:T(8,128)(2,1)S(1)}, u32[]{:S(2)}, u32[]{:S(2)}) %collective-permute-start.12) | collective-permute-done | bytes 98336 | tf_op jit(solution)/shard_map/ppermute | solution.py:307
  35.9 1.4 %collective-permute-start.13 = (bf16[192,256]{1,0:T(8,128)(2,1)S(1)}, bf16[192,256]{1,0:T(8,128)(2,1)S(1)}, u32[]{:S(2)}, u32[]{:S(2)}) collective-permute-start(bf16[192,256]{1,0:T(8,128)(2,1)S(1)} %shard_map.84.part0), channel_id=1, source_target_pairs={{0,2},{1,3},{2,0},{3,1},{4,6},{5,7},{6,4},{7,5},{8,10},{9,11},{10,... | collective-permute-start | bytes 294920 | tf_op jit(solution)/shard_map/ppermute | solution.py:307
  37.2 4.5 %shard_map.83 = (f32[1,512]{1,0:T(1,128)}, f32[8,128]{1,0:T(8,128)S(1)}, f32[512,512]{1,0:T(8,128)S(1)}) custom-call(bf16[512,512]{1,0:T(8,128)(2,1)S(1)} %get-tuple-element.48.gram_hi, bf16[512,512]{1,0:T(8,128)(2,1)S(1)} %get-tuple-element.49.gram_lo, f32[16,512]{1,0:T(8,128)S(1)} %get-tuple-element.50.linear_ref, ...), custom_call_target="tpu_custom_call" | custom-call | flops 5000000000 | bytes 1024 | tf_op jit(solution)/shard_map/pallas_call | solution.py:287
  41.7 0.0 collective-permute-start.14
  41.7 0.0 collective-permute-done.13.sum_ref
  41.8 0.0 copy-start
  41.8 0.6 %collective-permute-start.15 = (bf16[192,256]{1,0:T(8,128)(2,1)S(1)}, bf16[192,256]{1,0:T(8,128)(2,1)S(1)}, u32[]{:S(2)}, u32[]{:S(2)}) collective-permute-start(bf16[192,256]{1,0:T(8,128)(2,1)S(1)} %shard_map.85.part1), channel_id=1, source_target_pairs={{0,1},{1,0},{2,3},{3,2},{4,5},{5,4},{6,7},{7,6},{8,9},{9,8},{10,11... | collective-permute-start | bytes 294920 | tf_op jit(solution)/shard_map/ppermute | solution.py:307
  42.3 0.7 %collective-permute-done.14.part2 = bf16[192,256]{1,0:T(8,128)(2,1)S(1)} collective-permute-done((bf16[192,256]{1,0:T(8,128)(2,1)S(1)}, bf16[192,256]{1,0:T(8,128)(2,1)S(1)}, u32[]{:S(2)}, u32[]{:S(2)}) %collective-permute-start.14) | collective-permute-done | bytes 98336 | tf_op jit(solution)/shard_map/ppermute | solution.py:307
  43.0 0.2 collective-permute-done.15.part3
  43.3 0.0 copy-done
  43.3 11.5 %shard_map.86 = f32[512,128]{1,0:T(8,128)} custom-call(f32[512,512]{1,0:T(8,128)S(1)} %get-tuple-element.55.power_in, f32[1,512]{1,0:T(1,128)S(1)} %copy-done, f32[8,128]{1,0:T(8,128)S(1)} %get-tuple-element.56.after_ref.factor_ref, bf16[512,1024]{1,0:T(8,128)(2,1)S(1)} %get-tuple-element.52.scaled_hi, bf16[512,1024]{1,0:T(8,128)(2,1)S(1)} %get-tuple-element.53.scaled_lo, ...), custom_call_target="tpu_custom_call" | custom-call | tf_op jit(solution)/shard_map/pallas_call | solution.py:287
  (4 shorter events, 0.1 us)
Async XLA Ops:
  4.9 1.7 %collective-permute-start.1 = (bf16[256,128]{1,0:T(8,128)(2,1)S(1)}, bf16[256,128]{1,0:T(8,128)(2,1)S(1)}, u32[]{:S(2)}, u32[]{:S(2)}) collective-permute-start(bf16[256,128]{1,0:T(8,128)(2,1)S(1)} %get-tuple-element.32), channel_id=1, source_target_pairs={{0,1},{1,0},{2,3},{3,2},{4,5},{5,4},{6,7},{7,6},{8,9},{9,8},{10,11... | collective-permute-start | bytes 196616 | tf_op jit(solution)/shard_map/ppermute | solution.py:307
  5.4 1.2 %collective-permute-start = (f32[8,256]{1,0:T(8,128)S(1)}, f32[8,256]{1,0:T(8,128)S(1)}, u32[]{:S(2)}, u32[]{:S(2)}) collective-permute-start(f32[8,256]{1,0:T(8,128)S(1)} %get-tuple-element.30.stat_a), channel_id=1, source_target_pairs={{0,1},{1,0},{2,3},{3,2},{4,5},{5,4},{6,7},{7,6},{8,9},{9,8},{10,11... | collective-permute-start | bytes 24584 | tf_op jit(solution)/shard_map/ppermute | solution.py:307
  6.6 6.7 %collective-permute-start.4 = (bf16[192,512]{1,0:T(8,128)(2,1)S(1)}, bf16[192,512]{1,0:T(8,128)(2,1)S(1)}, u32[]{:S(2)}, u32[]{:S(2)}) collective-permute-start(bf16[192,512]{1,0:T(8,128)(2,1)S(1)} %get-tuple-element.38), channel_id=1, source_target_pairs={{0,1},{1,0},{2,3},{3,2},{4,5},{5,4},{6,7},{7,6},{8,9},{9,8},{10,11... | collective-permute-start | bytes 589832 | tf_op jit(solution)/shard_map/ppermute | solution.py:307
  6.9 6.5 %collective-permute-start.3 = (bf16[256,128]{1,0:T(8,128)(2,1)S(1)}, bf16[256,128]{1,0:T(8,128)(2,1)S(1)}, u32[]{:S(2)}, u32[]{:S(2)}) collective-permute-start(bf16[256,128]{1,0:T(8,128)(2,1)S(1)} %get-tuple-element.36.key_a), channel_id=1, source_target_pairs={{0,2},{1,3},{2,0},{3,1},{4,6},{5,7},{6,4},{7,5},{8,10},{9,11},{10,... | collective-permute-start | bytes 196616 | tf_op jit(solution)/shard_map/ppermute | solution.py:307
  9.7 3.7 %collective-permute-start.2 = (f32[8,256]{1,0:T(8,128)S(1)}, f32[8,256]{1,0:T(8,128)S(1)}, u32[]{:S(2)}, u32[]{:S(2)}) collective-permute-start(f32[8,256]{1,0:T(8,128)S(1)} %get-tuple-element.35.stat_a), channel_id=1, source_target_pairs={{0,2},{1,3},{2,0},{3,1},{4,6},{5,7},{6,4},{7,5},{8,10},{9,11},{10,... | collective-permute-start | bytes 24584 | tf_op jit(solution)/shard_map/ppermute | solution.py:307
  13.5 6.0 %collective-permute-start.7 = (bf16[192,256]{1,0:T(8,128)(2,1)S(1)}, bf16[192,256]{1,0:T(8,128)(2,1)S(1)}, u32[]{:S(2)}, u32[]{:S(2)}) collective-permute-start(bf16[192,256]{1,0:T(8,128)(2,1)S(1)} %get-tuple-element.42), channel_id=1, source_target_pairs={{0,2},{1,3},{2,0},{3,1},{4,6},{5,7},{6,4},{7,5},{8,10},{9,11},{10,... | collective-permute-start | bytes 294920 | tf_op jit(solution)/shard_map/ppermute | solution.py:307
  14.2 5.3 %collective-permute-start.6 = (bf16[256,128]{1,0:T(8,128)(2,1)S(1)}, bf16[256,128]{1,0:T(8,128)(2,1)S(1)}, u32[]{:S(2)}, u32[]{:S(2)}) collective-permute-start(bf16[256,128]{1,0:T(8,128)(2,1)S(1)} %get-tuple-element.40.key_a), channel_id=1, source_target_pairs={{0,4},{1,5},{2,6},{3,7},{4,0},{5,1},{6,2},{7,3},{8,12},{9,13},{10,... | collective-permute-start | bytes 196616 | tf_op jit(solution)/shard_map/ppermute | solution.py:307
  15.8 3.7 %collective-permute-start.5 = (f32[8,256]{1,0:T(8,128)S(1)}, f32[8,256]{1,0:T(8,128)S(1)}, u32[]{:S(2)}, u32[]{:S(2)}) collective-permute-start(f32[8,256]{1,0:T(8,128)S(1)} %get-tuple-element.39.stat_a), channel_id=1, source_target_pairs={{0,4},{1,5},{2,6},{3,7},{4,0},{5,1},{6,2},{7,3},{8,12},{9,13},{10,... | collective-permute-start | bytes 24584 | tf_op jit(solution)/shard_map/ppermute | solution.py:307
  19.6 9.3 %copy-start.1 = (bf16[1024,128]{1,0:T(8,128)(2,1)S(1)}, bf16[1024,128]{1,0:T(8,128)(2,1)}, u32[]{:S(2)}) copy-start(bf16[1024,128]{1,0:T(8,128)(2,1)} %query_ref.1) | copy-start | bytes 786436
  19.6 7.9 %collective-permute-start.10 = (bf16[192,256]{1,0:T(8,128)(2,1)S(1)}, bf16[192,256]{1,0:T(8,128)(2,1)S(1)}, u32[]{:S(2)}, u32[]{:S(2)}) collective-permute-start(bf16[192,256]{1,0:T(8,128)(2,1)S(1)} %get-tuple-element.45.sum_a), channel_id=1, source_target_pairs={{0,4},{1,5},{2,6},{3,7},{4,0},{5,1},{6,2},{7,3},{8,12},{9,13},{10,... | collective-permute-start | bytes 294920 | tf_op jit(solution)/shard_map/ppermute | solution.py:307
  20.3 7.1 %collective-permute-start.9 = (bf16[256,128]{1,0:T(8,128)(2,1)S(1)}, bf16[256,128]{1,0:T(8,128)(2,1)S(1)}, u32[]{:S(2)}, u32[]{:S(2)}) collective-permute-start(bf16[256,128]{1,0:T(8,128)(2,1)S(1)} %get-tuple-element.44.key_a), channel_id=1, source_target_pairs={{0,8},{1,9},{2,10},{3,11},{4,12},{5,13},{6,14},{7,15},{8,0},{9,1},... | collective-permute-start | bytes 196616 | tf_op jit(solution)/shard_map/ppermute | solution.py:307
  22.9 4.5 %collective-permute-start.8 = (f32[8,256]{1,0:T(8,128)S(1)}, f32[8,256]{1,0:T(8,128)S(1)}, u32[]{:S(2)}, u32[]{:S(2)}) collective-permute-start(f32[8,256]{1,0:T(8,128)S(1)} %get-tuple-element.43.stat_a), channel_id=1, source_target_pairs={{0,8},{1,9},{2,10},{3,11},{4,12},{5,13},{6,14},{7,15},{8,0},{9,1},... | collective-permute-start | bytes 24584 | tf_op jit(solution)/shard_map/ppermute | solution.py:307
  27.5 1.3 %collective-permute-start.11 = (bf16[256,128]{1,0:T(8,128)(2,1)S(1)}, bf16[256,128]{1,0:T(8,128)(2,1)S(1)}, u32[]{:S(2)}, u32[]{:S(2)}) collective-permute-start(bf16[256,128]{1,0:T(8,128)(2,1)S(1)} %get-tuple-element.47.own_key_ref), channel_id=1, source_target_pairs={{0,1},{1,0},{2,3},{3,2},{4,5},{5,4},{6,7},{7,6},{8,9},{9,8},{10,11... | collective-permute-start | bytes 196616 | tf_op jit(solution)/shard_map/ppermute | solution.py:307
  27.6 1.2 %copy-start.2 = (s32[16]{0:T(128)S(1)}, s32[16]{0:T(128)}, u32[]{:S(2)}) copy-start(s32[16]{0:T(128)} %len_ref.1) | copy-start | bytes 196
  27.6 8.2 %collective-permute-start.12 = (bf16[192,256]{1,0:T(8,128)(2,1)S(1)}, bf16[192,256]{1,0:T(8,128)(2,1)S(1)}, u32[]{:S(2)}, u32[]{:S(2)}) collective-permute-start(bf16[192,256]{1,0:T(8,128)(2,1)S(1)} %get-tuple-element.57.sum_a), channel_id=1, source_target_pairs={{0,8},{1,9},{2,10},{3,11},{4,12},{5,13},{6,14},{7,15},{8,0},{9,1},... | collective-permute-start | bytes 294920 | tf_op jit(solution)/shard_map/ppermute | solution.py:307
  35.9 5.9 %collective-permute-start.13 = (bf16[192,256]{1,0:T(8,128)(2,1)S(1)}, bf16[192,256]{1,0:T(8,128)(2,1)S(1)}, u32[]{:S(2)}, u32[]{:S(2)}) collective-permute-start(bf16[192,256]{1,0:T(8,128)(2,1)S(1)} %shard_map.84.part0), channel_id=1, source_target_pairs={{0,2},{1,3},{2,0},{3,1},{4,6},{5,7},{6,4},{7,5},{8,10},{9,11},{10,... | collective-permute-start | bytes 294920 | tf_op jit(solution)/shard_map/ppermute | solution.py:307
  41.7 1.3 %collective-permute-start.14 = (bf16[192,256]{1,0:T(8,128)(2,1)S(1)}, bf16[192,256]{1,0:T(8,128)(2,1)S(1)}, u32[]{:S(2)}, u32[]{:S(2)}) collective-permute-start(bf16[192,256]{1,0:T(8,128)(2,1)S(1)} %shard_map.84.part0), channel_id=1, source_target_pairs={{0,1},{1,0},{2,3},{3,2},{4,5},{5,4},{6,7},{7,6},{8,9},{9,8},{10,11... | collective-permute-start | bytes 294920 | tf_op jit(solution)/shard_map/ppermute | solution.py:307
  41.8 1.5 %copy-start = (f32[1,512]{1,0:T(1,128)S(1)}, f32[1,512]{1,0:T(1,128)}, u32[]{:S(2)}) copy-start(f32[1,512]{1,0:T(1,128)} %get-tuple-element.54.weight_ref) | copy-start | bytes 6148
  41.8 1.5 %collective-permute-start.15 = (bf16[192,256]{1,0:T(8,128)(2,1)S(1)}, bf16[192,256]{1,0:T(8,128)(2,1)S(1)}, u32[]{:S(2)}, u32[]{:S(2)}) collective-permute-start(bf16[192,256]{1,0:T(8,128)(2,1)S(1)} %shard_map.85.part1), channel_id=1, source_target_pairs={{0,1},{1,0},{2,3},{3,2},{4,5},{5,4},{6,7},{7,6},{8,9},{9,8},{10,11... | collective-permute-start | bytes 294920 | tf_op jit(solution)/shard_map/ppermute | solution.py:307

commit v4 on v3

v4 whole, which is shorter than its diff:
```python
import jax
import jax.numpy as jnp
from jax import lax
from jax.experimental import pallas as pl
from jax.experimental.pallas import tpu as pltpu
from jax.sharding import PartitionSpec as P

DH = 128
NQ = 1024
M = 512
QB = 32
SELECT_FROM = 256
NNLS_STEPS = 8
NS_ITERS = 9
SUM_FLOPS = 10**9
CHUNKS = 4
CHUNK = NQ // CHUNKS
QUARTER_M = M // CHUNKS
SUM_ROWS = DH + QUARTER_M // 2
PAIR_ROWS = SUM_ROWS + DH
HALF_M = M // 2

ridge_weight = 4.0
nnls_ridge = 0.1
floor_value = -1e30
EXP2_SCALE = DH ** (-0.5) * 1.4426950408889634

f32 = jnp.float32
bf16 = jnp.bfloat16
NN = (((1,), (0,)), ((), ()))
NT = (((1,), (1,)), ((), ()))
TN = (((0,), (0,)), ((), ()))


def mm(left, right, dims):
    return lax.dot_general(left, right, dims, preferred_element_type=f32)


def split(x):
    high = x.astype(bf16)
    return high, (x - high.astype(f32)).astype(bf16)


def mm3(left, right, dims):
    return mm(left[0], right[0], dims) + (mm(left[0], right[1], dims) + mm(left[1], right[0], dims))


def total_of(x):
    return jnp.sum(jnp.sum(x, axis=0, keepdims=True), axis=1, keepdims=True)


def place(number, size):
    return pl.ds(pl.multiple_of(number * size, size), size)


def bits():
    me = lax.axis_index("wide")
    return me, lax.rem(me, 2), lax.rem(lax.div(me, 2), 2)


PRIOR = SUM_ROWS - DH
PIECE_ROWS = SUM_ROWS // 2
EVERYTHING = slice(0, CHUNK)


def put_pair(out_ref, columns, prior, sums):
    high, low = split(sums)
    out_ref[:PRIOR, columns] = prior
    out_ref[PRIOR:SUM_ROWS, columns] = high
    out_ref[SUM_ROWS:, columns] = low


def get_pair(ref, columns):
    high = ref[PRIOR:SUM_ROWS, columns].astype(f32)
    return ref[:PRIOR, columns], high + ref[SUM_ROWS:, columns].astype(f32)


def put_pieces(first_ref, second_ref, prior, sums):
    sums = sums.astype(bf16)
    first_ref[:PRIOR, :] = prior
    first_ref[PRIOR:, :] = sums[: PIECE_ROWS - PRIOR]
    second_ref[...] = sums[PIECE_ROWS - PRIOR :]


def get_pieces(first_ref, second_ref):
    sums = jnp.concatenate([first_ref[PRIOR:, :], second_ref[...]], axis=0)
    return first_ref[:PRIOR, :], sums.astype(f32)


KEY_ROWS = HALF_M // 2
HEAD_ROWS = KEY_ROWS + 32


def put_keys(out_ref, keys):
    out_ref[:KEY_ROWS, :DH] = keys[:KEY_ROWS]
    out_ref[:KEY_ROWS, DH:] = keys[KEY_ROWS:]


def put_stats(out_ref, stats):
    high = stats.astype(bf16).astype(f32)
    middle = (stats - high).astype(bf16).astype(f32)
    low = stats - high - middle
    out_ref[KEY_ROWS:, :] = jnp.concatenate([high, middle, low, jnp.zeros_like(low)], axis=0).astype(bf16)


def get_stats(ref):
    parts = ref[KEY_ROWS:, :].astype(f32)
    return parts[:8] + parts[8:16] + parts[16:24]


def attention_kernel(
    len_hbm, exp_hbm, index_hbm, mant_hbm, value_hbm, query_hbm,
    send_head_ref, keep_head_ref, send_ref, keep_ref,
    stat_ref, len_ref, exp_ref, index_ref, mant_ref, value_ref, query_ref, key_ref, sems,
):
    copies = [
        pltpu.make_async_copy(source, target, sems.at[i])
        for i, (source, target) in enumerate(
            (
                (exp_hbm, exp_ref),
                (mant_hbm, mant_ref),
                (query_hbm, query_ref),
                (len_hbm, len_ref),
                (index_hbm, index_ref),
                (value_hbm, value_ref),
            )
        )
    ]
    for copy in copies:
        copy.start()
    ctx = mant_ref.shape[0]
    me, core, bit = bits()
    for copy in copies:
        copy.wait()
    for b in range(ctx // QB):
        exponent = exp_ref[b]
        factor = jnp.where(exponent > 0, 2.0, jnp.where(exponent < 0, 0.5, 1.0)).astype(f32)
        rows = pl.ds(b * QB, QB)
        key_ref[rows, :] = (mant_ref[rows, :].astype(f32) * factor).astype(bf16)
    half_m = M // 2
    position = lax.broadcasted_iota(jnp.int32, (SELECT_FROM, half_m), 0)
    for half, head_out, out in ((1 - core, send_head_ref, send_ref), (core, keep_head_ref, keep_ref)):
        wanted = index_ref[:, place(half, half_m)] - me * ctx
        chosen = jnp.where(position == wanted, 1.0, 0.0).astype(bf16)
        put_keys(head_out, mm(chosen, key_ref[:SELECT_FROM, :], TN).astype(bf16))
        prior = mm(value_ref[:SELECT_FROM, :], chosen, TN).astype(bf16)
        for piece in range(2):
            for part in range(2):
                begin = piece * CHUNK + part * QUARTER_M
                out[:PRIOR, begin : begin + QUARTER_M] = prior[
                    part * (DH // 2) : (part + 1) * (DH // 2), piece * QUARTER_M : (piece + 1) * QUARTER_M
                ]
    dead = lax.broadcasted_iota(jnp.int32, (ctx, CHUNK), 0) >= len_ref[me]
    for half, out in ((1 - core, send_ref), (core, keep_ref)):
        for c in range(2):
            number = half * 2 + c
            scores = mm(key_ref[...], query_ref[place(number, CHUNK), :], NT)
            scores = jnp.where(dead, floor_value, scores)
            row_max = jnp.max(scores, axis=0, keepdims=True)
            attn = jnp.exp2((scores - row_max) * EXP2_SCALE)
            stat_ref[pl.ds(number, 1), :] = row_max
            stat_ref[pl.ds(CHUNKS + number, 1), :] = jnp.sum(attn, axis=0, keepdims=True)
            sums = mm(value_ref[...], attn.astype(bf16), TN)
            high, low = split(sums)
            out[PRIOR:SUM_ROWS, c * CHUNK : (c + 1) * CHUNK] = high
            out[SUM_ROWS:, c * CHUNK : (c + 1) * CHUNK] = low
    put_stats(send_head_ref, stat_ref[...])
    put_stats(keep_head_ref, stat_ref[...])


def join_kernel(first_ref, second_ref, out_ref, scale_out):
    first, second = get_stats(first_ref), get_stats(second_ref)
    joint = jnp.maximum(first[:CHUNKS], second[:CHUNKS])
    scale_first = jnp.exp2((first[:CHUNKS] - joint) * EXP2_SCALE)
    scale_second = jnp.exp2((second[:CHUNKS] - joint) * EXP2_SCALE)
    mass = first[CHUNKS:] * scale_first + second[CHUNKS:] * scale_second
    put_stats(out_ref, jnp.concatenate([joint, mass], axis=0))
    out_ref[:KEY_ROWS, :] = first_ref[:KEY_ROWS, :] + second_ref[:KEY_ROWS, :]
    scale_out[...] = scale_first


def last_join_kernel(first_ref, second_ref, key_out, stat_out, scale_out):
    first, second = get_stats(first_ref), get_stats(second_ref)
    joint = jnp.maximum(first[:CHUNKS], second[:CHUNKS])
    scale_first = jnp.exp2((first[:CHUNKS] - joint) * EXP2_SCALE)
    scale_second = jnp.exp2((second[:CHUNKS] - joint) * EXP2_SCALE)
    stat_out[:CHUNKS, :] = joint
    stat_out[CHUNKS:, :] = first[CHUNKS:] * scale_first + second[CHUNKS:] * scale_second
    for c in range(2):
        columns = slice(c * DH, (c + 1) * DH)
        rows = slice(c * KEY_ROWS, (c + 1) * KEY_ROWS)
        key_out[rows, :] = first_ref[:KEY_ROWS, columns] + second_ref[:KEY_ROWS, columns]
    scale_out[...] = scale_first


def core_sum_kernel(scale_ref, send_in, keep_in, send_out, keep_out):
    me, core, bit = bits()
    for half, source, out in ((1 - core, send_in, send_out), (core, keep_in, keep_out)):
        for c in range(2):
            columns = pl.ds(c * CHUNK, CHUNK)
            prior, sums = get_pair(source, columns)
            put_pair(out, columns, prior, sums * scale_ref[pl.ds(half * 2 + c, 1), :])


def halve_sum_kernel(scale_ref, sum_a, sum_b, first_out, second_out, keep_out):
    me, core, bit = bits()

    def half_of(half):
        columns = place(half, CHUNK)
        prior_a, sums_a = get_pair(sum_a, columns)
        prior_b, sums_b = get_pair(sum_b, columns)
        return prior_a + prior_b, (sums_a + sums_b) * scale_ref[pl.ds(core * 2 + half, 1), :]

    put_pieces(first_out, second_out, *half_of(1 - bit))
    put_pair(keep_out, EVERYTHING, *half_of(bit))


def own_sums(refs):
    return get_pair(refs[0], EVERYTHING) if len(refs) == 1 else get_pieces(*refs)


def join_sum_kernel(scale_ref, *refs):
    me, core, bit = bits()
    prior_a, sums_a = own_sums(refs[:-4])
    prior_b, sums_b = get_pieces(*refs[-4:-2])
    factor = scale_ref[pl.ds(core * 2 + bit, 1), :]
    put_pieces(*refs[-2:], prior_a + prior_b, (sums_a + sums_b) * factor)


def outputs_kernel(stat_ref, first_a, second_a, first_b, second_b, after_ref, first_out, second_out):
    me, core, bit = bits()
    prior_a, sums_a = get_pieces(first_a, second_a)
    prior_b, sums_b = get_pieces(first_b, second_b)
    row_mass = stat_ref[pl.ds(CHUNKS + core * 2 + bit, 1), :]
    put_pieces(first_out, second_out, prior_a + prior_b, (sums_a + sums_b) / row_mass)


def gram3(high, low):
    top = mm3((high[:HALF_M], low[:HALF_M]), (high, low), NT)
    corner = mm3((high[HALF_M:], low[HALF_M:]), (high[HALF_M:], low[HALF_M:]), NT)
    return top, jnp.concatenate([top[:, HALF_M:].T, corner], axis=1)


def feature_kernel(
    len_ref, query_ref, stat_ref, own_key_ref, other_key_ref,
    gram_ref, linear_ref, norm_ref, scaled_hi, scaled_lo,
    key_ref, feat_hi, feat_lo,
):
    me, core, bit = bits()
    total = len_ref[0]
    for i in range(1, len_ref.shape[0]):
        total = total + len_ref[i]
    live_total = jnp.full((1, 1), total, jnp.int32).astype(f32)
    key_ref[place(core, M // 2), :] = own_key_ref[...]
    key_ref[place(1 - core, M // 2), :] = other_key_ref[...]
    frobenius = jnp.zeros((1, 1), f32)
    linear = jnp.zeros((M, DH), f32)
    for c in range(CHUNKS):
        columns = pl.ds(c * CHUNK, CHUNK)
        row_max, row_mass = stat_ref[c : c + 1, :], stat_ref[CHUNKS + c : CHUNKS + c + 1, :]
        scores = mm(key_ref[...], query_ref[columns, :], NT)
        features = jnp.exp2((scores - row_max) * EXP2_SCALE)
        target = row_mass * (M / live_total)
        high, low = split(features)
        feat_hi[:, columns] = high
        feat_lo[:, columns] = low
        frobenius = frobenius + total_of(features * features)
        weighted = features * target
        for tile in range(CHUNK // DH):
            linear = linear + weighted[:, tile * DH : (tile + 1) * DH]
        high, low = split(features * (1.0 / target))
        scaled_hi[:, columns] = high
        scaled_lo[:, columns] = low
    gram_ref[:HALF_M, :], gram_ref[HALF_M:, :] = gram3(feat_hi[...], feat_lo[...])
    linear_ref[...] = jnp.broadcast_to(jnp.sum(linear, axis=1, keepdims=True), (M, DH))
    norm_ref[...] = jnp.broadcast_to(frobenius, norm_ref.shape)


def weight_kernel(
    gram_ref, linear_ref, norm_ref, scaled_hi, scaled_lo,
    weight_out, factor_out, power_out, attend_ref,
):
    frobenius = norm_ref[:1, :1]
    damping = nnls_ridge * (frobenius / M + 1e-6)
    stepsize = 1.0 / (frobenius + damping)
    linear_column = linear_ref[...]
    linear_row = linear_column.T[:1]
    row = jnp.ones((1, M), f32)
    column = jnp.ones((M, DH), f32)
    tiles = [slice(t * DH, (t + 1) * DH) for t in range(M // DH)]

    def moved(weights, product, linear):
        gradient = product - linear + damping * weights
        return jnp.maximum(weights - stepsize * gradient, 0.0)

    for number in range(NNLS_STEPS):
        down = [jnp.sum(gram_ref[:, t] * column, axis=0, keepdims=True) for t in tiles]
        along = gram_ref[:, tiles[0]] * row[:, tiles[0]]
        for t in tiles[1:]:
            along = along + gram_ref[:, t] * row[:, t]
        along = jnp.broadcast_to(jnp.sum(along, axis=1, keepdims=True), (M, DH))
        row = moved(row, jnp.concatenate(down, axis=1), linear_row)
        column = moved(column, along, linear_column)
        if number % 2 == 0 and number // 2 < CHUNKS:
            columns = pl.ds(number // 2 * CHUNK, CHUNK)
            top, corner = gram3(scaled_hi[:, columns], scaled_lo[:, columns])
            attend_ref[:HALF_M, :] = top if number == 0 else attend_ref[:HALF_M, :] + top
            attend_ref[HALF_M:, :] = corner if number == 0 else attend_ref[HALF_M:, :] + corner
    weight_out[...] = row
    gram = attend_ref[...] * row
    gram = gram * jnp.concatenate([column] * (M // DH), axis=1)
    diagonal = lax.broadcasted_iota(jnp.int32, (M, M), 0) == lax.broadcasted_iota(
        jnp.int32, (M, M), 1
    )
    ridge = ridge_weight * (total_of(jnp.where(diagonal, gram, 0.0)) / M + 1e-6)
    system = gram + jnp.where(diagonal, ridge, 0.0)
    bound = jnp.max(jnp.sum(jnp.abs(system), axis=0, keepdims=True), axis=1, keepdims=True)
    row = lax.broadcasted_iota(jnp.int32, factor_out.shape, 0)
    factor_out[...] = jnp.where(row == 0, ridge, bound)
    power_out[...] = system * (1.0 / bound)


def forward_kernel(own_first, own_second, side_first, side_second, after_ref, out_ref):
    for i, ref in enumerate((own_first, own_second, side_first, side_second)):
        out_ref[i * PIECE_ROWS : (i + 1) * PIECE_ROWS, :] = ref[...]


def right_side(half_ref, half, bit, scaled_hi, scaled_lo, prior_ref):
    product = None
    for i, lo_bit in enumerate((bit, 1 - bit)):
        number = half * 2 + lo_bit
        begin = i * SUM_ROWS
        lanes = place(number, QUARTER_M)
        prior_ref[: DH // 2, lanes] = half_ref[begin : begin + PRIOR, :QUARTER_M].astype(f32)
        prior_ref[DH // 2 :, lanes] = half_ref[begin : begin + PRIOR, QUARTER_M:].astype(f32)
        outputs = half_ref[begin + PRIOR : begin + SUM_ROWS, :]
        columns = place(number, CHUNK)
        part = mm(outputs, scaled_hi[:, columns], NT) + mm(outputs, scaled_lo[:, columns], NT)
        product = part if product is None else product + part
    return product


def refit_kernel(
    power_in, weight_ref, factor_ref, scaled_hi, scaled_lo, own_ref, half_ref,
    value_out, both_ref, prior_ref,
):
    me, core, bit = bits()
    product = right_side(own_ref, core, bit, scaled_hi, scaled_lo, prior_ref)
    product = product + right_side(half_ref, 1 - core, bit, scaled_hi, scaled_lo, prior_ref)
    ridge, bound = factor_ref[0:1, :1], factor_ref[1:2, :1]
    both_ref[DH:, :] = power_in[...]
    both_ref[:DH, :] = (weight_ref[...] * product + ridge * prior_ref[...]) * (1.0 / bound)
    above = DH + HALF_M

    def newton_step(number, carry):
        high, low = split(both_ref[...])
        power = (high[DH:], low[DH:])
        top = 2.0 * both_ref[:above, :] - mm3((high[:above], low[:above]), power, NN)
        corner = mm3((high[above:], low[above:]), (power[0][:, HALF_M:], power[1][:, HALF_M:]), NN)
        both_ref[above:, HALF_M:] = 2.0 * both_ref[above:, HALF_M:] - corner
        both_ref[above:, :HALF_M] = top[DH:, HALF_M:].T
        both_ref[:above, :] = top
        return carry

    lax.fori_loop(0, NS_ITERS - 2, newton_step, 0)
    power = split(both_ref[DH:, :])
    refit = both_ref[:DH, :]
    refit = 2.0 * refit - mm3(split(refit), power, NN)
    once = mm3(split(refit), power, NN)
    refit = 2.0 * (refit - once) + mm3(split(once), power, NN)
    value_out[...] = refit.T


def shape(rows, columns, dtype):
    return jax.ShapeDtypeStruct((rows, columns), dtype)


def call(kernel, outs, arrays, scalars=0, scratch=(), in_specs=None, flops=None, limit=48):
    return pl.pallas_call(
        kernel,
        out_shape=tuple(outs),
        in_specs=in_specs
        or [pl.BlockSpec(memory_space=pltpu.SMEM)] * scalars
        + [pl.BlockSpec(memory_space=pltpu.VMEM)] * (len(arrays) - scalars),
        out_specs=tuple([pl.BlockSpec(memory_space=pltpu.VMEM)] * len(outs)),
        scratch_shapes=list(scratch),
        compiler_params=pltpu.CompilerParams(vmem_limit_bytes=int(limit * 1024 * 1024)),
        cost_estimate=None
        if flops is None
        else pl.CostEstimate(flops=flops, bytes_accessed=1024, transcendentals=0),
    )(*arrays)


def per_device(key_mant, scale_exp, values, queries, compact_index, shard_lengths):
    wide_count = lax.axis_size("wide")
    ctx = key_mant.shape[0]

    def exchanged(array, mask):
        return lax.ppermute(array, "wide", [(i, i ^ mask) for i in range(wide_count)])

    head_shape = shape(HEAD_ROWS, CHUNK, bf16)
    scale_shape = shape(CHUNKS, CHUNK, f32)
    half_sum = shape(PAIR_ROWS, 2 * CHUNK, bf16)
    pieces = (shape(PIECE_ROWS, CHUNK, bf16),) * 2

    send_head, head, send, keep = call(
        attention_kernel,
        (head_shape, head_shape, half_sum, half_sum),
        [
            pltpu.with_memory_space_constraint(array, pltpu.HBM)
            for array in (
                shard_lengths, scale_exp, compact_index.reshape(1, M), key_mant, values, queries
            )
        ],
        in_specs=[pl.BlockSpec(memory_space=pltpu.HBM)] * 6,
        flops=10**9,
        scratch=[
            pltpu.VMEM((2 * CHUNKS, CHUNK), f32),
            pltpu.SMEM(shard_lengths.shape, jnp.int32),
            pltpu.SMEM(scale_exp.shape, jnp.int32),
            pltpu.VMEM((1, M), jnp.int32),
            pltpu.VMEM((ctx, DH), bf16),
            pltpu.VMEM((ctx, DH), bf16),
            pltpu.VMEM((NQ, DH), bf16),
            pltpu.VMEM((ctx, DH), bf16),
            pltpu.SemaphoreType.DMA((6,)),
        ],
    )
    def both_exchanged(arrays, mask):
        return tuple(exchanged(array, mask) for array in arrays)

    head, scale = call(join_kernel, (head_shape, scale_shape), (head, exchanged(send_head, 1)))
    got_head = exchanged(head, 2)
    send, keep = call(core_sum_kernel, (half_sum, half_sum), (scale, send, keep), flops=SUM_FLOPS)
    got = exchanged(send, 1)
    masks = [4]
    while 2 * masks[-1] < wide_count:
        masks.append(2 * masks[-1])
    head, scale = call(join_kernel, (head_shape, scale_shape), (head, got_head))
    got_head = exchanged(head, masks[0])
    first, second, keep = call(
        halve_sum_kernel,
        pieces + (shape(PAIR_ROWS, CHUNK, bf16),),
        (scale, keep, got),
        flops=SUM_FLOPS,
    )
    sums, got = (keep,), both_exchanged((first, second), 2)
    for number, mask in enumerate(masks):
        if number + 1 < len(masks):
            head, scale = call(join_kernel, (head_shape, scale_shape), (head, got_head))
            got_head = exchanged(head, masks[number + 1])
        else:
            keys, stats, scale = call(
                last_join_kernel,
                (shape(HALF_M, DH, bf16), shape(2 * CHUNKS, CHUNK, f32), scale_shape),
                (head, got_head),
            )
            got_keys = exchanged(keys, 1)
        sums = call(join_sum_kernel, pieces, (scale,) + sums + got, flops=SUM_FLOPS)
        got = both_exchanged(sums, mask)
    gram, linear, norm, scaled_hi, scaled_lo = call(
        feature_kernel,
        (shape(M, M, f32), shape(M, DH, f32), shape(8, DH, f32)) + (shape(M, NQ, bf16),) * 2,
        (shard_lengths, queries, stats, keys, got_keys),
        scalars=1,
        flops=4 * 10**9,
        scratch=[pltpu.VMEM((M, DH), bf16), pltpu.VMEM((M, NQ), bf16), pltpu.VMEM((M, NQ), bf16)],
    )
    outputs = call(outputs_kernel, pieces, (stats,) + tuple(sums) + got + (norm,))
    side = both_exchanged(outputs, 2)
    weights, factor, power = call(
        weight_kernel,
        (shape(1, M, f32), shape(8, DH, f32), shape(M, M, f32)),
        (gram, linear, norm, scaled_hi, scaled_lo),
        flops=5 * 10**9,
        scratch=[pltpu.VMEM((M, M), f32)],
    )
    (half,) = call(
        forward_kernel,
        (shape(2 * SUM_ROWS, CHUNK, bf16),),
        tuple(outputs) + side + (factor,),
    )
    (compact_values,) = call(
        refit_kernel,
        (shape(M, DH, f32),),
        (power, weights, factor, scaled_hi, scaled_lo, half, exchanged(half, 1)),
        scratch=[
            pltpu.VMEM((M + DH, M), f32),
            pltpu.VMEM((DH, M), f32),
        ],
    )
    return weights.reshape(M), compact_values


def solution(mesh):
    placed = (
        P(("groups", "wide"), None),
        P(("groups", "wide")),
        P(("groups", "wide"), None),
        P("groups", None),
        P("groups"),
        P("groups"),
    )
    return jax.shard_map(
        per_device,
        mesh=mesh,
        in_specs=placed,
        out_specs=(P("groups"), P("groups", None)),
        check_vma=False,
    )
```

time: 55 us -> 50.4 us (0.916)
  Pallas kernels: 25.7 us -> 20.9 us
  starting transfers between devices: 13.1 us -> 17.8 us
  waiting for transfers between devices: 15.3 us -> 10.9 us
    pallas_call x10 -> x14, Pallas kernels: 25.7 us -> 20.9 us  [call(): pl.pallas_call(kernel, out_shape=tuple(outs), in_specs=in_specs or [pl.Bl...]
    ppermute x16 -> x15, starting transfers between devices: 13.1 us -> 17.8 us  [exchanged(): lax.ppermute(array, 'wide', [(i, i ^ mask) for i in range(wide_count)])]
    ppermute x16 -> x15, waiting for transfers between devices: 15.3 us -> 10.9 us  [exchanged(): lax.ppermute(array, 'wide', [(i, i ^ mask) for i in range(wide_count)])]
  transfers between devices with their start and end apart: 16 -> 15, of which waited for: 8 -> 10; matrix products, arithmetic and copies ran while one was open for 0% -> 0% of each run, Pallas kernels for 18% -> 13%
where the time goes in v4:
time: 50.4 us; the launch traced here: 50.3 us
  Pallas kernels  20.9 us (41%)
  starting transfers between devices  17.8 us (35%)
  waiting for transfers between devices  10.9 us (22%)
  between operations  0.73 us (1%)
    pallas_call x14, Pallas kernels, call(): pl.pallas_call(kernel, out_shape=tuple(outs), in_specs=in_specs or [pl.Bl...  20.9 us
    ppermute x15, starting transfers between devices, exchanged(): lax.ppermute(array, 'wide', [(i, i ^ mask) for i in range(wide_count)])  17.8 us
    ppermute x15, waiting for transfers between devices, exchanged(): lax.ppermute(array, 'wide', [(i, i ^ mask) for i in range(wide_count)])  10.9 us
  transfers between devices with their start and end apart: 15, of which 10 were waited for; matrix products, arithmetic and copies ran while one was open for 0% of the time, Pallas kernels for 13%

profile of v4, /device:TPU:0, one launch (start us, length us, event | category | flops | bytes accessed | tf_op | source)
XLA Modules:
  0.0 50.3 jit_solution(6134007657066205969)
XLA Ops:
  0.6 4.2 %shard_map.77 = (bf16[160,256]{1,0:T(8,128)(2,1)S(1)}, bf16[160,256]{1,0:T(8,128)(2,1)S(1)}, bf16[320,512]{1,0:T(8,128)(2,1)S(1)}, bf16[320,512]{1,0:T(8,128)(2,1)S(1)}) custom-call(s32[16]{0:T(128)} %len_ref.1, s32[32]{0:T(128)} %exp_hbm.1, s32[1,512]{1,0:T(1,128)} %bitcast.3, bf16[1024,128]{1,0:T(8,128)(2,1)} %mant_hbm.1, bf16[1024,128]{1,0:T(8,128)(2,1)} %value_hbm.1, ...), custom_call_target="tpu_custom_call" | custom-call | flops 1000000000 | bytes 1024 | tf_op jit(solution)/shard_map/pallas_call | solution.py:379
  4.9 0.5 %collective-permute-start = (bf16[160,256]{1,0:T(8,128)(2,1)S(1)}, bf16[160,256]{1,0:T(8,128)(2,1)S(1)}, u32[]{:S(2)}, u32[]{:S(2)}) collective-permute-start(bf16[160,256]{1,0:T(8,128)(2,1)S(1)} %get-tuple-element.35), channel_id=1, source_target_pairs={{0,1},{1,0},{2,3},{3,2},{4,5},{5,4},{6,7},{7,6},{8,9},{9,8},{10,11... | collective-permute-start | bytes 245768 | tf_op jit(solution)/shard_map/ppermute | solution.py:399
  5.4 0.9 %collective-permute-done.second_ref = bf16[160,256]{1,0:T(8,128)(2,1)S(1)} collective-permute-done((bf16[160,256]{1,0:T(8,128)(2,1)S(1)}, bf16[160,256]{1,0:T(8,128)(2,1)S(1)}, u32[]{:S(2)}, u32[]{:S(2)}) %collective-permute-start) | collective-permute-done | bytes 81952 | tf_op jit(solution)/shard_map/ppermute | solution.py:399
  6.4 0.1 shard_map.84
  6.5 0.4 collective-permute-start.5
  6.9 2.7 %collective-permute-start.1 = (bf16[160,256]{1,0:T(8,128)(2,1)S(1)}, bf16[160,256]{1,0:T(8,128)(2,1)S(1)}, u32[]{:S(2)}, u32[]{:S(2)}) collective-permute-start(bf16[160,256]{1,0:T(8,128)(2,1)S(1)} %get-tuple-element.36.first_ref), channel_id=1, source_target_pairs={{0,2},{1,3},{2,0},{3,1},{4,6},{5,7},{6,4},{7,5},{8,10},{9,11},{10,... | collective-permute-start | bytes 245768 | tf_op jit(solution)/shard_map/ppermute | solution.py:399
  9.6 3.0 %collective-permute-done.1.second_ref = bf16[160,256]{1,0:T(8,128)(2,1)S(1)} collective-permute-done((bf16[160,256]{1,0:T(8,128)(2,1)S(1)}, bf16[160,256]{1,0:T(8,128)(2,1)S(1)}, u32[]{:S(2)}, u32[]{:S(2)}) %collective-permute-start.1) | collective-permute-done | bytes 81952 | tf_op jit(solution)/shard_map/ppermute | solution.py:399
  12.6 1.9 %collective-permute-start.2 = (bf16[160,256]{1,0:T(8,128)(2,1)S(1)}, bf16[160,256]{1,0:T(8,128)(2,1)S(1)}, u32[]{:S(2)}, u32[]{:S(2)}) collective-permute-start(bf16[160,256]{1,0:T(8,128)(2,1)S(1)} %get-tuple-element.37.first_ref), channel_id=1, source_target_pairs={{0,4},{1,5},{2,6},{3,7},{4,0},{5,1},{6,2},{7,3},{8,12},{9,13},{10,... | collective-permute-start | bytes 245768 | tf_op jit(solution)/shard_map/ppermute | solution.py:399
  14.4 0.0 collective-permute-done.5.sum_b
  14.4 0.1 shard_map.85
  14.5 1.6 %collective-permute-start.6 = (bf16[96,256]{1,0:T(8,128)(2,1)S(1)}, bf16[96,256]{1,0:T(8,128)(2,1)S(1)}, u32[]{:S(2)}, u32[]{:S(2)}) collective-permute-start(bf16[96,256]{1,0:T(8,128)(2,1)S(1)} %get-tuple-element.58), channel_id=1, source_target_pairs={{0,2},{1,3},{2,0},{3,1},{4,6},{5,7},{6,4},{7,5},{8,10},{9,11},{10,... | collective-permute-start | bytes 147464 | tf_op jit(solution)/shard_map/ppermute | solution.py:399
  16.1 0.5 %collective-permute-start.7 = (bf16[96,256]{1,0:T(8,128)(2,1)S(1)}, bf16[96,256]{1,0:T(8,128)(2,1)S(1)}, u32[]{:S(2)}, u32[]{:S(2)}) collective-permute-start(bf16[96,256]{1,0:T(8,128)(2,1)S(1)} %get-tuple-element.59), channel_id=1, source_target_pairs={{0,2},{1,3},{2,0},{3,1},{4,6},{5,7},{6,4},{7,5},{8,10},{9,11},{10,... | collective-permute-start | bytes 147464 | tf_op jit(solution)/shard_map/ppermute | solution.py:399
  16.6 0.4 collective-permute-done.2.second_ref
  17.1 2.9 %collective-permute-start.3 = (bf16[160,256]{1,0:T(8,128)(2,1)S(1)}, bf16[160,256]{1,0:T(8,128)(2,1)S(1)}, u32[]{:S(2)}, u32[]{:S(2)}) collective-permute-start(bf16[160,256]{1,0:T(8,128)(2,1)S(1)} %get-tuple-element.38.first_ref), channel_id=1, source_target_pairs={{0,8},{1,9},{2,10},{3,11},{4,12},{5,13},{6,14},{7,15},{8,0},{9,1},... | collective-permute-start | bytes 245768 | tf_op jit(solution)/shard_map/ppermute | solution.py:399
  20.0 0.0 collective-permute-done.6.refs_1_
  20.0 0.2 collective-permute-done.7.refs_2_
  20.3 1.4 %collective-permute-start.8 = (bf16[96,256]{1,0:T(8,128)(2,1)S(1)}, bf16[96,256]{1,0:T(8,128)(2,1)S(1)}, u32[]{:S(2)}, u32[]{:S(2)}) collective-permute-start(bf16[96,256]{1,0:T(8,128)(2,1)S(1)} %get-tuple-element.60.refs_0_), channel_id=1, source_target_pairs={{0,4},{1,5},{2,6},{3,7},{4,0},{5,1},{6,2},{7,3},{8,12},{9,13},{10,... | collective-permute-start | bytes 147464 | tf_op jit(solution)/shard_map/ppermute | solution.py:399
  21.7 0.7 %collective-permute-start.9 = (bf16[96,256]{1,0:T(8,128)(2,1)S(1)}, bf16[96,256]{1,0:T(8,128)(2,1)S(1)}, u32[]{:S(2)}, u32[]{:S(2)}) collective-permute-start(bf16[96,256]{1,0:T(8,128)(2,1)S(1)} %get-tuple-element.61.refs_1_), channel_id=1, source_target_pairs={{0,4},{1,5},{2,6},{3,7},{4,0},{5,1},{6,2},{7,3},{8,12},{9,13},{10,... | collective-permute-start | bytes 147464 | tf_op jit(solution)/shard_map/ppermute | solution.py:399
  22.3 0.3 collective-permute-done.3.second_ref
  22.6 0.1 collective-permute-start.4
  22.7 1.7 %collective-permute-done.8.refs_2_ = bf16[96,256]{1,0:T(8,128)(2,1)S(1)} collective-permute-done((bf16[96,256]{1,0:T(8,128)(2,1)S(1)}, bf16[96,256]{1,0:T(8,128)(2,1)S(1)}, u32[]{:S(2)}, u32[]{:S(2)}) %collective-permute-start.8) | collective-permute-done | bytes 49184 | tf_op jit(solution)/shard_map/ppermute | solution.py:399
  24.4 1.4 %collective-permute-done.9.refs_3_ = bf16[96,256]{1,0:T(8,128)(2,1)S(1)} collective-permute-done((bf16[96,256]{1,0:T(8,128)(2,1)S(1)}, bf16[96,256]{1,0:T(8,128)(2,1)S(1)}, u32[]{:S(2)}, u32[]{:S(2)}) %collective-permute-start.9) | collective-permute-done | bytes 49184 | tf_op jit(solution)/shard_map/ppermute | solution.py:399
  25.8 0.0 copy-start.1
  25.8 1.8 %collective-permute-start.10 = (bf16[96,256]{1,0:T(8,128)(2,1)S(1)}, bf16[96,256]{1,0:T(8,128)(2,1)S(1)}, u32[]{:S(2)}, u32[]{:S(2)}) collective-permute-start(bf16[96,256]{1,0:T(8,128)(2,1)S(1)} %get-tuple-element.62.first_a), channel_id=1, source_target_pairs={{0,8},{1,9},{2,10},{3,11},{4,12},{5,13},{6,14},{7,15},{8,0},{9,1},... | collective-permute-start | bytes 147464 | tf_op jit(solution)/shard_map/ppermute | solution.py:399
  27.6 0.0 copy-start.2
  27.6 1.2 %collective-permute-start.11 = (bf16[96,256]{1,0:T(8,128)(2,1)S(1)}, bf16[96,256]{1,0:T(8,128)(2,1)S(1)}, u32[]{:S(2)}, u32[]{:S(2)}) collective-permute-start(bf16[96,256]{1,0:T(8,128)(2,1)S(1)} %get-tuple-element.63.second_a), channel_id=1, source_target_pairs={{0,8},{1,9},{2,10},{3,11},{4,12},{5,13},{6,14},{7,15},{8,0},{9,1},... | collective-permute-start | bytes 147464 | tf_op jit(solution)/shard_map/ppermute | solution.py:399
  28.8 0.0 collective-permute-done.4.other_key_ref
  28.8 0.0 copy-done.1
  28.8 0.0 copy-done.2
  28.8 3.1 %shard_map.82 = (f32[512,512]{1,0:T(8,128)S(1)}, f32[512,128]{1,0:T(8,128)S(1)}, f32[8,128]{1,0:T(8,128)S(1)}, bf16[512,1024]{1,0:T(8,128)(2,1)S(1)}, bf16[512,1024]{1,0:T(8,128)(2,1)S(1)}) custom-call(s32[16]{0:T(128)S(1)} %copy-done.2, bf16[1024,128]{1,0:T(8,128)(2,1)S(1)} %copy-done.1, f32[8,256]{1,0:T(8,128)S(1)} %get-tuple-element.39.stat_ref, ...), custom_call_target="tpu_custom_call" | custom-call | flops 4000000000 | bytes 1024 | tf_op jit(solution)/shard_map/pallas_call | solution.py:379
  31.9 0.0 collective-permute-done.10.first_b
  31.9 0.7 %collective-permute-done.11.second_b = bf16[96,256]{1,0:T(8,128)(2,1)S(1)} collective-permute-done((bf16[96,256]{1,0:T(8,128)(2,1)S(1)}, bf16[96,256]{1,0:T(8,128)(2,1)S(1)}, u32[]{:S(2)}, u32[]{:S(2)}) %collective-permute-start.11) | collective-permute-done | bytes 49184 | tf_op jit(solution)/shard_map/ppermute | solution.py:399
  32.6 1.9 %collective-permute-start.12 = (bf16[96,256]{1,0:T(8,128)(2,1)S(1)}, bf16[96,256]{1,0:T(8,128)(2,1)S(1)}, u32[]{:S(2)}, u32[]{:S(2)}) collective-permute-start(bf16[96,256]{1,0:T(8,128)(2,1)S(1)} %get-tuple-element.64.own_first), channel_id=1, source_target_pairs={{0,2},{1,3},{2,0},{3,1},{4,6},{5,7},{6,4},{7,5},{8,10},{9,11},{10,... | collective-permute-start | bytes 147464 | tf_op jit(solution)/shard_map/ppermute | solution.py:399
  34.5 0.2 collective-permute-start.13
  34.7 3.1 %shard_map.83 = (f32[1,512]{1,0:T(1,128)}, f32[8,128]{1,0:T(8,128)S(1)}, f32[512,512]{1,0:T(8,128)S(1)}) custom-call(f32[512,512]{1,0:T(8,128)S(1)} %get-tuple-element.41.gram_ref, f32[512,128]{1,0:T(8,128)S(1)} %get-tuple-element.42.linear_ref, f32[8,128]{1,0:T(8,128)S(1)} %get-tuple-element.43.norm_ref.after_ref, ...), custom_call_target="tpu_custom_call" | custom-call | flops 5000000000 | bytes 1024 | tf_op jit(solution)/shard_map/pallas_call | solution.py:379
  37.8 0.0 collective-permute-done.12.side_first
  37.8 0.8 %collective-permute-done.13.side_second = bf16[96,256]{1,0:T(8,128)(2,1)S(1)} collective-permute-done((bf16[96,256]{1,0:T(8,128)(2,1)S(1)}, bf16[96,256]{1,0:T(8,128)(2,1)S(1)}, u32[]{:S(2)}, u32[]{:S(2)}) %collective-permute-start.13) | collective-permute-done | bytes 49184 | tf_op jit(solution)/shard_map/ppermute | solution.py:399
  38.7 0.0 copy-start
  38.7 0.1 collective-permute-start.14
  38.7 1.4 %collective-permute-done.14.half_ref = bf16[384,256]{1,0:T(8,128)(2,1)S(1)} collective-permute-done((bf16[384,256]{1,0:T(8,128)(2,1)S(1)}, bf16[384,256]{1,0:T(8,128)(2,1)S(1)}, u32[]{:S(2)}, u32[]{:S(2)}) %collective-permute-start.14) | collective-permute-done | bytes 196640 | tf_op jit(solution)/shard_map/ppermute | solution.py:399
  40.2 0.0 copy-done
  40.2 10.1 %shard_map.90 = f32[512,128]{1,0:T(8,128)} custom-call(f32[512,512]{1,0:T(8,128)S(1)} %get-tuple-element.47.power_in, f32[1,512]{1,0:T(1,128)S(1)} %copy-done, f32[8,128]{1,0:T(8,128)S(1)} %get-tuple-element.48.after_ref.factor_ref, bf16[512,1024]{1,0:T(8,128)(2,1)S(1)} %get-tuple-element.44.scaled_hi, bf16[512,1024]{1,0:T(8,128)(2,1)S(1)} %get-tuple-element.45.scaled_lo, ...), custom_call_target="tpu_custom_call" | custom-call | tf_op jit(solution)/shard_map/pallas_call | solution.py:379
  (8 shorter events, 0.2 us)
Async XLA Ops:
  4.9 1.4 %collective-permute-start = (bf16[160,256]{1,0:T(8,128)(2,1)S(1)}, bf16[160,256]{1,0:T(8,128)(2,1)S(1)}, u32[]{:S(2)}, u32[]{:S(2)}) collective-permute-start(bf16[160,256]{1,0:T(8,128)(2,1)S(1)} %get-tuple-element.35), channel_id=1, source_target_pairs={{0,1},{1,0},{2,3},{3,2},{4,5},{5,4},{6,7},{7,6},{8,9},{9,8},{10,11... | collective-permute-start | bytes 245768 | tf_op jit(solution)/shard_map/ppermute | solution.py:399
  6.5 8.0 %collective-permute-start.5 = (bf16[320,512]{1,0:T(8,128)(2,1)S(1)}, bf16[320,512]{1,0:T(8,128)(2,1)S(1)}, u32[]{:S(2)}, u32[]{:S(2)}) collective-permute-start(bf16[320,512]{1,0:T(8,128)(2,1)S(1)} %get-tuple-element.56), channel_id=1, source_target_pairs={{0,1},{1,0},{2,3},{3,2},{4,5},{5,4},{6,7},{7,6},{8,9},{9,8},{10,11... | collective-permute-start | bytes 983048 | tf_op jit(solution)/shard_map/ppermute | solution.py:399
  6.9 5.6 %collective-permute-start.1 = (bf16[160,256]{1,0:T(8,128)(2,1)S(1)}, bf16[160,256]{1,0:T(8,128)(2,1)S(1)}, u32[]{:S(2)}, u32[]{:S(2)}) collective-permute-start(bf16[160,256]{1,0:T(8,128)(2,1)S(1)} %get-tuple-element.36.first_ref), channel_id=1, source_target_pairs={{0,2},{1,3},{2,0},{3,1},{4,6},{5,7},{6,4},{7,5},{8,10},{9,11},{10,... | collective-permute-start | bytes 245768 | tf_op jit(solution)/shard_map/ppermute | solution.py:399
  12.6 4.5 %collective-permute-start.2 = (bf16[160,256]{1,0:T(8,128)(2,1)S(1)}, bf16[160,256]{1,0:T(8,128)(2,1)S(1)}, u32[]{:S(2)}, u32[]{:S(2)}) collective-permute-start(bf16[160,256]{1,0:T(8,128)(2,1)S(1)} %get-tuple-element.37.first_ref), channel_id=1, source_target_pairs={{0,4},{1,5},{2,6},{3,7},{4,0},{5,1},{6,2},{7,3},{8,12},{9,13},{10,... | collective-permute-start | bytes 245768 | tf_op jit(solution)/shard_map/ppermute | solution.py:399
  14.5 5.5 %collective-permute-start.6 = (bf16[96,256]{1,0:T(8,128)(2,1)S(1)}, bf16[96,256]{1,0:T(8,128)(2,1)S(1)}, u32[]{:S(2)}, u32[]{:S(2)}) collective-permute-start(bf16[96,256]{1,0:T(8,128)(2,1)S(1)} %get-tuple-element.58), channel_id=1, source_target_pairs={{0,2},{1,3},{2,0},{3,1},{4,6},{5,7},{6,4},{7,5},{8,10},{9,11},{10,... | collective-permute-start | bytes 147464 | tf_op jit(solution)/shard_map/ppermute | solution.py:399
  16.1 4.1 %collective-permute-start.7 = (bf16[96,256]{1,0:T(8,128)(2,1)S(1)}, bf16[96,256]{1,0:T(8,128)(2,1)S(1)}, u32[]{:S(2)}, u32[]{:S(2)}) collective-permute-start(bf16[96,256]{1,0:T(8,128)(2,1)S(1)} %get-tuple-element.59), channel_id=1, source_target_pairs={{0,2},{1,3},{2,0},{3,1},{4,6},{5,7},{6,4},{7,5},{8,10},{9,11},{10,... | collective-permute-start | bytes 147464 | tf_op jit(solution)/shard_map/ppermute | solution.py:399
  17.1 5.5 %collective-permute-start.3 = (bf16[160,256]{1,0:T(8,128)(2,1)S(1)}, bf16[160,256]{1,0:T(8,128)(2,1)S(1)}, u32[]{:S(2)}, u32[]{:S(2)}) collective-permute-start(bf16[160,256]{1,0:T(8,128)(2,1)S(1)} %get-tuple-element.38.first_ref), channel_id=1, source_target_pairs={{0,8},{1,9},{2,10},{3,11},{4,12},{5,13},{6,14},{7,15},{8,0},{9,1},... | collective-permute-start | bytes 245768 | tf_op jit(solution)/shard_map/ppermute | solution.py:399
  20.3 4.2 %collective-permute-start.8 = (bf16[96,256]{1,0:T(8,128)(2,1)S(1)}, bf16[96,256]{1,0:T(8,128)(2,1)S(1)}, u32[]{:S(2)}, u32[]{:S(2)}) collective-permute-start(bf16[96,256]{1,0:T(8,128)(2,1)S(1)} %get-tuple-element.60.refs_0_), channel_id=1, source_target_pairs={{0,4},{1,5},{2,6},{3,7},{4,0},{5,1},{6,2},{7,3},{8,12},{9,13},{10,... | collective-permute-start | bytes 147464 | tf_op jit(solution)/shard_map/ppermute | solution.py:399
  21.7 4.1 %collective-permute-start.9 = (bf16[96,256]{1,0:T(8,128)(2,1)S(1)}, bf16[96,256]{1,0:T(8,128)(2,1)S(1)}, u32[]{:S(2)}, u32[]{:S(2)}) collective-permute-start(bf16[96,256]{1,0:T(8,128)(2,1)S(1)} %get-tuple-element.61.refs_1_), channel_id=1, source_target_pairs={{0,4},{1,5},{2,6},{3,7},{4,0},{5,1},{6,2},{7,3},{8,12},{9,13},{10,... | collective-permute-start | bytes 147464 | tf_op jit(solution)/shard_map/ppermute | solution.py:399
  22.6 6.2 %collective-permute-start.4 = (bf16[256,128]{1,0:T(8,128)(2,1)S(1)}, bf16[256,128]{1,0:T(8,128)(2,1)S(1)}, u32[]{:S(2)}, u32[]{:S(2)}) collective-permute-start(bf16[256,128]{1,0:T(8,128)(2,1)S(1)} %get-tuple-element.40.own_key_ref), channel_id=1, source_target_pairs={{0,1},{1,0},{2,3},{3,2},{4,5},{5,4},{6,7},{7,6},{8,9},{9,8},{10,11... | collective-permute-start | bytes 196616 | tf_op jit(solution)/shard_map/ppermute | solution.py:399
  25.8 3.0 %copy-start.1 = (bf16[1024,128]{1,0:T(8,128)(2,1)S(1)}, bf16[1024,128]{1,0:T(8,128)(2,1)}, u32[]{:S(2)}) copy-start(bf16[1024,128]{1,0:T(8,128)(2,1)} %query_ref.1) | copy-start | bytes 786436
  25.8 6.1 %collective-permute-start.10 = (bf16[96,256]{1,0:T(8,128)(2,1)S(1)}, bf16[96,256]{1,0:T(8,128)(2,1)S(1)}, u32[]{:S(2)}, u32[]{:S(2)}) collective-permute-start(bf16[96,256]{1,0:T(8,128)(2,1)S(1)} %get-tuple-element.62.first_a), channel_id=1, source_target_pairs={{0,8},{1,9},{2,10},{3,11},{4,12},{5,13},{6,14},{7,15},{8,0},{9,1},... | collective-permute-start | bytes 147464 | tf_op jit(solution)/shard_map/ppermute | solution.py:399
  27.6 1.2 %copy-start.2 = (s32[16]{0:T(128)S(1)}, s32[16]{0:T(128)}, u32[]{:S(2)}) copy-start(s32[16]{0:T(128)} %len_ref.1) | copy-start | bytes 196
  27.6 5.0 %collective-permute-start.11 = (bf16[96,256]{1,0:T(8,128)(2,1)S(1)}, bf16[96,256]{1,0:T(8,128)(2,1)S(1)}, u32[]{:S(2)}, u32[]{:S(2)}) collective-permute-start(bf16[96,256]{1,0:T(8,128)(2,1)S(1)} %get-tuple-element.63.second_a), channel_id=1, source_target_pairs={{0,8},{1,9},{2,10},{3,11},{4,12},{5,13},{6,14},{7,15},{8,0},{9,1},... | collective-permute-start | bytes 147464 | tf_op jit(solution)/shard_map/ppermute | solution.py:399
  32.6 5.2 %collective-permute-start.12 = (bf16[96,256]{1,0:T(8,128)(2,1)S(1)}, bf16[96,256]{1,0:T(8,128)(2,1)S(1)}, u32[]{:S(2)}, u32[]{:S(2)}) collective-permute-start(bf16[96,256]{1,0:T(8,128)(2,1)S(1)} %get-tuple-element.64.own_first), channel_id=1, source_target_pairs={{0,2},{1,3},{2,0},{3,1},{4,6},{5,7},{6,4},{7,5},{8,10},{9,11},{10,... | collective-permute-start | bytes 147464 | tf_op jit(solution)/shard_map/ppermute | solution.py:399
  34.5 4.1 %collective-permute-start.13 = (bf16[96,256]{1,0:T(8,128)(2,1)S(1)}, bf16[96,256]{1,0:T(8,128)(2,1)S(1)}, u32[]{:S(2)}, u32[]{:S(2)}) collective-permute-start(bf16[96,256]{1,0:T(8,128)(2,1)S(1)} %get-tuple-element.65.own_second), channel_id=1, source_target_pairs={{0,2},{1,3},{2,0},{3,1},{4,6},{5,7},{6,4},{7,5},{8,10},{9,11},{10,... | collective-permute-start | bytes 147464 | tf_op jit(solution)/shard_map/ppermute | solution.py:399
  38.7 1.5 %copy-start = (f32[1,512]{1,0:T(1,128)S(1)}, f32[1,512]{1,0:T(1,128)}, u32[]{:S(2)}) copy-start(f32[1,512]{1,0:T(1,128)} %get-tuple-element.46.weight_ref) | copy-start | bytes 6148
  38.7 1.5 %collective-permute-start.14 = (bf16[384,256]{1,0:T(8,128)(2,1)S(1)}, bf16[384,256]{1,0:T(8,128)(2,1)S(1)}, u32[]{:S(2)}, u32[]{:S(2)}) collective-permute-start(bf16[384,256]{1,0:T(8,128)(2,1)S(1)} %shard_map.89.own_ref), channel_id=1, source_target_pairs={{0,1},{1,0},{2,3},{3,2},{4,5},{5,4},{6,7},{7,6},{8,9},{9,8},{10,11... | collective-permute-start | bytes 589832 | tf_op jit(solution)/shard_map/ppermute | solution.py:399

commit v5 on v4

--- a/solution.py
+++ b/solution.py
@@ -168,71 +168,63 @@
     put_stats(keep_head_ref, stat_ref[...])
 
 
-def join_kernel(first_ref, second_ref, out_ref, scale_out):
+def joined_stats(first_ref, second_ref, scale_first_out, scale_second_out):
     first, second = get_stats(first_ref), get_stats(second_ref)
     joint = jnp.maximum(first[:CHUNKS], second[:CHUNKS])
     scale_first = jnp.exp2((first[:CHUNKS] - joint) * EXP2_SCALE)
     scale_second = jnp.exp2((second[:CHUNKS] - joint) * EXP2_SCALE)
+    scale_first_out[...] = scale_first
+    scale_second_out[...] = scale_second
     mass = first[CHUNKS:] * scale_first + second[CHUNKS:] * scale_second
-    put_stats(out_ref, jnp.concatenate([joint, mass], axis=0))
+    return jnp.concatenate([joint, mass], axis=0)
+
+
+def join_kernel(first_ref, second_ref, *refs):
+    out_ref, scale_first_out, scale_second_out = refs[-3:]
+    put_stats(out_ref, joined_stats(first_ref, second_ref, scale_first_out, scale_second_out))
     out_ref[:KEY_ROWS, :] = first_ref[:KEY_ROWS, :] + second_ref[:KEY_ROWS, :]
-    scale_out[...] = scale_first
-
-
-def last_join_kernel(first_ref, second_ref, key_out, stat_out, scale_out):
-    first, second = get_stats(first_ref), get_stats(second_ref)
-    joint = jnp.maximum(first[:CHUNKS], second[:CHUNKS])
-    scale_first = jnp.exp2((first[:CHUNKS] - joint) * EXP2_SCALE)
-    scale_second = jnp.exp2((second[:CHUNKS] - joint) * EXP2_SCALE)
-    stat_out[:CHUNKS, :] = joint
-    stat_out[CHUNKS:, :] = first[CHUNKS:] * scale_first + second[CHUNKS:] * scale_second
+
+
+def last_join_kernel(first_ref, second_ref, after_ref, key_out, stat_out, scale_first_out, scale_second_out):
+    stat_out[...] = joined_stats(first_ref, second_ref, scale_first_out, scale_second_out)
     for c in range(2):
         columns = slice(c * DH, (c + 1) * DH)
         rows = slice(c * KEY_ROWS, (c + 1) * KEY_ROWS)
         key_out[rows, :] = first_ref[:KEY_ROWS, columns] + second_ref[:KEY_ROWS, columns]
-    scale_out[...] = scale_first
-
-
-def core_sum_kernel(scale_ref, send_in, keep_in, send_out, keep_out):
-    me, core, bit = bits()
-    for half, source, out in ((1 - core, send_in, send_out), (core, keep_in, keep_out)):
-        for c in range(2):
-            columns = pl.ds(c * CHUNK, CHUNK)
-            prior, sums = get_pair(source, columns)
-            put_pair(out, columns, prior, sums * scale_ref[pl.ds(half * 2 + c, 1), :])
-
-
-def halve_sum_kernel(scale_ref, sum_a, sum_b, first_out, second_out, keep_out):
+
+
+def halve_sum_kernel(scale_a, scale_b, sum_a, sum_b, first_out, second_out, keep_out):
     me, core, bit = bits()
 
     def half_of(half):
         columns = place(half, CHUNK)
+        row = pl.ds(core * 2 + half, 1)
         prior_a, sums_a = get_pair(sum_a, columns)
         prior_b, sums_b = get_pair(sum_b, columns)
-        return prior_a + prior_b, (sums_a + sums_b) * scale_ref[pl.ds(core * 2 + half, 1), :]
+        return prior_a + prior_b, sums_a * scale_a[row, :] + sums_b * scale_b[row, :]
 
     put_pieces(first_out, second_out, *half_of(1 - bit))
     put_pair(keep_out, EVERYTHING, *half_of(bit))
 
 
-def own_sums(refs):
-    return get_pair(refs[0], EVERYTHING) if len(refs) == 1 else get_pieces(*refs)
-
-
-def join_sum_kernel(scale_ref, *refs):
+def joined_sums(scale_a, scale_b, own, got):
     me, core, bit = bits()
-    prior_a, sums_a = own_sums(refs[:-4])
-    prior_b, sums_b = get_pieces(*refs[-4:-2])
-    factor = scale_ref[pl.ds(core * 2 + bit, 1), :]
-    put_pieces(*refs[-2:], prior_a + prior_b, (sums_a + sums_b) * factor)
-
-
-def outputs_kernel(stat_ref, first_a, second_a, first_b, second_b, after_ref, first_out, second_out):
+    row = pl.ds(core * 2 + bit, 1)
+    prior_a, sums_a = get_pair(own[0], EVERYTHING) if len(own) == 1 else get_pieces(*own)
+    prior_b, sums_b = get_pieces(*got)
+    return prior_a + prior_b, sums_a * scale_a[row, :] + sums_b * scale_b[row, :]
+
+
+def join_sum_kernel(scale_a, scale_b, *refs):
+    put_pieces(*refs[-2:], *joined_sums(scale_a, scale_b, refs[:-4], refs[-4:-2]))
+
+
+def outputs_kernel(
+    scale_a, scale_b, stat_ref, first_a, second_a, first_b, second_b, after_ref, first_out, second_out
+):
     me, core, bit = bits()
-    prior_a, sums_a = get_pieces(first_a, second_a)
-    prior_b, sums_b = get_pieces(first_b, second_b)
-    row_mass = stat_ref[pl.ds(CHUNKS + core * 2 + bit, 1), :]
-    put_pieces(first_out, second_out, prior_a + prior_b, (sums_a + sums_b) / row_mass)
+    prior, sums = joined_sums(scale_a, scale_b, (first_a, second_a), (first_b, second_b))
+    put_pieces(first_out, second_out, prior, sums / stat_ref[pl.ds(CHUNKS + core * 2 + bit, 1), :])
 
 
 def gram3(high, low):
@@ -429,44 +421,43 @@
     def both_exchanged(arrays, mask):
         return tuple(exchanged(array, mask) for array in arrays)
 
-    head, scale = call(join_kernel, (head_shape, scale_shape), (head, exchanged(send_head, 1)))
+    def joined(*arrays):
+        head, *scales = call(join_kernel, (head_shape, scale_shape, scale_shape), arrays)
+        return head, tuple(scales)
+
+    got = exchanged(send, 1)
+    head, scales = joined(head, exchanged(send_head, 1))
     got_head = exchanged(head, 2)
-    send, keep = call(core_sum_kernel, (half_sum, half_sum), (scale, send, keep), flops=SUM_FLOPS)
-    got = exchanged(send, 1)
-    masks = [4]
-    while 2 * masks[-1] < wide_count:
-        masks.append(2 * masks[-1])
-    head, scale = call(join_kernel, (head_shape, scale_shape), (head, got_head))
-    got_head = exchanged(head, masks[0])
     first, second, keep = call(
         halve_sum_kernel,
         pieces + (shape(PAIR_ROWS, CHUNK, bf16),),
-        (scale, keep, got),
+        scales + (keep, got),
         flops=SUM_FLOPS,
     )
     sums, got = (keep,), both_exchanged((first, second), 2)
-    for number, mask in enumerate(masks):
-        if number + 1 < len(masks):
-            head, scale = call(join_kernel, (head_shape, scale_shape), (head, got_head))
-            got_head = exchanged(head, masks[number + 1])
-        else:
-            keys, stats, scale = call(
-                last_join_kernel,
-                (shape(HALF_M, DH, bf16), shape(2 * CHUNKS, CHUNK, f32), scale_shape),
-                (head, got_head),
-            )
-            got_keys = exchanged(keys, 1)
-        sums = call(join_sum_kernel, pieces, (scale,) + sums + got, flops=SUM_FLOPS)
+    mask = 4
+    while mask < wide_count:
+        head, scales = joined(head, got_head, first)
+        got_head = exchanged(head, mask)
+        sums = call(join_sum_kernel, pieces, scales + sums + got, flops=SUM_FLOPS)
+        first = sums[0]
         got = both_exchanged(sums, mask)
+        mask *= 2
+    keys, stats, *scales = call(
+        last_join_kernel,
+        (shape(HALF_M, DH, bf16), shape(2 * CHUNKS, CHUNK, f32), scale_shape, scale_shape),
+        (head, got_head, first),
+    )
+    got_keys = exchanged(keys, 1)
     gram, linear, norm, scaled_hi, scaled_lo = call(
         feature_kernel,
         (shape(M, M, f32), shape(M, DH, f32), shape(8, DH, f32)) + (shape(M, NQ, bf16),) * 2,
         (shard_lengths, queries, stats, keys, got_keys),
         scalars=1,
-        flops=4 * 10**9,
+        flops=1000000000,
         scratch=[pltpu.VMEM((M, DH), bf16), pltpu.VMEM((M, NQ), bf16), pltpu.VMEM((M, NQ), bf16)],
     )
-    outputs = call(outputs_kernel, pieces, (stats,) + tuple(sums) + got + (norm,))
+    outputs = call(outputs_kernel, pieces, (*scales, stats, *sums, *got, norm))
     side = both_exchanged(outputs, 2)
     weights, factor, power = call(
         weight_kernel,

time: 50.4 us -> 49.2 us (0.976)
  waiting for transfers between devices: 10.9 us -> 8.66 us
  starting transfers between devices: 17.8 us -> 18.4 us
  local copies, waits for them, and re-layouts: 0.01 us -> 0.56 us
    ppermute x15, waiting for transfers between devices: 10.9 us -> 8.66 us  [exchanged(): lax.ppermute(array, 'wide', [(i, i ^ mask) for i in range(wide_count)])]
    ppermute x15, starting transfers between devices: 17.8 us -> 18.4 us  [exchanged(): lax.ppermute(array, 'wide', [(i, i ^ mask) for i in range(wide_count)])]
    unnamed x6, local copies, waits for them, and re-layouts: 0.01 us -> 0.56 us
    pallas_call x14 -> x13, Pallas kernels: 20.9 us -> 20.8 us  [call(): pl.pallas_call(kernel, out_shape=tuple(outs), in_specs=in_specs or [pl.Bl...]
  transfers between devices with their start and end apart: 15 -> 15, of which waited for: 10 -> 7; matrix products, arithmetic and copies ran while one was open for 0% -> 0% of each run, Pallas kernels for 13% -> 13%
where the time goes in v5:
time: 49.2 us; the launch traced here: 49.1 us
  Pallas kernels  20.8 us (42%)
  starting transfers between devices  18.4 us (37%)
  waiting for transfers between devices  8.66 us (18%)
  between operations  0.73 us (1%)
  local copies, waits for them, and re-layouts  0.56 us (1%)
    pallas_call x13, Pallas kernels, call(): pl.pallas_call(kernel, out_shape=tuple(outs), in_specs=in_specs or [pl.Bl...  20.8 us
    ppermute x15, starting transfers between devices, exchanged(): lax.ppermute(array, 'wide', [(i, i ^ mask) for i in range(wide_count)])  18.4 us
    ppermute x15, waiting for transfers between devices, exchanged(): lax.ppermute(array, 'wide', [(i, i ^ mask) for i in range(wide_count)])  8.66 us
  transfers between devices with their start and end apart: 15, of which 7 were waited for; matrix products, arithmetic and copies ran while one was open for 0% of the time, Pallas kernels for 13%

profile of v5, /device:TPU:0, one launch (start us, length us, event | category | flops | bytes accessed | tf_op | source)
XLA Modules:
  0.0 49.1 jit_solution(8333118365106491391)
XLA Ops:
  0.6 4.2 %shard_map.77 = (bf16[160,256]{1,0:T(8,128)(2,1)S(1)}, bf16[160,256]{1,0:T(8,128)(2,1)S(1)}, bf16[320,512]{1,0:T(8,128)(2,1)S(1)}, bf16[320,512]{1,0:T(8,128)(2,1)S(1)}) custom-call(s32[16]{0:T(128)} %len_ref.1, s32[32]{0:T(128)} %exp_hbm.1, s32[1,512]{1,0:T(1,128)} %bitcast.3, bf16[1024,128]{1,0:T(8,128)(2,1)} %mant_hbm.1, bf16[1024,128]{1,0:T(8,128)(2,1)} %value_hbm.1, ...), custom_call_target="tpu_custom_call" | custom-call | flops 1000000000 | bytes 1024 | tf_op jit(solution)/shard_map/pallas_call | solution.py:371
  4.9 0.5 %collective-permute-start.2 = (bf16[320,512]{1,0:T(8,128)(2,1)S(1)}, bf16[320,512]{1,0:T(8,128)(2,1)S(1)}, u32[]{:S(2)}, u32[]{:S(2)}) collective-permute-start(bf16[320,512]{1,0:T(8,128)(2,1)S(1)} %get-tuple-element.42), channel_id=1, source_target_pairs={{0,1},{1,0},{2,3},{3,2},{4,5},{5,4},{6,7},{7,6},{8,9},{9,8},{10,11... | collective-permute-start | bytes 983048 | tf_op jit(solution)/shard_map/ppermute | solution.py:391
  5.4 0.1 collective-permute-start
  5.5 1.3 %collective-permute-done.second_ref = bf16[160,256]{1,0:T(8,128)(2,1)S(1)} collective-permute-done((bf16[160,256]{1,0:T(8,128)(2,1)S(1)}, bf16[160,256]{1,0:T(8,128)(2,1)S(1)}, u32[]{:S(2)}, u32[]{:S(2)}) %collective-permute-start) | collective-permute-done | bytes 81952 | tf_op jit(solution)/shard_map/ppermute | solution.py:391
  6.8 3.0 %collective-permute-start.1 = (bf16[160,256]{1,0:T(8,128)(2,1)S(1)}, bf16[160,256]{1,0:T(8,128)(2,1)S(1)}, u32[]{:S(2)}, u32[]{:S(2)}) collective-permute-start(bf16[160,256]{1,0:T(8,128)(2,1)S(1)} %get-tuple-element.38.first_ref), channel_id=1, source_target_pairs={{0,2},{1,3},{2,0},{3,1},{4,6},{5,7},{6,4},{7,5},{8,10},{9,11},{10,... | collective-permute-start | bytes 245768 | tf_op jit(solution)/shard_map/ppermute | solution.py:391
  9.8 0.0 collective-permute-done.2.sum_b
  9.8 0.1 shard_map.79
  9.9 0.1 collective-permute-start.5
  10.0 2.0 %collective-permute-start.4 = (bf16[96,256]{1,0:T(8,128)(2,1)S(1)}, bf16[96,256]{1,0:T(8,128)(2,1)S(1)}, u32[]{:S(2)}, u32[]{:S(2)}) collective-permute-start(bf16[96,256]{1,0:T(8,128)(2,1)S(1)} %get-tuple-element.43.refs_0_), channel_id=1, source_target_pairs={{0,2},{1,3},{2,0},{3,1},{4,6},{5,7},{6,4},{7,5},{8,10},{9,11},{10,... | collective-permute-start | bytes 147464 | tf_op jit(solution)/shard_map/ppermute | solution.py:391
  12.0 0.7 %collective-permute-done.1.second_ref = bf16[160,256]{1,0:T(8,128)(2,1)S(1)} collective-permute-done((bf16[160,256]{1,0:T(8,128)(2,1)S(1)}, bf16[160,256]{1,0:T(8,128)(2,1)S(1)}, u32[]{:S(2)}, u32[]{:S(2)}) %collective-permute-start.1) | collective-permute-done | bytes 81952 | tf_op jit(solution)/shard_map/ppermute | solution.py:391
  12.6 2.2 %collective-permute-start.3 = (bf16[160,256]{1,0:T(8,128)(2,1)S(1)}, bf16[160,256]{1,0:T(8,128)(2,1)S(1)}, u32[]{:S(2)}, u32[]{:S(2)}) collective-permute-start(bf16[160,256]{1,0:T(8,128)(2,1)S(1)} %get-tuple-element.44.first_ref), channel_id=1, source_target_pairs={{0,4},{1,5},{2,6},{3,7},{4,0},{5,1},{6,2},{7,3},{8,12},{9,13},{10,... | collective-permute-start | bytes 245768 | tf_op jit(solution)/shard_map/ppermute | solution.py:391
  14.8 0.0 collective-permute-done.5.refs_2_
  14.8 0.0 collective-permute-done.4.refs_1_
  14.8 1.7 %collective-permute-start.8 = (bf16[96,256]{1,0:T(8,128)(2,1)S(1)}, bf16[96,256]{1,0:T(8,128)(2,1)S(1)}, u32[]{:S(2)}, u32[]{:S(2)}) collective-permute-start(bf16[96,256]{1,0:T(8,128)(2,1)S(1)} %get-tuple-element.53.refs_1_), channel_id=1, source_target_pairs={{0,4},{1,5},{2,6},{3,7},{4,0},{5,1},{6,2},{7,3},{8,12},{9,13},{10,... | collective-permute-start | bytes 147464 | tf_op jit(solution)/shard_map/ppermute | solution.py:391
  16.5 0.4 collective-permute-start.7
  16.9 0.8 %collective-permute-done.3.second_ref = bf16[160,256]{1,0:T(8,128)(2,1)S(1)} collective-permute-done((bf16[160,256]{1,0:T(8,128)(2,1)S(1)}, bf16[160,256]{1,0:T(8,128)(2,1)S(1)}, u32[]{:S(2)}, u32[]{:S(2)}) %collective-permute-start.3) | collective-permute-done | bytes 81952 | tf_op jit(solution)/shard_map/ppermute | solution.py:391
  17.8 3.1 %collective-permute-start.6 = (bf16[160,256]{1,0:T(8,128)(2,1)S(1)}, bf16[160,256]{1,0:T(8,128)(2,1)S(1)}, u32[]{:S(2)}, u32[]{:S(2)}) collective-permute-start(bf16[160,256]{1,0:T(8,128)(2,1)S(1)} %get-tuple-element.50.first_ref), channel_id=1, source_target_pairs={{0,8},{1,9},{2,10},{3,11},{4,12},{5,13},{6,14},{7,15},{8,0},{9,1},... | collective-permute-start | bytes 245768 | tf_op jit(solution)/shard_map/ppermute | solution.py:391
  20.9 0.0 collective-permute-done.8.refs_3_
  20.9 0.0 collective-permute-done.7.refs_2_
  20.9 0.0 copy-start.1
  20.9 2.4 %collective-permute-done.6.second_ref = bf16[160,256]{1,0:T(8,128)(2,1)S(1)} collective-permute-done((bf16[160,256]{1,0:T(8,128)(2,1)S(1)}, bf16[160,256]{1,0:T(8,128)(2,1)S(1)}, u32[]{:S(2)}, u32[]{:S(2)}) %collective-permute-start.6) | collective-permute-done | bytes 81952 | tf_op jit(solution)/shard_map/ppermute | solution.py:391
  23.3 0.1 collective-permute-start.9
  23.4 3.0 %collective-permute-start.10 = (bf16[96,256]{1,0:T(8,128)(2,1)S(1)}, bf16[96,256]{1,0:T(8,128)(2,1)S(1)}, u32[]{:S(2)}, u32[]{:S(2)}) collective-permute-start(bf16[96,256]{1,0:T(8,128)(2,1)S(1)} %get-tuple-element.54.after_ref.first_a), channel_id=1, source_target_pairs={{0,8},{1,9},{2,10},{3,11},{4,12},{5,13},{6,14},{7,15},{8,0},{9,1},... | collective-permute-start | bytes 147464 | tf_op jit(solution)/shard_map/ppermute | solution.py:391
  26.4 0.0 copy-start.2
  26.4 0.1 collective-permute-start.11
  26.5 0.0 collective-permute-done.9.other_key_ref
  26.5 0.0 copy-done.1
  26.5 0.5 %copy-done.2 = s32[16]{0:T(128)S(1)} copy-done((s32[16]{0:T(128)S(1)}, s32[16]{0:T(128)}, u32[]{:S(2)}) %copy-start.2) | copy-done | bytes 88
  27.1 3.1 %shard_map.85 = (f32[512,512]{1,0:T(8,128)S(1)}, f32[512,128]{1,0:T(8,128)S(1)}, f32[8,128]{1,0:T(8,128)S(1)}, bf16[512,1024]{1,0:T(8,128)(2,1)S(1)}, bf16[512,1024]{1,0:T(8,128)(2,1)S(1)}) custom-call(s32[16]{0:T(128)S(1)} %copy-done.2, bf16[1024,128]{1,0:T(8,128)(2,1)S(1)} %copy-done.1, f32[8,256]{1,0:T(8,128)S(1)} %get-tuple-element.55.stat_ref, ...), custom_call_target="tpu_custom_call" | custom-call | flops 1000000000 | bytes 1024 | tf_op jit(solution)/shard_map/pallas_call | solution.py:371
  30.2 1.4 %collective-permute-done.11.second_b = bf16[96,256]{1,0:T(8,128)(2,1)S(1)} collective-permute-done((bf16[96,256]{1,0:T(8,128)(2,1)S(1)}, bf16[96,256]{1,0:T(8,128)(2,1)S(1)}, u32[]{:S(2)}, u32[]{:S(2)}) %collective-permute-start.11) | collective-permute-done | bytes 49184 | tf_op jit(solution)/shard_map/ppermute | solution.py:391
  31.5 0.0 collective-permute-done.10.first_b
  31.6 1.8 %collective-permute-start.12 = (bf16[96,256]{1,0:T(8,128)(2,1)S(1)}, bf16[96,256]{1,0:T(8,128)(2,1)S(1)}, u32[]{:S(2)}, u32[]{:S(2)}) collective-permute-start(bf16[96,256]{1,0:T(8,128)(2,1)S(1)} %get-tuple-element.68.own_first), channel_id=1, source_target_pairs={{0,2},{1,3},{2,0},{3,1},{4,6},{5,7},{6,4},{7,5},{8,10},{9,11},{10,... | collective-permute-start | bytes 147464 | tf_op jit(solution)/shard_map/ppermute | solution.py:391
  33.4 0.3 collective-permute-start.13
  33.7 3.0 %shard_map.86 = (f32[1,512]{1,0:T(1,128)}, f32[8,128]{1,0:T(8,128)S(1)}, f32[512,512]{1,0:T(8,128)S(1)}) custom-call(f32[512,512]{1,0:T(8,128)S(1)} %get-tuple-element.57.gram_ref, f32[512,128]{1,0:T(8,128)S(1)} %get-tuple-element.58.linear_ref, f32[8,128]{1,0:T(8,128)S(1)} %get-tuple-element.59.norm_ref.after_ref, ...), custom_call_target="tpu_custom_call" | custom-call | flops 5000000000 | bytes 1024 | tf_op jit(solution)/shard_map/pallas_call | solution.py:371
  36.7 0.0 collective-permute-done.12.side_first
  36.7 0.7 %collective-permute-done.13.side_second = bf16[96,256]{1,0:T(8,128)(2,1)S(1)} collective-permute-done((bf16[96,256]{1,0:T(8,128)(2,1)S(1)}, bf16[96,256]{1,0:T(8,128)(2,1)S(1)}, u32[]{:S(2)}, u32[]{:S(2)}) %collective-permute-start.13) | collective-permute-done | bytes 49184 | tf_op jit(solution)/shard_map/ppermute | solution.py:391
  37.5 0.0 copy-start
  37.5 0.1 collective-permute-start.14
  37.6 1.4 %collective-permute-done.14.half_ref = bf16[384,256]{1,0:T(8,128)(2,1)S(1)} collective-permute-done((bf16[384,256]{1,0:T(8,128)(2,1)S(1)}, bf16[384,256]{1,0:T(8,128)(2,1)S(1)}, u32[]{:S(2)}, u32[]{:S(2)}) %collective-permute-start.14) | collective-permute-done | bytes 196640 | tf_op jit(solution)/shard_map/ppermute | solution.py:391
  39.0 0.0 copy-done
  39.0 10.1 %shard_map.89 = f32[512,128]{1,0:T(8,128)} custom-call(f32[512,512]{1,0:T(8,128)S(1)} %get-tuple-element.63.power_in, f32[1,512]{1,0:T(1,128)S(1)} %copy-done, f32[8,128]{1,0:T(8,128)S(1)} %get-tuple-element.64.after_ref.factor_ref, bf16[512,1024]{1,0:T(8,128)(2,1)S(1)} %get-tuple-element.60.scaled_hi, bf16[512,1024]{1,0:T(8,128)(2,1)S(1)} %get-tuple-element.61.scaled_lo, ...), custom_call_target="tpu_custom_call" | custom-call | tf_op jit(solution)/shard_map/pallas_call | solution.py:371
  (8 shorter events, 0.2 us)
Async XLA Ops:
  4.9 4.9 %collective-permute-start.2 = (bf16[320,512]{1,0:T(8,128)(2,1)S(1)}, bf16[320,512]{1,0:T(8,128)(2,1)S(1)}, u32[]{:S(2)}, u32[]{:S(2)}) collective-permute-start(bf16[320,512]{1,0:T(8,128)(2,1)S(1)} %get-tuple-element.42), channel_id=1, source_target_pairs={{0,1},{1,0},{2,3},{3,2},{4,5},{5,4},{6,7},{7,6},{8,9},{9,8},{10,11... | collective-permute-start | bytes 983048 | tf_op jit(solution)/shard_map/ppermute | solution.py:391
  5.4 1.4 %collective-permute-start = (bf16[160,256]{1,0:T(8,128)(2,1)S(1)}, bf16[160,256]{1,0:T(8,128)(2,1)S(1)}, u32[]{:S(2)}, u32[]{:S(2)}) collective-permute-start(bf16[160,256]{1,0:T(8,128)(2,1)S(1)} %get-tuple-element.37), channel_id=1, source_target_pairs={{0,1},{1,0},{2,3},{3,2},{4,5},{5,4},{6,7},{7,6},{8,9},{9,8},{10,11... | collective-permute-start | bytes 245768 | tf_op jit(solution)/shard_map/ppermute | solution.py:391
  6.8 5.8 %collective-permute-start.1 = (bf16[160,256]{1,0:T(8,128)(2,1)S(1)}, bf16[160,256]{1,0:T(8,128)(2,1)S(1)}, u32[]{:S(2)}, u32[]{:S(2)}) collective-permute-start(bf16[160,256]{1,0:T(8,128)(2,1)S(1)} %get-tuple-element.38.first_ref), channel_id=1, source_target_pairs={{0,2},{1,3},{2,0},{3,1},{4,6},{5,7},{6,4},{7,5},{8,10},{9,11},{10,... | collective-permute-start | bytes 245768 | tf_op jit(solution)/shard_map/ppermute | solution.py:391
  9.9 4.9 %collective-permute-start.5 = (bf16[96,256]{1,0:T(8,128)(2,1)S(1)}, bf16[96,256]{1,0:T(8,128)(2,1)S(1)}, u32[]{:S(2)}, u32[]{:S(2)}) collective-permute-start(bf16[96,256]{1,0:T(8,128)(2,1)S(1)} %get-tuple-element.48), channel_id=1, source_target_pairs={{0,2},{1,3},{2,0},{3,1},{4,6},{5,7},{6,4},{7,5},{8,10},{9,11},{10,... | collective-permute-start | bytes 147464 | tf_op jit(solution)/shard_map/ppermute | solution.py:391
  10.0 4.8 %collective-permute-start.4 = (bf16[96,256]{1,0:T(8,128)(2,1)S(1)}, bf16[96,256]{1,0:T(8,128)(2,1)S(1)}, u32[]{:S(2)}, u32[]{:S(2)}) collective-permute-start(bf16[96,256]{1,0:T(8,128)(2,1)S(1)} %get-tuple-element.43.refs_0_), channel_id=1, source_target_pairs={{0,2},{1,3},{2,0},{3,1},{4,6},{5,7},{6,4},{7,5},{8,10},{9,11},{10,... | collective-permute-start | bytes 147464 | tf_op jit(solution)/shard_map/ppermute | solution.py:391
  12.6 5.1 %collective-permute-start.3 = (bf16[160,256]{1,0:T(8,128)(2,1)S(1)}, bf16[160,256]{1,0:T(8,128)(2,1)S(1)}, u32[]{:S(2)}, u32[]{:S(2)}) collective-permute-start(bf16[160,256]{1,0:T(8,128)(2,1)S(1)} %get-tuple-element.44.first_ref), channel_id=1, source_target_pairs={{0,4},{1,5},{2,6},{3,7},{4,0},{5,1},{6,2},{7,3},{8,12},{9,13},{10,... | collective-permute-start | bytes 245768 | tf_op jit(solution)/shard_map/ppermute | solution.py:391
  14.8 6.0 %collective-permute-start.8 = (bf16[96,256]{1,0:T(8,128)(2,1)S(1)}, bf16[96,256]{1,0:T(8,128)(2,1)S(1)}, u32[]{:S(2)}, u32[]{:S(2)}) collective-permute-start(bf16[96,256]{1,0:T(8,128)(2,1)S(1)} %get-tuple-element.53.refs_1_), channel_id=1, source_target_pairs={{0,4},{1,5},{2,6},{3,7},{4,0},{5,1},{6,2},{7,3},{8,12},{9,13},{10,... | collective-permute-start | bytes 147464 | tf_op jit(solution)/shard_map/ppermute | solution.py:391
  16.5 4.4 %collective-permute-start.7 = (bf16[96,256]{1,0:T(8,128)(2,1)S(1)}, bf16[96,256]{1,0:T(8,128)(2,1)S(1)}, u32[]{:S(2)}, u32[]{:S(2)}) collective-permute-start(bf16[96,256]{1,0:T(8,128)(2,1)S(1)} %get-tuple-element.49.refs_0_), channel_id=1, source_target_pairs={{0,4},{1,5},{2,6},{3,7},{4,0},{5,1},{6,2},{7,3},{8,12},{9,13},{10,... | collective-permute-start | bytes 147464 | tf_op jit(solution)/shard_map/ppermute | solution.py:391
  17.8 5.5 %collective-permute-start.6 = (bf16[160,256]{1,0:T(8,128)(2,1)S(1)}, bf16[160,256]{1,0:T(8,128)(2,1)S(1)}, u32[]{:S(2)}, u32[]{:S(2)}) collective-permute-start(bf16[160,256]{1,0:T(8,128)(2,1)S(1)} %get-tuple-element.50.first_ref), channel_id=1, source_target_pairs={{0,8},{1,9},{2,10},{3,11},{4,12},{5,13},{6,14},{7,15},{8,0},{9,1},... | collective-permute-start | bytes 245768 | tf_op jit(solution)/shard_map/ppermute | solution.py:391
  20.9 5.7 %copy-start.1 = (bf16[1024,128]{1,0:T(8,128)(2,1)S(1)}, bf16[1024,128]{1,0:T(8,128)(2,1)}, u32[]{:S(2)}) copy-start(bf16[1024,128]{1,0:T(8,128)(2,1)} %query_ref.1) | copy-start | bytes 786436
  23.3 3.2 %collective-permute-start.9 = (bf16[256,128]{1,0:T(8,128)(2,1)S(1)}, bf16[256,128]{1,0:T(8,128)(2,1)S(1)}, u32[]{:S(2)}, u32[]{:S(2)}) collective-permute-start(bf16[256,128]{1,0:T(8,128)(2,1)S(1)} %get-tuple-element.56.own_key_ref), channel_id=1, source_target_pairs={{0,1},{1,0},{2,3},{3,2},{4,5},{5,4},{6,7},{7,6},{8,9},{9,8},{10,11... | collective-permute-start | bytes 196616 | tf_op jit(solution)/shard_map/ppermute | solution.py:391
  23.4 8.2 %collective-permute-start.10 = (bf16[96,256]{1,0:T(8,128)(2,1)S(1)}, bf16[96,256]{1,0:T(8,128)(2,1)S(1)}, u32[]{:S(2)}, u32[]{:S(2)}) collective-permute-start(bf16[96,256]{1,0:T(8,128)(2,1)S(1)} %get-tuple-element.54.after_ref.first_a), channel_id=1, source_target_pairs={{0,8},{1,9},{2,10},{3,11},{4,12},{5,13},{6,14},{7,15},{8,0},{9,1},... | collective-permute-start | bytes 147464 | tf_op jit(solution)/shard_map/ppermute | solution.py:391
  26.4 0.7 %copy-start.2 = (s32[16]{0:T(128)S(1)}, s32[16]{0:T(128)}, u32[]{:S(2)}) copy-start(s32[16]{0:T(128)} %len_ref.1) | copy-start | bytes 196
  26.4 5.1 %collective-permute-start.11 = (bf16[96,256]{1,0:T(8,128)(2,1)S(1)}, bf16[96,256]{1,0:T(8,128)(2,1)S(1)}, u32[]{:S(2)}, u32[]{:S(2)}) collective-permute-start(bf16[96,256]{1,0:T(8,128)(2,1)S(1)} %get-tuple-element.67.second_a), channel_id=1, source_target_pairs={{0,8},{1,9},{2,10},{3,11},{4,12},{5,13},{6,14},{7,15},{8,0},{9,1},... | collective-permute-start | bytes 147464 | tf_op jit(solution)/shard_map/ppermute | solution.py:391
  31.6 5.1 %collective-permute-start.12 = (bf16[96,256]{1,0:T(8,128)(2,1)S(1)}, bf16[96,256]{1,0:T(8,128)(2,1)S(1)}, u32[]{:S(2)}, u32[]{:S(2)}) collective-permute-start(bf16[96,256]{1,0:T(8,128)(2,1)S(1)} %get-tuple-element.68.own_first), channel_id=1, source_target_pairs={{0,2},{1,3},{2,0},{3,1},{4,6},{5,7},{6,4},{7,5},{8,10},{9,11},{10,... | collective-permute-start | bytes 147464 | tf_op jit(solution)/shard_map/ppermute | solution.py:391
  33.4 4.1 %collective-permute-start.13 = (bf16[96,256]{1,0:T(8,128)(2,1)S(1)}, bf16[96,256]{1,0:T(8,128)(2,1)S(1)}, u32[]{:S(2)}, u32[]{:S(2)}) collective-permute-start(bf16[96,256]{1,0:T(8,128)(2,1)S(1)} %get-tuple-element.69.own_second), channel_id=1, source_target_pairs={{0,2},{1,3},{2,0},{3,1},{4,6},{5,7},{6,4},{7,5},{8,10},{9,11},{10,... | collective-permute-start | bytes 147464 | tf_op jit(solution)/shard_map/ppermute | solution.py:391
  37.5 1.5 %copy-start = (f32[1,512]{1,0:T(1,128)S(1)}, f32[1,512]{1,0:T(1,128)}, u32[]{:S(2)}) copy-start(f32[1,512]{1,0:T(1,128)} %get-tuple-element.62.weight_ref) | copy-start | bytes 6148
  37.5 1.5 %collective-permute-start.14 = (bf16[384,256]{1,0:T(8,128)(2,1)S(1)}, bf16[384,256]{1,0:T(8,128)(2,1)S(1)}, u32[]{:S(2)}, u32[]{:S(2)}) collective-permute-start(bf16[384,256]{1,0:T(8,128)(2,1)S(1)} %shard_map.88.own_ref), channel_id=1, source_target_pairs={{0,1},{1,0},{2,3},{3,2},{4,5},{5,4},{6,7},{7,6},{8,9},{9,8},{10,11... | collective-permute-start | bytes 589832 | tf_op jit(solution)/shard_map/ppermute | solution.py:391

commit v6 on v5

--- a/solution.py
+++ b/solution.py
@@ -12,6 +12,8 @@
 SELECT_FROM = 256
 NNLS_STEPS = 8
 NS_ITERS = 9
+EARLY_STEPS = 4
+LATE_STEPS = 2
 SUM_FLOPS = 10**9
 CHUNKS = 4
 CHUNK = NQ // CHUNKS
@@ -111,7 +113,7 @@
 def attention_kernel(
     len_hbm, exp_hbm, index_hbm, mant_hbm, value_hbm, query_hbm,
     send_head_ref, keep_head_ref, send_ref, keep_ref,
-    stat_ref, len_ref, exp_ref, index_ref, mant_ref, value_ref, query_ref, key_ref, sems,
+    stat_ref, len_ref, exp_ref, index_ref, mant_ref, value_ref, query_ref, key_ref, attn_ref, sems,
 ):
     copies = [
         pltpu.make_async_copy(source, target, sems.at[i])
@@ -160,10 +162,10 @@
             attn = jnp.exp2((scores - row_max) * EXP2_SCALE)
             stat_ref[pl.ds(number, 1), :] = row_max
             stat_ref[pl.ds(CHUNKS + number, 1), :] = jnp.sum(attn, axis=0, keepdims=True)
-            sums = mm(value_ref[...], attn.astype(bf16), TN)
-            high, low = split(sums)
-            out[PRIOR:SUM_ROWS, c * CHUNK : (c + 1) * CHUNK] = high
-            out[SUM_ROWS:, c * CHUNK : (c + 1) * CHUNK] = low
+            attn_ref[:, c * CHUNK : (c + 1) * CHUNK] = attn.astype(bf16)
+        high, low = split(mm(value_ref[...], attn_ref[...], TN))
+        out[PRIOR:SUM_ROWS, :] = high
+        out[SUM_ROWS:, :] = low
     put_stats(send_head_ref, stat_ref[...])
     put_stats(keep_head_ref, stat_ref[...])
 
@@ -307,8 +309,8 @@
     ridge = ridge_weight * (total_of(jnp.where(diagonal, gram, 0.0)) / M + 1e-6)
     system = gram + jnp.where(diagonal, ridge, 0.0)
     bound = jnp.max(jnp.sum(jnp.abs(system), axis=0, keepdims=True), axis=1, keepdims=True)
-    row = lax.broadcasted_iota(jnp.int32, factor_out.shape, 0)
-    factor_out[...] = jnp.where(row == 0, ridge, bound)
+    number = lax.broadcasted_iota(jnp.int32, factor_out.shape, 0)
+    factor_out[...] = jnp.where(number == 0, ridge, jnp.where(number == 1, bound, row))
     power_out[...] = system * (1.0 / bound)
 
 
@@ -332,16 +334,48 @@
     return product
 
 
+def squared(power, pair):
+    high, low = pair
+    top = 2.0 * power[:HALF_M] - mm3((high[:HALF_M], low[:HALF_M]), pair, NN)
+    corner = mm3((high[HALF_M:], low[HALF_M:]), (high[:, HALF_M:], low[:, HALF_M:]), NN)
+    corner = 2.0 * power[HALF_M:, HALF_M:] - corner
+    return top, jnp.concatenate([top[:, HALF_M:].T, corner], axis=1)
+
+
+def times_power(refit, high, low):
+    rows = refit.shape[0]
+    pair = jnp.concatenate(split(refit), axis=0)
+    by_high = mm(pair, high, NN)
+    return by_high[:rows] + (by_high[rows:] + mm(pair[:rows], low, NN))
+
+
+def power_kernel(power_in, after_ref, high_out, low_out, power_out):
+    power_out[...] = power_in[...]
+
+    def step(number, carry):
+        pair = split(power_out[...])
+        high_out[place(number, M), :], low_out[place(number, M), :] = pair
+        power_out[:HALF_M, :], power_out[HALF_M:, :] = squared(power_out[...], pair)
+        return carry
+
+    lax.fori_loop(0, high_out.shape[0] // M, step, 0)
+
+
 def refit_kernel(
-    power_in, weight_ref, factor_ref, scaled_hi, scaled_lo, own_ref, half_ref,
+    early_hi, early_lo, late_hi, late_lo, power_in, factor_ref, scaled_hi, scaled_lo, own_ref, half_ref,
     value_out, both_ref, prior_ref,
 ):
     me, core, bit = bits()
     product = right_side(own_ref, core, bit, scaled_hi, scaled_lo, prior_ref)
     product = product + right_side(half_ref, 1 - core, bit, scaled_hi, scaled_lo, prior_ref)
-    ridge, bound = factor_ref[0:1, :1], factor_ref[1:2, :1]
+    ridge, bound, weights = factor_ref[0:1, :1], factor_ref[1:2, :1], factor_ref[2:3, :]
+    refit = (weights * product + ridge * prior_ref[...]) * (1.0 / bound)
+    for high, low in ((early_hi, early_lo), (late_hi, late_lo)):
+        for begin in range(0, high.shape[0], M):
+            rows = slice(begin, begin + M)
+            refit = 2.0 * refit - times_power(refit, high[rows, :], low[rows, :])
     both_ref[DH:, :] = power_in[...]
-    both_ref[:DH, :] = (weight_ref[...] * product + ridge * prior_ref[...]) * (1.0 / bound)
+    both_ref[:DH, :] = refit
     above = DH + HALF_M
 
     def newton_step(number, carry):
@@ -354,12 +388,12 @@
         both_ref[:above, :] = top
         return carry
 
-    lax.fori_loop(0, NS_ITERS - 2, newton_step, 0)
+    lax.fori_loop(EARLY_STEPS + LATE_STEPS, NS_ITERS - 2, newton_step, 0)
     power = split(both_ref[DH:, :])
     refit = both_ref[:DH, :]
-    refit = 2.0 * refit - mm3(split(refit), power, NN)
-    once = mm3(split(refit), power, NN)
-    refit = 2.0 * (refit - once) + mm3(split(once), power, NN)
+    refit = 2.0 * refit - times_power(refit, *power)
+    once = times_power(refit, *power)
+    refit = 2.0 * (refit - once) + times_power(once, *power)
     value_out[...] = refit.T
 
 
@@ -367,7 +401,7 @@
     return jax.ShapeDtypeStruct((rows, columns), dtype)
 
 
-def call(kernel, outs, arrays, scalars=0, scratch=(), in_specs=None, flops=None, limit=48):
+def call(kernel, outs, arrays, scalars=0, scratch=(), in_specs=None, flops=None, limit=38):
     return pl.pallas_call(
         kernel,
         out_shape=tuple(outs),
@@ -415,6 +449,7 @@
             pltpu.VMEM((ctx, DH), bf16),
             pltpu.VMEM((NQ, DH), bf16),
             pltpu.VMEM((ctx, DH), bf16),
+            pltpu.VMEM((ctx, 2 * CHUNK), bf16),
             pltpu.SemaphoreType.DMA((6,)),
         ],
     )
@@ -457,28 +492,33 @@
         flops=1000000000,
         scratch=[pltpu.VMEM((M, DH), bf16), pltpu.VMEM((M, NQ), bf16), pltpu.VMEM((M, NQ), bf16)],
     )
-    outputs = call(outputs_kernel, pieces, (*scales, stats, *sums, *got, norm))
-    side = both_exchanged(outputs, 2)
     weights, factor, power = call(
         weight_kernel,
-        (shape(1, M, f32), shape(8, DH, f32), shape(M, M, f32)),
+        (shape(1, M, f32), shape(8, M, f32), shape(M, M, f32)),
         (gram, linear, norm, scaled_hi, scaled_lo),
         flops=5 * 10**9,
         scratch=[pltpu.VMEM((M, M), f32)],
     )
+    outputs = call(outputs_kernel, pieces, (*scales, stats, *sums, *got, factor))
+    side = both_exchanged(outputs, 2)
+
+    def powers(power, after, steps):
+        pairs = (shape(steps * M, M, bf16),) * 2
+        return call(power_kernel, pairs + (shape(M, M, f32),), (power, after), flops=steps * 10**9)
+
+    early_hi, early_lo, power = powers(power, outputs[0], EARLY_STEPS)
     (half,) = call(
         forward_kernel,
         (shape(2 * SUM_ROWS, CHUNK, bf16),),
-        tuple(outputs) + side + (factor,),
-    )
+        tuple(outputs) + side + (power,),
+    )
+    other = exchanged(half, 1)
+    late_hi, late_lo, power = powers(power, half, LATE_STEPS)
     (compact_values,) = call(
         refit_kernel,
         (shape(M, DH, f32),),
-        (power, weights, factor, scaled_hi, scaled_lo, half, exchanged(half, 1)),
-        scratch=[
-            pltpu.VMEM((M + DH, M), f32),
-            pltpu.VMEM((DH, M), f32),
-        ],
+        (early_hi, early_lo, late_hi, late_lo, power, factor, scaled_hi, scaled_lo, half, other),
+        scratch=[pltpu.VMEM((M + DH, M), f32), pltpu.VMEM((DH, M), f32)],
     )
     return weights.reshape(M), compact_values
 

time: 49.2 us -> 45.5 us (0.925)
  waiting for transfers between devices: 8.66 us -> 5.31 us
  local copies, waits for them, and re-layouts: 0.56 us -> 0.01 us
    ppermute x15, waiting for transfers between devices: 8.66 us -> 5.31 us  [exchanged(): lax.ppermute(array, 'wide', [(i, i ^ mask) for i in range(wide_count)])]
    unnamed x6 -> x4, local copies, waits for them, and re-layouts: 0.56 us -> 0.01 us
    pallas_call x13 -> x15, Pallas kernels: 20.8 us -> 20.7 us  [call(): pl.pallas_call(kernel, out_shape=tuple(outs), in_specs=in_specs or [pl.Bl...]
  transfers between devices with their start and end apart: 15 -> 15, of which waited for: 7 -> 5; matrix products, arithmetic and copies ran while one was open for 0% -> 0% of each run, Pallas kernels for 13% -> 26%
where the time goes in v6:
time: 45.5 us; the launch traced here: 45.1 us
  Pallas kernels  20.7 us (45%)
  starting transfers between devices  18.4 us (40%)
  waiting for transfers between devices  5.31 us (12%)
  between operations  0.76 us (2%)
    pallas_call x15, Pallas kernels, call(): pl.pallas_call(kernel, out_shape=tuple(outs), in_specs=in_specs or [pl.Bl...  20.7 us
    ppermute x15, starting transfers between devices, exchanged(): lax.ppermute(array, 'wide', [(i, i ^ mask) for i in range(wide_count)])  18.4 us
    ppermute x15, waiting for transfers between devices, exchanged(): lax.ppermute(array, 'wide', [(i, i ^ mask) for i in range(wide_count)])  5.31 us
  transfers between devices with their start and end apart: 15, of which 5 were waited for; matrix products, arithmetic and copies ran while one was open for 0% of the time, Pallas kernels for 26%

profile of v6, /device:TPU:0, one launch (start us, length us, event | category | flops | bytes accessed | tf_op | source)
XLA Modules:
  0.0 45.1 jit_solution(11376151784687862248)
XLA Ops:
  0.6 3.2 %shard_map.77 = (bf16[160,256]{1,0:T(8,128)(2,1)S(1)}, bf16[160,256]{1,0:T(8,128)(2,1)S(1)}, bf16[320,512]{1,0:T(8,128)(2,1)S(1)}, bf16[320,512]{1,0:T(8,128)(2,1)S(1)}) custom-call(s32[16]{0:T(128)} %len_ref.1, s32[32]{0:T(128)} %exp_hbm.1, s32[1,512]{1,0:T(1,128)} %bitcast.2, bf16[1024,128]{1,0:T(8,128)(2,1)} %mant_hbm.1, bf16[1024,128]{1,0:T(8,128)(2,1)} %value_hbm.1, ...), custom_call_target="tpu_custom_call" | custom-call | flops 1000000000 | bytes 1024 | tf_op jit(solution)/shard_map/pallas_call | solution.py:405
  3.9 0.5 %collective-permute-start.2 = (bf16[320,512]{1,0:T(8,128)(2,1)S(1)}, bf16[320,512]{1,0:T(8,128)(2,1)S(1)}, u32[]{:S(2)}, u32[]{:S(2)}) collective-permute-start(bf16[320,512]{1,0:T(8,128)(2,1)S(1)} %get-tuple-element.48), channel_id=1, source_target_pairs={{0,1},{1,0},{2,3},{3,2},{4,5},{5,4},{6,7},{7,6},{8,9},{9,8},{10,11... | collective-permute-start | bytes 983048 | tf_op jit(solution)/shard_map/ppermute | solution.py:425
  4.4 0.1 collective-permute-start
  4.5 1.3 %collective-permute-done.second_ref = bf16[160,256]{1,0:T(8,128)(2,1)S(1)} collective-permute-done((bf16[160,256]{1,0:T(8,128)(2,1)S(1)}, bf16[160,256]{1,0:T(8,128)(2,1)S(1)}, u32[]{:S(2)}, u32[]{:S(2)}) %collective-permute-start) | collective-permute-done | bytes 81952 | tf_op jit(solution)/shard_map/ppermute | solution.py:425
  5.8 3.0 %collective-permute-start.1 = (bf16[160,256]{1,0:T(8,128)(2,1)S(1)}, bf16[160,256]{1,0:T(8,128)(2,1)S(1)}, u32[]{:S(2)}, u32[]{:S(2)}) collective-permute-start(bf16[160,256]{1,0:T(8,128)(2,1)S(1)} %get-tuple-element.44.first_ref), channel_id=1, source_target_pairs={{0,2},{1,3},{2,0},{3,1},{4,6},{5,7},{6,4},{7,5},{8,10},{9,11},{10,... | collective-permute-start | bytes 245768 | tf_op jit(solution)/shard_map/ppermute | solution.py:425
  8.8 0.0 collective-permute-done.2.sum_b
  8.8 0.1 shard_map.79
  8.9 0.1 collective-permute-start.4
  9.0 2.0 %collective-permute-start.5 = (bf16[96,256]{1,0:T(8,128)(2,1)S(1)}, bf16[96,256]{1,0:T(8,128)(2,1)S(1)}, u32[]{:S(2)}, u32[]{:S(2)}) collective-permute-start(bf16[96,256]{1,0:T(8,128)(2,1)S(1)} %get-tuple-element.54), channel_id=1, source_target_pairs={{0,2},{1,3},{2,0},{3,1},{4,6},{5,7},{6,4},{7,5},{8,10},{9,11},{10,... | collective-permute-start | bytes 147464 | tf_op jit(solution)/shard_map/ppermute | solution.py:425
  11.0 0.7 %collective-permute-done.1.second_ref = bf16[160,256]{1,0:T(8,128)(2,1)S(1)} collective-permute-done((bf16[160,256]{1,0:T(8,128)(2,1)S(1)}, bf16[160,256]{1,0:T(8,128)(2,1)S(1)}, u32[]{:S(2)}, u32[]{:S(2)}) %collective-permute-start.1) | collective-permute-done | bytes 81952 | tf_op jit(solution)/shard_map/ppermute | solution.py:425
  11.6 2.1 %collective-permute-start.3 = (bf16[160,256]{1,0:T(8,128)(2,1)S(1)}, bf16[160,256]{1,0:T(8,128)(2,1)S(1)}, u32[]{:S(2)}, u32[]{:S(2)}) collective-permute-start(bf16[160,256]{1,0:T(8,128)(2,1)S(1)} %get-tuple-element.50.first_ref), channel_id=1, source_target_pairs={{0,4},{1,5},{2,6},{3,7},{4,0},{5,1},{6,2},{7,3},{8,12},{9,13},{10,... | collective-permute-start | bytes 245768 | tf_op jit(solution)/shard_map/ppermute | solution.py:425
  13.8 0.0 collective-permute-done.4.refs_1_
  13.8 0.0 collective-permute-done.5.refs_2_
  13.8 0.0 copy-start
  13.9 0.0 copy-start.1
  13.9 1.7 %collective-permute-start.7 = (bf16[96,256]{1,0:T(8,128)(2,1)S(1)}, bf16[96,256]{1,0:T(8,128)(2,1)S(1)}, u32[]{:S(2)}, u32[]{:S(2)}) collective-permute-start(bf16[96,256]{1,0:T(8,128)(2,1)S(1)} %get-tuple-element.55.refs_0_), channel_id=1, source_target_pairs={{0,4},{1,5},{2,6},{3,7},{4,0},{5,1},{6,2},{7,3},{8,12},{9,13},{10,... | collective-permute-start | bytes 147464 | tf_op jit(solution)/shard_map/ppermute | solution.py:425
  15.5 0.4 collective-permute-start.8
  16.0 0.8 %collective-permute-done.3.second_ref = bf16[160,256]{1,0:T(8,128)(2,1)S(1)} collective-permute-done((bf16[160,256]{1,0:T(8,128)(2,1)S(1)}, bf16[160,256]{1,0:T(8,128)(2,1)S(1)}, u32[]{:S(2)}, u32[]{:S(2)}) %collective-permute-start.3) | collective-permute-done | bytes 81952 | tf_op jit(solution)/shard_map/ppermute | solution.py:425
  16.8 3.1 %collective-permute-start.6 = (bf16[160,256]{1,0:T(8,128)(2,1)S(1)}, bf16[160,256]{1,0:T(8,128)(2,1)S(1)}, u32[]{:S(2)}, u32[]{:S(2)}) collective-permute-start(bf16[160,256]{1,0:T(8,128)(2,1)S(1)} %get-tuple-element.56.first_ref), channel_id=1, source_target_pairs={{0,8},{1,9},{2,10},{3,11},{4,12},{5,13},{6,14},{7,15},{8,0},{9,1},... | collective-permute-start | bytes 245768 | tf_op jit(solution)/shard_map/ppermute | solution.py:425
  19.9 0.0 collective-permute-done.7.refs_2_
  19.9 0.0 collective-permute-done.8.refs_3_
  19.9 2.4 %collective-permute-done.6.second_ref = bf16[160,256]{1,0:T(8,128)(2,1)S(1)} collective-permute-done((bf16[160,256]{1,0:T(8,128)(2,1)S(1)}, bf16[160,256]{1,0:T(8,128)(2,1)S(1)}, u32[]{:S(2)}, u32[]{:S(2)}) %collective-permute-start.6) | collective-permute-done | bytes 81952 | tf_op jit(solution)/shard_map/ppermute | solution.py:425
  22.3 0.1 collective-permute-start.9
  22.4 3.0 %collective-permute-start.10 = (bf16[96,256]{1,0:T(8,128)(2,1)S(1)}, bf16[96,256]{1,0:T(8,128)(2,1)S(1)}, u32[]{:S(2)}, u32[]{:S(2)}) collective-permute-start(bf16[96,256]{1,0:T(8,128)(2,1)S(1)} %get-tuple-element.60.after_ref.first_a), channel_id=1, source_target_pairs={{0,8},{1,9},{2,10},{3,11},{4,12},{5,13},{6,14},{7,15},{8,0},{9,1},... | collective-permute-start | bytes 147464 | tf_op jit(solution)/shard_map/ppermute | solution.py:425
  25.4 0.1 collective-permute-start.11
  25.5 0.0 collective-permute-done.9.other_key_ref
  25.5 0.0 copy-done
  25.5 0.0 copy-done.1
  25.6 3.1 %shard_map.85 = (f32[512,512]{1,0:T(8,128)S(1)}, f32[512,128]{1,0:T(8,128)S(1)}, f32[8,128]{1,0:T(8,128)S(1)}, bf16[512,1024]{1,0:T(8,128)(2,1)S(1)}, bf16[512,1024]{1,0:T(8,128)(2,1)S(1)}) custom-call(s32[16]{0:T(128)S(1)} %copy-done.1, bf16[1024,128]{1,0:T(8,128)(2,1)S(1)} %copy-done, f32[8,256]{1,0:T(8,128)S(1)} %get-tuple-element.61.stat_ref, ...), custom_call_target="tpu_custom_call" | custom-call | flops 1000000000 | bytes 1024 | tf_op jit(solution)/shard_map/pallas_call | solution.py:405
  28.6 2.9 %shard_map.86 = (f32[1,512]{1,0:T(1,128)}, f32[8,512]{1,0:T(8,128)S(1)}, f32[512,512]{1,0:T(8,128)S(1)}) custom-call(f32[512,512]{1,0:T(8,128)S(1)} %get-tuple-element.63.gram_ref, f32[512,128]{1,0:T(8,128)S(1)} %get-tuple-element.64.linear_ref, f32[8,128]{1,0:T(8,128)S(1)} %get-tuple-element.65.norm_ref, bf16[512,1024]{1,0:T(8,128)(2,1)S(1)} %get-tuple-element.66.scaled_hi, ...), custom_call_target="tpu_custom_call" | custom-call | flops 5000000000 | bytes 1024 | tf_op jit(solution)/shard_map/pallas_call | solution.py:405
  31.5 0.0 collective-permute-done.10.first_b
  31.5 0.0 collective-permute-done.11.second_b
  31.5 2.0 %collective-permute-start.12 = (bf16[96,256]{1,0:T(8,128)(2,1)S(1)}, bf16[96,256]{1,0:T(8,128)(2,1)S(1)}, u32[]{:S(2)}, u32[]{:S(2)}) collective-permute-start(bf16[96,256]{1,0:T(8,128)(2,1)S(1)} %get-tuple-element.74.after_ref.own_first), channel_id=1, source_target_pairs={{0,2},{1,3},{2,0},{3,1},{4,6},{5,7},{6,4},{7,5},{8,10},{9,11},{10,... | collective-permute-start | bytes 147464 | tf_op jit(solution)/shard_map/ppermute | solution.py:425
  33.5 0.1 collective-permute-start.13
  33.6 3.8 %shard_map.88 = (bf16[2048,512]{1,0:T(8,128)(2,1)S(1)}, bf16[2048,512]{1,0:T(8,128)(2,1)S(1)}, f32[512,512]{1,0:T(8,128)S(1)}) custom-call(f32[512,512]{1,0:T(8,128)S(1)} %get-tuple-element.69.power_in, bf16[96,256]{1,0:T(8,128)(2,1)S(1)} %get-tuple-element.74.after_ref.own_first), custom_call_target="tpu_custom_call" | custom-call | flops 4000000000 | bytes 1024 | tf_op jit(solution)/shard_map/pallas_call | solution.py:405
  37.4 0.0 collective-permute-done.12.side_first
  37.4 0.2 collective-permute-done.13.side_second
  37.6 0.1 collective-permute-start.14
  37.7 1.8 %shard_map.90 = (bf16[1024,512]{1,0:T(8,128)(2,1)S(1)}, bf16[1024,512]{1,0:T(8,128)(2,1)S(1)}, f32[512,512]{1,0:T(8,128)S(1)}) custom-call(f32[512,512]{1,0:T(8,128)S(1)} %get-tuple-element.77.after_ref.power_in, bf16[384,256]{1,0:T(8,128)(2,1)S(1)} %shard_map.89.after_ref.own_ref), custom_call_target="tpu_custom_call" | custom-call | flops 2000000000 | bytes 1024 | tf_op jit(solution)/shard_map/pallas_call | solution.py:405
  39.5 0.0 collective-permute-done.14.half_ref
  39.5 5.6 %shard_map.91 = f32[512,128]{1,0:T(8,128)} custom-call(bf16[2048,512]{1,0:T(8,128)(2,1)S(1)} %get-tuple-element.75.early_hi, bf16[2048,512]{1,0:T(8,128)(2,1)S(1)} %get-tuple-element.76.early_lo, bf16[1024,512]{1,0:T(8,128)(2,1)S(1)} %get-tuple-element.79.late_hi, bf16[1024,512]{1,0:T(8,128)(2,1)S(1)} %get-tuple-element.80.late_lo, ...), custom_call_target="tpu_custom_call" | custom-call | tf_op jit(solution)/shard_map/pallas_call | solution.py:405
  (8 shorter events, 0.2 us)
Async XLA Ops:
  3.9 4.9 %collective-permute-start.2 = (bf16[320,512]{1,0:T(8,128)(2,1)S(1)}, bf16[320,512]{1,0:T(8,128)(2,1)S(1)}, u32[]{:S(2)}, u32[]{:S(2)}) collective-permute-start(bf16[320,512]{1,0:T(8,128)(2,1)S(1)} %get-tuple-element.48), channel_id=1, source_target_pairs={{0,1},{1,0},{2,3},{3,2},{4,5},{5,4},{6,7},{7,6},{8,9},{9,8},{10,11... | collective-permute-start | bytes 983048 | tf_op jit(solution)/shard_map/ppermute | solution.py:425
  4.4 1.4 %collective-permute-start = (bf16[160,256]{1,0:T(8,128)(2,1)S(1)}, bf16[160,256]{1,0:T(8,128)(2,1)S(1)}, u32[]{:S(2)}, u32[]{:S(2)}) collective-permute-start(bf16[160,256]{1,0:T(8,128)(2,1)S(1)} %get-tuple-element.43), channel_id=1, source_target_pairs={{0,1},{1,0},{2,3},{3,2},{4,5},{5,4},{6,7},{7,6},{8,9},{9,8},{10,11... | collective-permute-start | bytes 245768 | tf_op jit(solution)/shard_map/ppermute | solution.py:425
  5.8 5.8 %collective-permute-start.1 = (bf16[160,256]{1,0:T(8,128)(2,1)S(1)}, bf16[160,256]{1,0:T(8,128)(2,1)S(1)}, u32[]{:S(2)}, u32[]{:S(2)}) collective-permute-start(bf16[160,256]{1,0:T(8,128)(2,1)S(1)} %get-tuple-element.44.first_ref), channel_id=1, source_target_pairs={{0,2},{1,3},{2,0},{3,1},{4,6},{5,7},{6,4},{7,5},{8,10},{9,11},{10,... | collective-permute-start | bytes 245768 | tf_op jit(solution)/shard_map/ppermute | solution.py:425
  8.9 4.9 %collective-permute-start.4 = (bf16[96,256]{1,0:T(8,128)(2,1)S(1)}, bf16[96,256]{1,0:T(8,128)(2,1)S(1)}, u32[]{:S(2)}, u32[]{:S(2)}) collective-permute-start(bf16[96,256]{1,0:T(8,128)(2,1)S(1)} %get-tuple-element.49.refs_0_), channel_id=1, source_target_pairs={{0,2},{1,3},{2,0},{3,1},{4,6},{5,7},{6,4},{7,5},{8,10},{9,11},{10,... | collective-permute-start | bytes 147464 | tf_op jit(solution)/shard_map/ppermute | solution.py:425
  9.0 4.8 %collective-permute-start.5 = (bf16[96,256]{1,0:T(8,128)(2,1)S(1)}, bf16[96,256]{1,0:T(8,128)(2,1)S(1)}, u32[]{:S(2)}, u32[]{:S(2)}) collective-permute-start(bf16[96,256]{1,0:T(8,128)(2,1)S(1)} %get-tuple-element.54), channel_id=1, source_target_pairs={{0,2},{1,3},{2,0},{3,1},{4,6},{5,7},{6,4},{7,5},{8,10},{9,11},{10,... | collective-permute-start | bytes 147464 | tf_op jit(solution)/shard_map/ppermute | solution.py:425
  11.6 5.1 %collective-permute-start.3 = (bf16[160,256]{1,0:T(8,128)(2,1)S(1)}, bf16[160,256]{1,0:T(8,128)(2,1)S(1)}, u32[]{:S(2)}, u32[]{:S(2)}) collective-permute-start(bf16[160,256]{1,0:T(8,128)(2,1)S(1)} %get-tuple-element.50.first_ref), channel_id=1, source_target_pairs={{0,4},{1,5},{2,6},{3,7},{4,0},{5,1},{6,2},{7,3},{8,12},{9,13},{10,... | collective-permute-start | bytes 245768 | tf_op jit(solution)/shard_map/ppermute | solution.py:425
  13.8 11.7 %copy-start = (bf16[1024,128]{1,0:T(8,128)(2,1)S(1)}, bf16[1024,128]{1,0:T(8,128)(2,1)}, u32[]{:S(2)}) copy-start(bf16[1024,128]{1,0:T(8,128)(2,1)} %query_ref.1) | copy-start | bytes 786436
  13.9 11.7 %copy-start.1 = (s32[16]{0:T(128)S(1)}, s32[16]{0:T(128)}, u32[]{:S(2)}) copy-start(s32[16]{0:T(128)} %len_ref.1) | copy-start | bytes 196
  13.9 6.0 %collective-permute-start.7 = (bf16[96,256]{1,0:T(8,128)(2,1)S(1)}, bf16[96,256]{1,0:T(8,128)(2,1)S(1)}, u32[]{:S(2)}, u32[]{:S(2)}) collective-permute-start(bf16[96,256]{1,0:T(8,128)(2,1)S(1)} %get-tuple-element.55.refs_0_), channel_id=1, source_target_pairs={{0,4},{1,5},{2,6},{3,7},{4,0},{5,1},{6,2},{7,3},{8,12},{9,13},{10,... | collective-permute-start | bytes 147464 | tf_op jit(solution)/shard_map/ppermute | solution.py:425
  15.5 4.3 %collective-permute-start.8 = (bf16[96,256]{1,0:T(8,128)(2,1)S(1)}, bf16[96,256]{1,0:T(8,128)(2,1)S(1)}, u32[]{:S(2)}, u32[]{:S(2)}) collective-permute-start(bf16[96,256]{1,0:T(8,128)(2,1)S(1)} %get-tuple-element.59.refs_1_), channel_id=1, source_target_pairs={{0,4},{1,5},{2,6},{3,7},{4,0},{5,1},{6,2},{7,3},{8,12},{9,13},{10,... | collective-permute-start | bytes 147464 | tf_op jit(solution)/shard_map/ppermute | solution.py:425
  16.8 5.5 %collective-permute-start.6 = (bf16[160,256]{1,0:T(8,128)(2,1)S(1)}, bf16[160,256]{1,0:T(8,128)(2,1)S(1)}, u32[]{:S(2)}, u32[]{:S(2)}) collective-permute-start(bf16[160,256]{1,0:T(8,128)(2,1)S(1)} %get-tuple-element.56.first_ref), channel_id=1, source_target_pairs={{0,8},{1,9},{2,10},{3,11},{4,12},{5,13},{6,14},{7,15},{8,0},{9,1},... | collective-permute-start | bytes 245768 | tf_op jit(solution)/shard_map/ppermute | solution.py:425
  22.3 3.2 %collective-permute-start.9 = (bf16[256,128]{1,0:T(8,128)(2,1)S(1)}, bf16[256,128]{1,0:T(8,128)(2,1)S(1)}, u32[]{:S(2)}, u32[]{:S(2)}) collective-permute-start(bf16[256,128]{1,0:T(8,128)(2,1)S(1)} %get-tuple-element.62.own_key_ref), channel_id=1, source_target_pairs={{0,1},{1,0},{2,3},{3,2},{4,5},{5,4},{6,7},{7,6},{8,9},{9,8},{10,11... | collective-permute-start | bytes 196616 | tf_op jit(solution)/shard_map/ppermute | solution.py:425
  22.4 9.1 %collective-permute-start.10 = (bf16[96,256]{1,0:T(8,128)(2,1)S(1)}, bf16[96,256]{1,0:T(8,128)(2,1)S(1)}, u32[]{:S(2)}, u32[]{:S(2)}) collective-permute-start(bf16[96,256]{1,0:T(8,128)(2,1)S(1)} %get-tuple-element.60.after_ref.first_a), channel_id=1, source_target_pairs={{0,8},{1,9},{2,10},{3,11},{4,12},{5,13},{6,14},{7,15},{8,0},{9,1},... | collective-permute-start | bytes 147464 | tf_op jit(solution)/shard_map/ppermute | solution.py:425
  25.4 6.0 %collective-permute-start.11 = (bf16[96,256]{1,0:T(8,128)(2,1)S(1)}, bf16[96,256]{1,0:T(8,128)(2,1)S(1)}, u32[]{:S(2)}, u32[]{:S(2)}) collective-permute-start(bf16[96,256]{1,0:T(8,128)(2,1)S(1)} %get-tuple-element.72.second_a), channel_id=1, source_target_pairs={{0,8},{1,9},{2,10},{3,11},{4,12},{5,13},{6,14},{7,15},{8,0},{9,1},... | collective-permute-start | bytes 147464 | tf_op jit(solution)/shard_map/ppermute | solution.py:425
  31.5 5.9 %collective-permute-start.12 = (bf16[96,256]{1,0:T(8,128)(2,1)S(1)}, bf16[96,256]{1,0:T(8,128)(2,1)S(1)}, u32[]{:S(2)}, u32[]{:S(2)}) collective-permute-start(bf16[96,256]{1,0:T(8,128)(2,1)S(1)} %get-tuple-element.74.after_ref.own_first), channel_id=1, source_target_pairs={{0,2},{1,3},{2,0},{3,1},{4,6},{5,7},{6,4},{7,5},{8,10},{9,11},{10,... | collective-permute-start | bytes 147464 | tf_op jit(solution)/shard_map/ppermute | solution.py:425
  33.5 4.1 %collective-permute-start.13 = (bf16[96,256]{1,0:T(8,128)(2,1)S(1)}, bf16[96,256]{1,0:T(8,128)(2,1)S(1)}, u32[]{:S(2)}, u32[]{:S(2)}) collective-permute-start(bf16[96,256]{1,0:T(8,128)(2,1)S(1)} %get-tuple-element.78.own_second), channel_id=1, source_target_pairs={{0,2},{1,3},{2,0},{3,1},{4,6},{5,7},{6,4},{7,5},{8,10},{9,11},{10,... | collective-permute-start | bytes 147464 | tf_op jit(solution)/shard_map/ppermute | solution.py:425
  37.6 1.9 %collective-permute-start.14 = (bf16[384,256]{1,0:T(8,128)(2,1)S(1)}, bf16[384,256]{1,0:T(8,128)(2,1)S(1)}, u32[]{:S(2)}, u32[]{:S(2)}) collective-permute-start(bf16[384,256]{1,0:T(8,128)(2,1)S(1)} %shard_map.89.after_ref.own_ref), channel_id=1, source_target_pairs={{0,1},{1,0},{2,3},{3,2},{4,5},{5,4},{6,7},{7,6},{8,9},{9,8},{10,11... | collective-permute-start | bytes 589832 | tf_op jit(solution)/shard_map/ppermute | solution.py:425

commit v7 on v6

--- a/solution.py
+++ b/solution.py
@@ -221,12 +221,19 @@
     put_pieces(*refs[-2:], *joined_sums(scale_a, scale_b, refs[:-4], refs[-4:-2]))
 
 
-def outputs_kernel(
-    scale_a, scale_b, stat_ref, first_a, second_a, first_b, second_b, after_ref, first_out, second_out
-):
+def last_join_sum_kernel(scale_a, scale_b, *refs):
+    out_ref = refs[-1]
+    prior, sums = joined_sums(scale_a, scale_b, refs[:-3], refs[-3:-1])
+    out_ref[:PRIOR, :] = prior
+    out_ref[PRIOR:, :] = sums.astype(bf16)
+
+
+def outputs_kernel(scale_a, scale_b, stat_ref, sum_a, sum_b, after_ref, out_ref):
     me, core, bit = bits()
-    prior, sums = joined_sums(scale_a, scale_b, (first_a, second_a), (first_b, second_b))
-    put_pieces(first_out, second_out, prior, sums / stat_ref[pl.ds(CHUNKS + core * 2 + bit, 1), :])
+    row = pl.ds(core * 2 + bit, 1)
+    sums = sum_a[PRIOR:, :].astype(f32) * scale_a[row, :] + sum_b[PRIOR:, :].astype(f32) * scale_b[row, :]
+    out_ref[:PRIOR, :] = sum_a[:PRIOR, :] + sum_b[:PRIOR, :]
+    out_ref[PRIOR:, :] = (sums / stat_ref[pl.ds(CHUNKS + core * 2 + bit, 1), :]).astype(bf16)
 
 
 def gram3(high, low):
@@ -255,9 +262,9 @@
         scores = mm(key_ref[...], query_ref[columns, :], NT)
         features = jnp.exp2((scores - row_max) * EXP2_SCALE)
         target = row_mass * (M / live_total)
-        high, low = split(features)
-        feat_hi[:, columns] = high
-        feat_lo[:, columns] = low
+        top, corner = gram3(*split(features))
+        gram_ref[:HALF_M, :] = top if c == 0 else gram_ref[:HALF_M, :] + top
+        gram_ref[HALF_M:, :] = corner if c == 0 else gram_ref[HALF_M:, :] + corner
         frobenius = frobenius + total_of(features * features)
         weighted = features * target
         for tile in range(CHUNK // DH):
@@ -265,7 +272,6 @@
         high, low = split(features * (1.0 / target))
         scaled_hi[:, columns] = high
         scaled_lo[:, columns] = low
-    gram_ref[:HALF_M, :], gram_ref[HALF_M:, :] = gram3(feat_hi[...], feat_lo[...])
     linear_ref[...] = jnp.broadcast_to(jnp.sum(linear, axis=1, keepdims=True), (M, DH))
     norm_ref[...] = jnp.broadcast_to(frobenius, norm_ref.shape)
 
@@ -314,9 +320,9 @@
     power_out[...] = system * (1.0 / bound)
 
 
-def forward_kernel(own_first, own_second, side_first, side_second, after_ref, out_ref):
-    for i, ref in enumerate((own_first, own_second, side_first, side_second)):
-        out_ref[i * PIECE_ROWS : (i + 1) * PIECE_ROWS, :] = ref[...]
+def forward_kernel(own_ref, side_ref, after_ref, out_ref):
+    out_ref[:SUM_ROWS, :] = own_ref[...]
+    out_ref[SUM_ROWS:, :] = side_ref[...]
 
 
 def right_side(half_ref, half, bit, scaled_hi, scaled_lo, prior_ref):
@@ -474,7 +480,13 @@
     while mask < wide_count:
         head, scales = joined(head, got_head, first)
         got_head = exchanged(head, mask)
-        sums = call(join_sum_kernel, pieces, scales + sums + got, flops=SUM_FLOPS)
+        last = 2 * mask >= wide_count
+        sums = call(
+            last_join_sum_kernel if last else join_sum_kernel,
+            (shape(SUM_ROWS, CHUNK, bf16),) if last else pieces,
+            (*scales, *sums, *got),
+            flops=SUM_FLOPS,
+        )
         first = sums[0]
         got = both_exchanged(sums, mask)
         mask *= 2
@@ -499,18 +511,22 @@
         flops=5 * 10**9,
         scratch=[pltpu.VMEM((M, M), f32)],
     )
-    outputs = call(outputs_kernel, pieces, (*scales, stats, *sums, *got, factor))
-    side = both_exchanged(outputs, 2)
+    (outputs,) = call(
+        outputs_kernel,
+        (shape(SUM_ROWS, CHUNK, bf16),),
+        (*scales, stats, *sums, *got, factor),
+    )
+    side = exchanged(outputs, 2)
 
     def powers(power, after, steps):
         pairs = (shape(steps * M, M, bf16),) * 2
         return call(power_kernel, pairs + (shape(M, M, f32),), (power, after), flops=steps * 10**9)
 
-    early_hi, early_lo, power = powers(power, outputs[0], EARLY_STEPS)
+    early_hi, early_lo, power = powers(power, outputs, EARLY_STEPS)
     (half,) = call(
         forward_kernel,
         (shape(2 * SUM_ROWS, CHUNK, bf16),),
-        tuple(outputs) + side + (power,),
+        (outputs, side, power),
     )
     other = exchanged(half, 1)
     late_hi, late_lo, power = powers(power, half, LATE_STEPS)

time: 45.5 us -> 44.6 us (0.980)
  starting transfers between devices: 18.4 us -> 17.9 us
    ppermute x15 -> x13, starting transfers between devices: 18.4 us -> 17.9 us  [exchanged(): lax.ppermute(array, 'wide', [(i, i ^ mask) for i in range(wide_count)])]
    ppermute x15 -> x13, waiting for transfers between devices: 5.31 us -> 5.12 us  [exchanged(): lax.ppermute(array, 'wide', [(i, i ^ mask) for i in range(wide_count)])]
  transfers between devices with their start and end apart: 15 -> 13, of which waited for: 5 -> 4; matrix products, arithmetic and copies ran while one was open for 0% -> 0% of each run, Pallas kernels for 26% -> 26%
where the time goes in v7:
time: 44.6 us; the launch traced here: 44.4 us
  Pallas kernels  20.5 us (46%)
  starting transfers between devices  17.9 us (40%)
  waiting for transfers between devices  5.12 us (11%)
  between operations  0.76 us (2%)
    pallas_call x15, Pallas kernels, call(): pl.pallas_call(kernel, out_shape=tuple(outs), in_specs=in_specs or [pl.Bl...  20.5 us
    ppermute x13, starting transfers between devices, exchanged(): lax.ppermute(array, 'wide', [(i, i ^ mask) for i in range(wide_count)])  17.9 us
    ppermute x13, waiting for transfers between devices, exchanged(): lax.ppermute(array, 'wide', [(i, i ^ mask) for i in range(wide_count)])  5.12 us
  transfers between devices with their start and end apart: 13, of which 4 were waited for; matrix products, arithmetic and copies ran while one was open for 0% of the time, Pallas kernels for 26%

profile of v7, /device:TPU:0, one launch (start us, length us, event | category | flops | bytes accessed | tf_op | source)
XLA Modules:
  0.0 44.4 jit_solution(15817033059133392370)
XLA Ops:
  0.6 3.2 %shard_map.77 = (bf16[160,256]{1,0:T(8,128)(2,1)S(1)}, bf16[160,256]{1,0:T(8,128)(2,1)S(1)}, bf16[320,512]{1,0:T(8,128)(2,1)S(1)}, bf16[320,512]{1,0:T(8,128)(2,1)S(1)}) custom-call(s32[16]{0:T(128)} %len_ref.1, s32[32]{0:T(128)} %exp_hbm.1, s32[1,512]{1,0:T(1,128)} %bitcast.2, bf16[1024,128]{1,0:T(8,128)(2,1)} %mant_hbm.1, bf16[1024,128]{1,0:T(8,128)(2,1)} %value_hbm.1, ...), custom_call_target="tpu_custom_call" | custom-call | flops 1000000000 | bytes 1024 | tf_op jit(solution)/shard_map/pallas_call | solution.py:411
  3.9 0.5 %collective-permute-start.2 = (bf16[320,512]{1,0:T(8,128)(2,1)S(1)}, bf16[320,512]{1,0:T(8,128)(2,1)S(1)}, u32[]{:S(2)}, u32[]{:S(2)}) collective-permute-start(bf16[320,512]{1,0:T(8,128)(2,1)S(1)} %get-tuple-element.44), channel_id=1, source_target_pairs={{0,1},{1,0},{2,3},{3,2},{4,5},{5,4},{6,7},{7,6},{8,9},{9,8},{10,11... | collective-permute-start | bytes 983048 | tf_op jit(solution)/shard_map/ppermute | solution.py:431
  4.4 0.1 collective-permute-start
  4.5 1.3 %collective-permute-done.second_ref = bf16[160,256]{1,0:T(8,128)(2,1)S(1)} collective-permute-done((bf16[160,256]{1,0:T(8,128)(2,1)S(1)}, bf16[160,256]{1,0:T(8,128)(2,1)S(1)}, u32[]{:S(2)}, u32[]{:S(2)}) %collective-permute-start) | collective-permute-done | bytes 81952 | tf_op jit(solution)/shard_map/ppermute | solution.py:431
  5.8 3.0 %collective-permute-start.1 = (bf16[160,256]{1,0:T(8,128)(2,1)S(1)}, bf16[160,256]{1,0:T(8,128)(2,1)S(1)}, u32[]{:S(2)}, u32[]{:S(2)}) collective-permute-start(bf16[160,256]{1,0:T(8,128)(2,1)S(1)} %get-tuple-element.40.first_ref), channel_id=1, source_target_pairs={{0,2},{1,3},{2,0},{3,1},{4,6},{5,7},{6,4},{7,5},{8,10},{9,11},{10,... | collective-permute-start | bytes 245768 | tf_op jit(solution)/shard_map/ppermute | solution.py:431
  8.8 0.0 collective-permute-done.2.sum_b
  8.8 0.1 shard_map.79
  8.9 0.1 collective-permute-start.4
  9.0 2.0 %collective-permute-start.5 = (bf16[96,256]{1,0:T(8,128)(2,1)S(1)}, bf16[96,256]{1,0:T(8,128)(2,1)S(1)}, u32[]{:S(2)}, u32[]{:S(2)}) collective-permute-start(bf16[96,256]{1,0:T(8,128)(2,1)S(1)} %get-tuple-element.50), channel_id=1, source_target_pairs={{0,2},{1,3},{2,0},{3,1},{4,6},{5,7},{6,4},{7,5},{8,10},{9,11},{10,... | collective-permute-start | bytes 147464 | tf_op jit(solution)/shard_map/ppermute | solution.py:431
  11.0 0.7 %collective-permute-done.1.second_ref = bf16[160,256]{1,0:T(8,128)(2,1)S(1)} collective-permute-done((bf16[160,256]{1,0:T(8,128)(2,1)S(1)}, bf16[160,256]{1,0:T(8,128)(2,1)S(1)}, u32[]{:S(2)}, u32[]{:S(2)}) %collective-permute-start.1) | collective-permute-done | bytes 81952 | tf_op jit(solution)/shard_map/ppermute | solution.py:431
  11.6 2.1 %collective-permute-start.3 = (bf16[160,256]{1,0:T(8,128)(2,1)S(1)}, bf16[160,256]{1,0:T(8,128)(2,1)S(1)}, u32[]{:S(2)}, u32[]{:S(2)}) collective-permute-start(bf16[160,256]{1,0:T(8,128)(2,1)S(1)} %get-tuple-element.46.first_ref), channel_id=1, source_target_pairs={{0,4},{1,5},{2,6},{3,7},{4,0},{5,1},{6,2},{7,3},{8,12},{9,13},{10,... | collective-permute-start | bytes 245768 | tf_op jit(solution)/shard_map/ppermute | solution.py:431
  13.8 0.0 collective-permute-done.4.refs_1_
  13.8 0.0 collective-permute-done.5.refs_2_
  13.8 0.0 copy-start
  13.9 0.0 copy-start.1
  13.9 1.7 %collective-permute-start.7 = (bf16[96,256]{1,0:T(8,128)(2,1)S(1)}, bf16[96,256]{1,0:T(8,128)(2,1)S(1)}, u32[]{:S(2)}, u32[]{:S(2)}) collective-permute-start(bf16[96,256]{1,0:T(8,128)(2,1)S(1)} %get-tuple-element.51.refs_0_), channel_id=1, source_target_pairs={{0,4},{1,5},{2,6},{3,7},{4,0},{5,1},{6,2},{7,3},{8,12},{9,13},{10,... | collective-permute-start | bytes 147464 | tf_op jit(solution)/shard_map/ppermute | solution.py:431
  15.5 0.4 collective-permute-start.8
  16.0 0.8 %collective-permute-done.3.second_ref = bf16[160,256]{1,0:T(8,128)(2,1)S(1)} collective-permute-done((bf16[160,256]{1,0:T(8,128)(2,1)S(1)}, bf16[160,256]{1,0:T(8,128)(2,1)S(1)}, u32[]{:S(2)}, u32[]{:S(2)}) %collective-permute-start.3) | collective-permute-done | bytes 81952 | tf_op jit(solution)/shard_map/ppermute | solution.py:431
  16.8 3.1 %collective-permute-start.6 = (bf16[160,256]{1,0:T(8,128)(2,1)S(1)}, bf16[160,256]{1,0:T(8,128)(2,1)S(1)}, u32[]{:S(2)}, u32[]{:S(2)}) collective-permute-start(bf16[160,256]{1,0:T(8,128)(2,1)S(1)} %get-tuple-element.52.first_ref), channel_id=1, source_target_pairs={{0,8},{1,9},{2,10},{3,11},{4,12},{5,13},{6,14},{7,15},{8,0},{9,1},... | collective-permute-start | bytes 245768 | tf_op jit(solution)/shard_map/ppermute | solution.py:431
  19.9 0.0 collective-permute-done.7.refs_2_
  19.9 0.0 collective-permute-done.8.refs_3_
  19.9 2.4 %collective-permute-done.6.second_ref = bf16[160,256]{1,0:T(8,128)(2,1)S(1)} collective-permute-done((bf16[160,256]{1,0:T(8,128)(2,1)S(1)}, bf16[160,256]{1,0:T(8,128)(2,1)S(1)}, u32[]{:S(2)}, u32[]{:S(2)}) %collective-permute-start.6) | collective-permute-done | bytes 81952 | tf_op jit(solution)/shard_map/ppermute | solution.py:431
  22.3 0.1 collective-permute-start.9
  22.4 3.0 %collective-permute-start.10 = (bf16[192,256]{1,0:T(8,128)(2,1)S(1)}, bf16[192,256]{1,0:T(8,128)(2,1)S(1)}, u32[]{:S(2)}, u32[]{:S(2)}) collective-permute-start(bf16[192,256]{1,0:T(8,128)(2,1)S(1)} %shard_map.83.after_ref.sum_a), channel_id=1, source_target_pairs={{0,8},{1,9},{2,10},{3,11},{4,12},{5,13},{6,14},{7,15},{8,0},{9,1},... | collective-permute-start | bytes 294920 | tf_op jit(solution)/shard_map/ppermute | solution.py:431
  25.5 0.0 collective-permute-done.9.other_key_ref
  25.5 0.0 copy-done
  25.5 0.0 copy-done.1
  25.5 2.9 %shard_map.85 = (f32[512,512]{1,0:T(8,128)S(1)}, f32[512,128]{1,0:T(8,128)S(1)}, f32[8,128]{1,0:T(8,128)S(1)}, bf16[512,1024]{1,0:T(8,128)(2,1)S(1)}, bf16[512,1024]{1,0:T(8,128)(2,1)S(1)}) custom-call(s32[16]{0:T(128)S(1)} %copy-done.1, bf16[1024,128]{1,0:T(8,128)(2,1)S(1)} %copy-done, f32[8,256]{1,0:T(8,128)S(1)} %get-tuple-element.56.stat_ref, ...), custom_call_target="tpu_custom_call" | custom-call | flops 1000000000 | bytes 1024 | tf_op jit(solution)/shard_map/pallas_call | solution.py:411
  28.4 2.9 %shard_map.86 = (f32[1,512]{1,0:T(1,128)}, f32[8,512]{1,0:T(8,128)S(1)}, f32[512,512]{1,0:T(8,128)S(1)}) custom-call(f32[512,512]{1,0:T(8,128)S(1)} %get-tuple-element.58.gram_ref, f32[512,128]{1,0:T(8,128)S(1)} %get-tuple-element.59.linear_ref, f32[8,128]{1,0:T(8,128)S(1)} %get-tuple-element.60.norm_ref, bf16[512,1024]{1,0:T(8,128)(2,1)S(1)} %get-tuple-element.61.scaled_hi, ...), custom_call_target="tpu_custom_call" | custom-call | flops 5000000000 | bytes 1024 | tf_op jit(solution)/shard_map/pallas_call | solution.py:411
  31.3 0.0 collective-permute-done.10.sum_b
  31.3 1.7 %collective-permute-start.11 = (bf16[192,256]{1,0:T(8,128)(2,1)S(1)}, bf16[192,256]{1,0:T(8,128)(2,1)S(1)}, u32[]{:S(2)}, u32[]{:S(2)}) collective-permute-start(bf16[192,256]{1,0:T(8,128)(2,1)S(1)} %shard_map.87.after_ref.own_ref), channel_id=1, source_target_pairs={{0,2},{1,3},{2,0},{3,1},{4,6},{5,7},{6,4},{7,5},{8,10},{9,11},{10,... | collective-permute-start | bytes 294920 | tf_op jit(solution)/shard_map/ppermute | solution.py:431
  33.1 3.8 %shard_map.88 = (bf16[2048,512]{1,0:T(8,128)(2,1)S(1)}, bf16[2048,512]{1,0:T(8,128)(2,1)S(1)}, f32[512,512]{1,0:T(8,128)S(1)}) custom-call(f32[512,512]{1,0:T(8,128)S(1)} %get-tuple-element.64.power_in, bf16[192,256]{1,0:T(8,128)(2,1)S(1)} %shard_map.87.after_ref.own_ref), custom_call_target="tpu_custom_call" | custom-call | flops 4000000000 | bytes 1024 | tf_op jit(solution)/shard_map/pallas_call | solution.py:411
  36.8 0.0 collective-permute-done.11.side_ref
  36.8 0.1 collective-permute-start.12
  36.9 1.8 %shard_map.90 = (bf16[1024,512]{1,0:T(8,128)(2,1)S(1)}, bf16[1024,512]{1,0:T(8,128)(2,1)S(1)}, f32[512,512]{1,0:T(8,128)S(1)}) custom-call(f32[512,512]{1,0:T(8,128)S(1)} %get-tuple-element.70.after_ref.power_in, bf16[384,256]{1,0:T(8,128)(2,1)S(1)} %shard_map.89.after_ref.own_ref), custom_call_target="tpu_custom_call" | custom-call | flops 2000000000 | bytes 1024 | tf_op jit(solution)/shard_map/pallas_call | solution.py:411
  38.8 0.0 collective-permute-done.12.half_ref
  38.8 5.6 %shard_map.91 = f32[512,128]{1,0:T(8,128)} custom-call(bf16[2048,512]{1,0:T(8,128)(2,1)S(1)} %get-tuple-element.68.early_hi, bf16[2048,512]{1,0:T(8,128)(2,1)S(1)} %get-tuple-element.69.early_lo, bf16[1024,512]{1,0:T(8,128)(2,1)S(1)} %get-tuple-element.71.late_hi, bf16[1024,512]{1,0:T(8,128)(2,1)S(1)} %get-tuple-element.72.late_lo, ...), custom_call_target="tpu_custom_call" | custom-call | tf_op jit(solution)/shard_map/pallas_call | solution.py:411
  (8 shorter events, 0.2 us)
Async XLA Ops:
  3.9 4.9 %collective-permute-start.2 = (bf16[320,512]{1,0:T(8,128)(2,1)S(1)}, bf16[320,512]{1,0:T(8,128)(2,1)S(1)}, u32[]{:S(2)}, u32[]{:S(2)}) collective-permute-start(bf16[320,512]{1,0:T(8,128)(2,1)S(1)} %get-tuple-element.44), channel_id=1, source_target_pairs={{0,1},{1,0},{2,3},{3,2},{4,5},{5,4},{6,7},{7,6},{8,9},{9,8},{10,11... | collective-permute-start | bytes 983048 | tf_op jit(solution)/shard_map/ppermute | solution.py:431
  4.4 1.4 %collective-permute-start = (bf16[160,256]{1,0:T(8,128)(2,1)S(1)}, bf16[160,256]{1,0:T(8,128)(2,1)S(1)}, u32[]{:S(2)}, u32[]{:S(2)}) collective-permute-start(bf16[160,256]{1,0:T(8,128)(2,1)S(1)} %get-tuple-element.39), channel_id=1, source_target_pairs={{0,1},{1,0},{2,3},{3,2},{4,5},{5,4},{6,7},{7,6},{8,9},{9,8},{10,11... | collective-permute-start | bytes 245768 | tf_op jit(solution)/shard_map/ppermute | solution.py:431
  5.8 5.8 %collective-permute-start.1 = (bf16[160,256]{1,0:T(8,128)(2,1)S(1)}, bf16[160,256]{1,0:T(8,128)(2,1)S(1)}, u32[]{:S(2)}, u32[]{:S(2)}) collective-permute-start(bf16[160,256]{1,0:T(8,128)(2,1)S(1)} %get-tuple-element.40.first_ref), channel_id=1, source_target_pairs={{0,2},{1,3},{2,0},{3,1},{4,6},{5,7},{6,4},{7,5},{8,10},{9,11},{10,... | collective-permute-start | bytes 245768 | tf_op jit(solution)/shard_map/ppermute | solution.py:431
  8.9 4.9 %collective-permute-start.4 = (bf16[96,256]{1,0:T(8,128)(2,1)S(1)}, bf16[96,256]{1,0:T(8,128)(2,1)S(1)}, u32[]{:S(2)}, u32[]{:S(2)}) collective-permute-start(bf16[96,256]{1,0:T(8,128)(2,1)S(1)} %get-tuple-element.45.refs_0_), channel_id=1, source_target_pairs={{0,2},{1,3},{2,0},{3,1},{4,6},{5,7},{6,4},{7,5},{8,10},{9,11},{10,... | collective-permute-start | bytes 147464 | tf_op jit(solution)/shard_map/ppermute | solution.py:431
  9.0 4.8 %collective-permute-start.5 = (bf16[96,256]{1,0:T(8,128)(2,1)S(1)}, bf16[96,256]{1,0:T(8,128)(2,1)S(1)}, u32[]{:S(2)}, u32[]{:S(2)}) collective-permute-start(bf16[96,256]{1,0:T(8,128)(2,1)S(1)} %get-tuple-element.50), channel_id=1, source_target_pairs={{0,2},{1,3},{2,0},{3,1},{4,6},{5,7},{6,4},{7,5},{8,10},{9,11},{10,... | collective-permute-start | bytes 147464 | tf_op jit(solution)/shard_map/ppermute | solution.py:431
  11.6 5.1 %collective-permute-start.3 = (bf16[160,256]{1,0:T(8,128)(2,1)S(1)}, bf16[160,256]{1,0:T(8,128)(2,1)S(1)}, u32[]{:S(2)}, u32[]{:S(2)}) collective-permute-start(bf16[160,256]{1,0:T(8,128)(2,1)S(1)} %get-tuple-element.46.first_ref), channel_id=1, source_target_pairs={{0,4},{1,5},{2,6},{3,7},{4,0},{5,1},{6,2},{7,3},{8,12},{9,13},{10,... | collective-permute-start | bytes 245768 | tf_op jit(solution)/shard_map/ppermute | solution.py:431
  13.8 11.6 %copy-start = (bf16[1024,128]{1,0:T(8,128)(2,1)S(1)}, bf16[1024,128]{1,0:T(8,128)(2,1)}, u32[]{:S(2)}) copy-start(bf16[1024,128]{1,0:T(8,128)(2,1)} %query_ref.1) | copy-start | bytes 786436
  13.9 11.6 %copy-start.1 = (s32[16]{0:T(128)S(1)}, s32[16]{0:T(128)}, u32[]{:S(2)}) copy-start(s32[16]{0:T(128)} %len_ref.1) | copy-start | bytes 196
  13.9 6.0 %collective-permute-start.7 = (bf16[96,256]{1,0:T(8,128)(2,1)S(1)}, bf16[96,256]{1,0:T(8,128)(2,1)S(1)}, u32[]{:S(2)}, u32[]{:S(2)}) collective-permute-start(bf16[96,256]{1,0:T(8,128)(2,1)S(1)} %get-tuple-element.51.refs_0_), channel_id=1, source_target_pairs={{0,4},{1,5},{2,6},{3,7},{4,0},{5,1},{6,2},{7,3},{8,12},{9,13},{10,... | collective-permute-start | bytes 147464 | tf_op jit(solution)/shard_map/ppermute | solution.py:431
  15.5 4.3 %collective-permute-start.8 = (bf16[96,256]{1,0:T(8,128)(2,1)S(1)}, bf16[96,256]{1,0:T(8,128)(2,1)S(1)}, u32[]{:S(2)}, u32[]{:S(2)}) collective-permute-start(bf16[96,256]{1,0:T(8,128)(2,1)S(1)} %get-tuple-element.55.refs_1_), channel_id=1, source_target_pairs={{0,4},{1,5},{2,6},{3,7},{4,0},{5,1},{6,2},{7,3},{8,12},{9,13},{10,... | collective-permute-start | bytes 147464 | tf_op jit(solution)/shard_map/ppermute | solution.py:431
  16.8 5.5 %collective-permute-start.6 = (bf16[160,256]{1,0:T(8,128)(2,1)S(1)}, bf16[160,256]{1,0:T(8,128)(2,1)S(1)}, u32[]{:S(2)}, u32[]{:S(2)}) collective-permute-start(bf16[160,256]{1,0:T(8,128)(2,1)S(1)} %get-tuple-element.52.first_ref), channel_id=1, source_target_pairs={{0,8},{1,9},{2,10},{3,11},{4,12},{5,13},{6,14},{7,15},{8,0},{9,1},... | collective-permute-start | bytes 245768 | tf_op jit(solution)/shard_map/ppermute | solution.py:431
  22.3 3.1 %collective-permute-start.9 = (bf16[256,128]{1,0:T(8,128)(2,1)S(1)}, bf16[256,128]{1,0:T(8,128)(2,1)S(1)}, u32[]{:S(2)}, u32[]{:S(2)}) collective-permute-start(bf16[256,128]{1,0:T(8,128)(2,1)S(1)} %get-tuple-element.57.own_key_ref), channel_id=1, source_target_pairs={{0,1},{1,0},{2,3},{3,2},{4,5},{5,4},{6,7},{7,6},{8,9},{9,8},{10,11... | collective-permute-start | bytes 196616 | tf_op jit(solution)/shard_map/ppermute | solution.py:431
  22.4 8.9 %collective-permute-start.10 = (bf16[192,256]{1,0:T(8,128)(2,1)S(1)}, bf16[192,256]{1,0:T(8,128)(2,1)S(1)}, u32[]{:S(2)}, u32[]{:S(2)}) collective-permute-start(bf16[192,256]{1,0:T(8,128)(2,1)S(1)} %shard_map.83.after_ref.sum_a), channel_id=1, source_target_pairs={{0,8},{1,9},{2,10},{3,11},{4,12},{5,13},{6,14},{7,15},{8,0},{9,1},... | collective-permute-start | bytes 294920 | tf_op jit(solution)/shard_map/ppermute | solution.py:431
  31.3 5.5 %collective-permute-start.11 = (bf16[192,256]{1,0:T(8,128)(2,1)S(1)}, bf16[192,256]{1,0:T(8,128)(2,1)S(1)}, u32[]{:S(2)}, u32[]{:S(2)}) collective-permute-start(bf16[192,256]{1,0:T(8,128)(2,1)S(1)} %shard_map.87.after_ref.own_ref), channel_id=1, source_target_pairs={{0,2},{1,3},{2,0},{3,1},{4,6},{5,7},{6,4},{7,5},{8,10},{9,11},{10,... | collective-permute-start | bytes 294920 | tf_op jit(solution)/shard_map/ppermute | solution.py:431
  36.8 1.9 %collective-permute-start.12 = (bf16[384,256]{1,0:T(8,128)(2,1)S(1)}, bf16[384,256]{1,0:T(8,128)(2,1)S(1)}, u32[]{:S(2)}, u32[]{:S(2)}) collective-permute-start(bf16[384,256]{1,0:T(8,128)(2,1)S(1)} %shard_map.89.after_ref.own_ref), channel_id=1, source_target_pairs={{0,1},{1,0},{2,3},{3,2},{4,5},{5,4},{6,7},{7,6},{8,9},{9,8},{10,11... | collective-permute-start | bytes 589832 | tf_op jit(solution)/shard_map/ppermute | solution.py:431

commit v8 on v7

--- a/solution.py
+++ b/solution.py
@@ -195,6 +195,10 @@
         key_out[rows, :] = first_ref[:KEY_ROWS, columns] + second_ref[:KEY_ROWS, columns]
 
 
+def copy_kernel(sum_ref, after_ref, out_ref):
+    out_ref[...] = sum_ref[...]
+
+
 def halve_sum_kernel(scale_a, scale_b, sum_a, sum_b, first_out, second_out, keep_out):
     me, core, bit = bits()
 
@@ -466,9 +470,10 @@
         head, *scales = call(join_kernel, (head_shape, scale_shape, scale_shape), arrays)
         return head, tuple(scales)
 
-    got = exchanged(send, 1)
     head, scales = joined(head, exchanged(send_head, 1))
     got_head = exchanged(head, 2)
+    (send,) = call(copy_kernel, (half_sum,), (send, head))
+    got = exchanged(send, 1)
     first, second, keep = call(
         halve_sum_kernel,
         pieces + (shape(PAIR_ROWS, CHUNK, bf16),),

time: 44.6 us -> 44.2 us (level)
    pallas_call x15 -> x16, Pallas kernels: 20.5 us -> 20.6 us  [call(): pl.pallas_call(kernel, out_shape=tuple(outs), in_specs=in_specs or [pl.Bl...]
  transfers between devices with their start and end apart: 13 -> 13, of which waited for: 4 -> 5; matrix products, arithmetic and copies ran while one was open for 0% -> 0% of each run, Pallas kernels for 26% -> 26%
where the time goes in v8:
time: 44.2 us; the launch traced here: 44 us
  Pallas kernels  20.6 us (47%)
  starting transfers between devices  18 us (41%)
  waiting for transfers between devices  4.7 us (11%)
  between operations  0.77 us (2%)
    pallas_call x16, Pallas kernels, call(): pl.pallas_call(kernel, out_shape=tuple(outs), in_specs=in_specs or [pl.Bl...  20.6 us
    ppermute x13, starting transfers between devices, exchanged(): lax.ppermute(array, 'wide', [(i, i ^ mask) for i in range(wide_count)])  18 us
    ppermute x13, waiting for transfers between devices, exchanged(): lax.ppermute(array, 'wide', [(i, i ^ mask) for i in range(wide_count)])  4.7 us
  transfers between devices with their start and end apart: 13, of which 5 were waited for; matrix products, arithmetic and copies ran while one was open for 0% of the time, Pallas kernels for 26%

profile of v8, /device:TPU:0, one launch (start us, length us, event | category | flops | bytes accessed | tf_op | source)
XLA Modules:
  0.0 44.0 jit_solution(14817027672568748240)
XLA Ops:
  0.6 3.2 %shard_map.77 = (bf16[160,256]{1,0:T(8,128)(2,1)S(1)}, bf16[160,256]{1,0:T(8,128)(2,1)S(1)}, bf16[320,512]{1,0:T(8,128)(2,1)S(1)}, bf16[320,512]{1,0:T(8,128)(2,1)S(1)}) custom-call(s32[16]{0:T(128)} %len_ref.1, s32[32]{0:T(128)} %exp_hbm.1, s32[1,512]{1,0:T(1,128)} %bitcast.2, bf16[1024,128]{1,0:T(8,128)(2,1)} %mant_hbm.1, bf16[1024,128]{1,0:T(8,128)(2,1)} %value_hbm.1, ...), custom_call_target="tpu_custom_call" | custom-call | flops 1000000000 | bytes 1024 | tf_op jit(solution)/shard_map/pallas_call | solution.py:415
  3.9 0.5 %collective-permute-start = (bf16[160,256]{1,0:T(8,128)(2,1)S(1)}, bf16[160,256]{1,0:T(8,128)(2,1)S(1)}, u32[]{:S(2)}, u32[]{:S(2)}) collective-permute-start(bf16[160,256]{1,0:T(8,128)(2,1)S(1)} %get-tuple-element.39), channel_id=1, source_target_pairs={{0,1},{1,0},{2,3},{3,2},{4,5},{5,4},{6,7},{7,6},{8,9},{9,8},{10,11... | collective-permute-start | bytes 245768 | tf_op jit(solution)/shard_map/ppermute | solution.py:435
  4.4 0.9 %collective-permute-done.second_ref = bf16[160,256]{1,0:T(8,128)(2,1)S(1)} collective-permute-done((bf16[160,256]{1,0:T(8,128)(2,1)S(1)}, bf16[160,256]{1,0:T(8,128)(2,1)S(1)}, u32[]{:S(2)}, u32[]{:S(2)}) %collective-permute-start) | collective-permute-done | bytes 81952 | tf_op jit(solution)/shard_map/ppermute | solution.py:435
  5.4 0.4 collective-permute-start.2
  5.8 2.7 %collective-permute-start.1 = (bf16[160,256]{1,0:T(8,128)(2,1)S(1)}, bf16[160,256]{1,0:T(8,128)(2,1)S(1)}, u32[]{:S(2)}, u32[]{:S(2)}) collective-permute-start(bf16[160,256]{1,0:T(8,128)(2,1)S(1)} %get-tuple-element.40.after_ref.first_ref), channel_id=1, source_target_pairs={{0,2},{1,3},{2,0},{3,1},{4,6},{5,7},{6,4},{7,5},{8,10},{9,11},{10,... | collective-permute-start | bytes 245768 | tf_op jit(solution)/shard_map/ppermute | solution.py:435
  8.5 0.0 collective-permute-done.2.sum_b
  8.5 0.1 shard_map.80
  8.6 1.5 %collective-permute-start.4 = (bf16[96,256]{1,0:T(8,128)(2,1)S(1)}, bf16[96,256]{1,0:T(8,128)(2,1)S(1)}, u32[]{:S(2)}, u32[]{:S(2)}) collective-permute-start(bf16[96,256]{1,0:T(8,128)(2,1)S(1)} %get-tuple-element.45.refs_0_), channel_id=1, source_target_pairs={{0,2},{1,3},{2,0},{3,1},{4,6},{5,7},{6,4},{7,5},{8,10},{9,11},{10,... | collective-permute-start | bytes 147464 | tf_op jit(solution)/shard_map/ppermute | solution.py:435
  10.1 0.6 %collective-permute-start.5 = (bf16[96,256]{1,0:T(8,128)(2,1)S(1)}, bf16[96,256]{1,0:T(8,128)(2,1)S(1)}, u32[]{:S(2)}, u32[]{:S(2)}) collective-permute-start(bf16[96,256]{1,0:T(8,128)(2,1)S(1)} %get-tuple-element.50), channel_id=1, source_target_pairs={{0,2},{1,3},{2,0},{3,1},{4,6},{5,7},{6,4},{7,5},{8,10},{9,11},{10,... | collective-permute-start | bytes 147464 | tf_op jit(solution)/shard_map/ppermute | solution.py:435
  10.7 0.8 %collective-permute-done.1.second_ref = bf16[160,256]{1,0:T(8,128)(2,1)S(1)} collective-permute-done((bf16[160,256]{1,0:T(8,128)(2,1)S(1)}, bf16[160,256]{1,0:T(8,128)(2,1)S(1)}, u32[]{:S(2)}, u32[]{:S(2)}) %collective-permute-start.1) | collective-permute-done | bytes 81952 | tf_op jit(solution)/shard_map/ppermute | solution.py:435
  11.5 2.1 %collective-permute-start.3 = (bf16[160,256]{1,0:T(8,128)(2,1)S(1)}, bf16[160,256]{1,0:T(8,128)(2,1)S(1)}, u32[]{:S(2)}, u32[]{:S(2)}) collective-permute-start(bf16[160,256]{1,0:T(8,128)(2,1)S(1)} %get-tuple-element.46.first_ref), channel_id=1, source_target_pairs={{0,4},{1,5},{2,6},{3,7},{4,0},{5,1},{6,2},{7,3},{8,12},{9,13},{10,... | collective-permute-start | bytes 245768 | tf_op jit(solution)/shard_map/ppermute | solution.py:435
  13.6 0.0 collective-permute-done.4.refs_1_
  13.6 0.6 %collective-permute-done.5.refs_2_ = bf16[96,256]{1,0:T(8,128)(2,1)S(1)} collective-permute-done((bf16[96,256]{1,0:T(8,128)(2,1)S(1)}, bf16[96,256]{1,0:T(8,128)(2,1)S(1)}, u32[]{:S(2)}, u32[]{:S(2)}) %collective-permute-start.5) | collective-permute-done | bytes 49184 | tf_op jit(solution)/shard_map/ppermute | solution.py:435
  14.3 0.0 copy-start
  14.3 0.0 copy-start.1
  14.3 1.7 %collective-permute-start.7 = (bf16[96,256]{1,0:T(8,128)(2,1)S(1)}, bf16[96,256]{1,0:T(8,128)(2,1)S(1)}, u32[]{:S(2)}, u32[]{:S(2)}) collective-permute-start(bf16[96,256]{1,0:T(8,128)(2,1)S(1)} %get-tuple-element.51.refs_0_), channel_id=1, source_target_pairs={{0,4},{1,5},{2,6},{3,7},{4,0},{5,1},{6,2},{7,3},{8,12},{9,13},{10,... | collective-permute-start | bytes 147464 | tf_op jit(solution)/shard_map/ppermute | solution.py:435
  16.0 0.4 collective-permute-start.8
  16.4 0.0 collective-permute-done.3.second_ref
  16.4 3.3 %collective-permute-start.6 = (bf16[160,256]{1,0:T(8,128)(2,1)S(1)}, bf16[160,256]{1,0:T(8,128)(2,1)S(1)}, u32[]{:S(2)}, u32[]{:S(2)}) collective-permute-start(bf16[160,256]{1,0:T(8,128)(2,1)S(1)} %get-tuple-element.52.first_ref), channel_id=1, source_target_pairs={{0,8},{1,9},{2,10},{3,11},{4,12},{5,13},{6,14},{7,15},{8,0},{9,1},... | collective-permute-start | bytes 245768 | tf_op jit(solution)/shard_map/ppermute | solution.py:435
  19.7 0.0 collective-permute-done.7.refs_2_
  19.7 0.3 collective-permute-done.8.refs_3_
  20.1 2.1 %collective-permute-done.6.second_ref = bf16[160,256]{1,0:T(8,128)(2,1)S(1)} collective-permute-done((bf16[160,256]{1,0:T(8,128)(2,1)S(1)}, bf16[160,256]{1,0:T(8,128)(2,1)S(1)}, u32[]{:S(2)}, u32[]{:S(2)}) %collective-permute-start.6) | collective-permute-done | bytes 81952 | tf_op jit(solution)/shard_map/ppermute | solution.py:435
  22.2 0.1 collective-permute-start.9
  22.3 3.0 %collective-permute-start.10 = (bf16[192,256]{1,0:T(8,128)(2,1)S(1)}, bf16[192,256]{1,0:T(8,128)(2,1)S(1)}, u32[]{:S(2)}, u32[]{:S(2)}) collective-permute-start(bf16[192,256]{1,0:T(8,128)(2,1)S(1)} %shard_map.84.after_ref.sum_a), channel_id=1, source_target_pairs={{0,8},{1,9},{2,10},{3,11},{4,12},{5,13},{6,14},{7,15},{8,0},{9,1},... | collective-permute-start | bytes 294920 | tf_op jit(solution)/shard_map/ppermute | solution.py:435
  25.3 0.0 collective-permute-done.9.other_key_ref
  25.3 0.0 copy-done
  25.3 0.0 copy-done.1
  25.3 2.9 %shard_map.86 = (f32[512,512]{1,0:T(8,128)S(1)}, f32[512,128]{1,0:T(8,128)S(1)}, f32[8,128]{1,0:T(8,128)S(1)}, bf16[512,1024]{1,0:T(8,128)(2,1)S(1)}, bf16[512,1024]{1,0:T(8,128)(2,1)S(1)}) custom-call(s32[16]{0:T(128)S(1)} %copy-done.1, bf16[1024,128]{1,0:T(8,128)(2,1)S(1)} %copy-done, f32[8,256]{1,0:T(8,128)S(1)} %get-tuple-element.56.stat_ref, ...), custom_call_target="tpu_custom_call" | custom-call | flops 1000000000 | bytes 1024 | tf_op jit(solution)/shard_map/pallas_call | solution.py:415
  28.3 2.9 %shard_map.87 = (f32[1,512]{1,0:T(1,128)}, f32[8,512]{1,0:T(8,128)S(1)}, f32[512,512]{1,0:T(8,128)S(1)}) custom-call(f32[512,512]{1,0:T(8,128)S(1)} %get-tuple-element.58.gram_ref, f32[512,128]{1,0:T(8,128)S(1)} %get-tuple-element.59.linear_ref, f32[8,128]{1,0:T(8,128)S(1)} %get-tuple-element.60.norm_ref, bf16[512,1024]{1,0:T(8,128)(2,1)S(1)} %get-tuple-element.61.scaled_hi, ...), custom_call_target="tpu_custom_call" | custom-call | flops 5000000000 | bytes 1024 | tf_op jit(solution)/shard_map/pallas_call | solution.py:415
  31.1 0.0 collective-permute-done.10.sum_b
  31.2 1.6 %collective-permute-start.11 = (bf16[192,256]{1,0:T(8,128)(2,1)S(1)}, bf16[192,256]{1,0:T(8,128)(2,1)S(1)}, u32[]{:S(2)}, u32[]{:S(2)}) collective-permute-start(bf16[192,256]{1,0:T(8,128)(2,1)S(1)} %shard_map.88.after_ref.own_ref), channel_id=1, source_target_pairs={{0,2},{1,3},{2,0},{3,1},{4,6},{5,7},{6,4},{7,5},{8,10},{9,11},{10,... | collective-permute-start | bytes 294920 | tf_op jit(solution)/shard_map/ppermute | solution.py:435
  32.8 3.8 %shard_map.89 = (bf16[2048,512]{1,0:T(8,128)(2,1)S(1)}, bf16[2048,512]{1,0:T(8,128)(2,1)S(1)}, f32[512,512]{1,0:T(8,128)S(1)}) custom-call(f32[512,512]{1,0:T(8,128)S(1)} %get-tuple-element.64.power_in, bf16[192,256]{1,0:T(8,128)(2,1)S(1)} %shard_map.88.after_ref.own_ref), custom_call_target="tpu_custom_call" | custom-call | flops 4000000000 | bytes 1024 | tf_op jit(solution)/shard_map/pallas_call | solution.py:415
  36.5 0.0 collective-permute-done.11.side_ref
  36.5 0.1 collective-permute-start.12
  36.6 1.8 %shard_map.91 = (bf16[1024,512]{1,0:T(8,128)(2,1)S(1)}, bf16[1024,512]{1,0:T(8,128)(2,1)S(1)}, f32[512,512]{1,0:T(8,128)S(1)}) custom-call(f32[512,512]{1,0:T(8,128)S(1)} %get-tuple-element.70.after_ref.power_in, bf16[384,256]{1,0:T(8,128)(2,1)S(1)} %shard_map.90.after_ref.own_ref), custom_call_target="tpu_custom_call" | custom-call | flops 2000000000 | bytes 1024 | tf_op jit(solution)/shard_map/pallas_call | solution.py:415
  38.5 0.0 collective-permute-done.12.half_ref
  38.5 5.6 %shard_map.92 = f32[512,128]{1,0:T(8,128)} custom-call(bf16[2048,512]{1,0:T(8,128)(2,1)S(1)} %get-tuple-element.68.early_hi, bf16[2048,512]{1,0:T(8,128)(2,1)S(1)} %get-tuple-element.69.early_lo, bf16[1024,512]{1,0:T(8,128)(2,1)S(1)} %get-tuple-element.71.late_hi, bf16[1024,512]{1,0:T(8,128)(2,1)S(1)} %get-tuple-element.72.late_lo, ...), custom_call_target="tpu_custom_call" | custom-call | tf_op jit(solution)/shard_map/pallas_call | solution.py:415
  (9 shorter events, 0.3 us)
Async XLA Ops:
  3.9 1.4 %collective-permute-start = (bf16[160,256]{1,0:T(8,128)(2,1)S(1)}, bf16[160,256]{1,0:T(8,128)(2,1)S(1)}, u32[]{:S(2)}, u32[]{:S(2)}) collective-permute-start(bf16[160,256]{1,0:T(8,128)(2,1)S(1)} %get-tuple-element.39), channel_id=1, source_target_pairs={{0,1},{1,0},{2,3},{3,2},{4,5},{5,4},{6,7},{7,6},{8,9},{9,8},{10,11... | collective-permute-start | bytes 245768 | tf_op jit(solution)/shard_map/ppermute | solution.py:435
  5.4 3.1 %collective-permute-start.2 = (bf16[320,512]{1,0:T(8,128)(2,1)S(1)}, bf16[320,512]{1,0:T(8,128)(2,1)S(1)}, u32[]{:S(2)}, u32[]{:S(2)}) collective-permute-start(bf16[320,512]{1,0:T(8,128)(2,1)S(1)} %shard_map.79), channel_id=1, source_target_pairs={{0,1},{1,0},{2,3},{3,2},{4,5},{5,4},{6,7},{7,6},{8,9},{9,8},{10,11... | collective-permute-start | bytes 983048 | tf_op jit(solution)/shard_map/ppermute | solution.py:435
  5.8 5.7 %collective-permute-start.1 = (bf16[160,256]{1,0:T(8,128)(2,1)S(1)}, bf16[160,256]{1,0:T(8,128)(2,1)S(1)}, u32[]{:S(2)}, u32[]{:S(2)}) collective-permute-start(bf16[160,256]{1,0:T(8,128)(2,1)S(1)} %get-tuple-element.40.after_ref.first_ref), channel_id=1, source_target_pairs={{0,2},{1,3},{2,0},{3,1},{4,6},{5,7},{6,4},{7,5},{8,10},{9,11},{10,... | collective-permute-start | bytes 245768 | tf_op jit(solution)/shard_map/ppermute | solution.py:435
  8.6 5.0 %collective-permute-start.4 = (bf16[96,256]{1,0:T(8,128)(2,1)S(1)}, bf16[96,256]{1,0:T(8,128)(2,1)S(1)}, u32[]{:S(2)}, u32[]{:S(2)}) collective-permute-start(bf16[96,256]{1,0:T(8,128)(2,1)S(1)} %get-tuple-element.45.refs_0_), channel_id=1, source_target_pairs={{0,2},{1,3},{2,0},{3,1},{4,6},{5,7},{6,4},{7,5},{8,10},{9,11},{10,... | collective-permute-start | bytes 147464 | tf_op jit(solution)/shard_map/ppermute | solution.py:435
  10.1 4.1 %collective-permute-start.5 = (bf16[96,256]{1,0:T(8,128)(2,1)S(1)}, bf16[96,256]{1,0:T(8,128)(2,1)S(1)}, u32[]{:S(2)}, u32[]{:S(2)}) collective-permute-start(bf16[96,256]{1,0:T(8,128)(2,1)S(1)} %get-tuple-element.50), channel_id=1, source_target_pairs={{0,2},{1,3},{2,0},{3,1},{4,6},{5,7},{6,4},{7,5},{8,10},{9,11},{10,... | collective-permute-start | bytes 147464 | tf_op jit(solution)/shard_map/ppermute | solution.py:435
  11.5 4.9 %collective-permute-start.3 = (bf16[160,256]{1,0:T(8,128)(2,1)S(1)}, bf16[160,256]{1,0:T(8,128)(2,1)S(1)}, u32[]{:S(2)}, u32[]{:S(2)}) collective-permute-start(bf16[160,256]{1,0:T(8,128)(2,1)S(1)} %get-tuple-element.46.first_ref), channel_id=1, source_target_pairs={{0,4},{1,5},{2,6},{3,7},{4,0},{5,1},{6,2},{7,3},{8,12},{9,13},{10,... | collective-permute-start | bytes 245768 | tf_op jit(solution)/shard_map/ppermute | solution.py:435
  14.3 11.0 %copy-start = (bf16[1024,128]{1,0:T(8,128)(2,1)S(1)}, bf16[1024,128]{1,0:T(8,128)(2,1)}, u32[]{:S(2)}) copy-start(bf16[1024,128]{1,0:T(8,128)(2,1)} %query_ref.1) | copy-start | bytes 786436
  14.3 11.0 %copy-start.1 = (s32[16]{0:T(128)S(1)}, s32[16]{0:T(128)}, u32[]{:S(2)}) copy-start(s32[16]{0:T(128)} %len_ref.1) | copy-start | bytes 196
  14.3 5.4 %collective-permute-start.7 = (bf16[96,256]{1,0:T(8,128)(2,1)S(1)}, bf16[96,256]{1,0:T(8,128)(2,1)S(1)}, u32[]{:S(2)}, u32[]{:S(2)}) collective-permute-start(bf16[96,256]{1,0:T(8,128)(2,1)S(1)} %get-tuple-element.51.refs_0_), channel_id=1, source_target_pairs={{0,4},{1,5},{2,6},{3,7},{4,0},{5,1},{6,2},{7,3},{8,12},{9,13},{10,... | collective-permute-start | bytes 147464 | tf_op jit(solution)/shard_map/ppermute | solution.py:435
  16.0 4.1 %collective-permute-start.8 = (bf16[96,256]{1,0:T(8,128)(2,1)S(1)}, bf16[96,256]{1,0:T(8,128)(2,1)S(1)}, u32[]{:S(2)}, u32[]{:S(2)}) collective-permute-start(bf16[96,256]{1,0:T(8,128)(2,1)S(1)} %get-tuple-element.55.refs_1_), channel_id=1, source_target_pairs={{0,4},{1,5},{2,6},{3,7},{4,0},{5,1},{6,2},{7,3},{8,12},{9,13},{10,... | collective-permute-start | bytes 147464 | tf_op jit(solution)/shard_map/ppermute | solution.py:435
  16.4 5.7 %collective-permute-start.6 = (bf16[160,256]{1,0:T(8,128)(2,1)S(1)}, bf16[160,256]{1,0:T(8,128)(2,1)S(1)}, u32[]{:S(2)}, u32[]{:S(2)}) collective-permute-start(bf16[160,256]{1,0:T(8,128)(2,1)S(1)} %get-tuple-element.52.first_ref), channel_id=1, source_target_pairs={{0,8},{1,9},{2,10},{3,11},{4,12},{5,13},{6,14},{7,15},{8,0},{9,1},... | collective-permute-start | bytes 245768 | tf_op jit(solution)/shard_map/ppermute | solution.py:435
  22.2 3.1 %collective-permute-start.9 = (bf16[256,128]{1,0:T(8,128)(2,1)S(1)}, bf16[256,128]{1,0:T(8,128)(2,1)S(1)}, u32[]{:S(2)}, u32[]{:S(2)}) collective-permute-start(bf16[256,128]{1,0:T(8,128)(2,1)S(1)} %get-tuple-element.57.own_key_ref), channel_id=1, source_target_pairs={{0,1},{1,0},{2,3},{3,2},{4,5},{5,4},{6,7},{7,6},{8,9},{9,8},{10,11... | collective-permute-start | bytes 196616 | tf_op jit(solution)/shard_map/ppermute | solution.py:435
  22.3 8.9 %collective-permute-start.10 = (bf16[192,256]{1,0:T(8,128)(2,1)S(1)}, bf16[192,256]{1,0:T(8,128)(2,1)S(1)}, u32[]{:S(2)}, u32[]{:S(2)}) collective-permute-start(bf16[192,256]{1,0:T(8,128)(2,1)S(1)} %shard_map.84.after_ref.sum_a), channel_id=1, source_target_pairs={{0,8},{1,9},{2,10},{3,11},{4,12},{5,13},{6,14},{7,15},{8,0},{9,1},... | collective-permute-start | bytes 294920 | tf_op jit(solution)/shard_map/ppermute | solution.py:435
  31.2 5.3 %collective-permute-start.11 = (bf16[192,256]{1,0:T(8,128)(2,1)S(1)}, bf16[192,256]{1,0:T(8,128)(2,1)S(1)}, u32[]{:S(2)}, u32[]{:S(2)}) collective-permute-start(bf16[192,256]{1,0:T(8,128)(2,1)S(1)} %shard_map.88.after_ref.own_ref), channel_id=1, source_target_pairs={{0,2},{1,3},{2,0},{3,1},{4,6},{5,7},{6,4},{7,5},{8,10},{9,11},{10,... | collective-permute-start | bytes 294920 | tf_op jit(solution)/shard_map/ppermute | solution.py:435
  36.5 1.9 %collective-permute-start.12 = (bf16[384,256]{1,0:T(8,128)(2,1)S(1)}, bf16[384,256]{1,0:T(8,128)(2,1)S(1)}, u32[]{:S(2)}, u32[]{:S(2)}) collective-permute-start(bf16[384,256]{1,0:T(8,128)(2,1)S(1)} %shard_map.90.after_ref.own_ref), channel_id=1, source_target_pairs={{0,1},{1,0},{2,3},{3,2},{4,5},{5,4},{6,7},{7,6},{8,9},{9,8},{10,11... | collective-permute-start | bytes 589832 | tf_op jit(solution)/shard_map/ppermute | solution.py:435

commit v9 on v8

--- a/solution.py
+++ b/solution.py
@@ -162,8 +162,11 @@
             attn = jnp.exp2((scores - row_max) * EXP2_SCALE)
             stat_ref[pl.ds(number, 1), :] = row_max
             stat_ref[pl.ds(CHUNKS + number, 1), :] = jnp.sum(attn, axis=0, keepdims=True)
-            attn_ref[:, c * CHUNK : (c + 1) * CHUNK] = attn.astype(bf16)
-        high, low = split(mm(value_ref[...], attn_ref[...], TN))
+            begin = (0 if out is send_ref else 2 * CHUNK) + c * CHUNK
+            attn_ref[:, begin : begin + CHUNK] = attn.astype(bf16)
+    sums = mm(value_ref[...], attn_ref[...], TN)
+    for i, out in enumerate((send_ref, keep_ref)):
+        high, low = split(sums[:, i * 2 * CHUNK : (i + 1) * 2 * CHUNK])
         out[PRIOR:SUM_ROWS, :] = high
         out[SUM_ROWS:, :] = low
     put_stats(send_head_ref, stat_ref[...])
@@ -459,7 +462,7 @@
             pltpu.VMEM((ctx, DH), bf16),
             pltpu.VMEM((NQ, DH), bf16),
             pltpu.VMEM((ctx, DH), bf16),
-            pltpu.VMEM((ctx, 2 * CHUNK), bf16),
+            pltpu.VMEM((ctx, NQ), bf16),
             pltpu.SemaphoreType.DMA((6,)),
         ],
     )

time: 44.2 us -> 44.1 us (level)
  no operation moved by 1% of the time
where the time goes in v9:
time: 44.1 us; the launch traced here: 43.9 us
  Pallas kernels  20.4 us (46%)
  starting transfers between devices  18 us (41%)
  waiting for transfers between devices  4.69 us (11%)
  between operations  0.77 us (2%)
    pallas_call x16, Pallas kernels, call(): pl.pallas_call(kernel, out_shape=tuple(outs), in_specs=in_specs or [pl.Bl...  20.4 us
    ppermute x13, starting transfers between devices, exchanged(): lax.ppermute(array, 'wide', [(i, i ^ mask) for i in range(wide_count)])  18 us
    ppermute x13, waiting for transfers between devices, exchanged(): lax.ppermute(array, 'wide', [(i, i ^ mask) for i in range(wide_count)])  4.69 us
  transfers between devices with their start and end apart: 13, of which 5 were waited for; matrix products, arithmetic and copies ran while one was open for 0% of the time, Pallas kernels for 26%

profile of v9, /device:TPU:0, one launch (start us, length us, event | category | flops | bytes accessed | tf_op | source)
XLA Modules:
  0.0 43.9 jit_solution(14224663089168415616)
XLA Ops:
  0.6 3.1 %shard_map.77 = (bf16[160,256]{1,0:T(8,128)(2,1)S(1)}, bf16[160,256]{1,0:T(8,128)(2,1)S(1)}, bf16[320,512]{1,0:T(8,128)(2,1)S(1)}, bf16[320,512]{1,0:T(8,128)(2,1)S(1)}) custom-call(s32[16]{0:T(128)} %len_ref.1, s32[32]{0:T(128)} %exp_hbm.1, s32[1,512]{1,0:T(1,128)} %bitcast.2, bf16[1024,128]{1,0:T(8,128)(2,1)} %mant_hbm.1, bf16[1024,128]{1,0:T(8,128)(2,1)} %value_hbm.1, ...), custom_call_target="tpu_custom_call" | custom-call | flops 1000000000 | bytes 1024 | tf_op jit(solution)/shard_map/pallas_call | solution.py:418
  3.7 0.5 %collective-permute-start = (bf16[160,256]{1,0:T(8,128)(2,1)S(1)}, bf16[160,256]{1,0:T(8,128)(2,1)S(1)}, u32[]{:S(2)}, u32[]{:S(2)}) collective-permute-start(bf16[160,256]{1,0:T(8,128)(2,1)S(1)} %get-tuple-element.39), channel_id=1, source_target_pairs={{0,1},{1,0},{2,3},{3,2},{4,5},{5,4},{6,7},{7,6},{8,9},{9,8},{10,11... | collective-permute-start | bytes 245768 | tf_op jit(solution)/shard_map/ppermute | solution.py:438
  4.2 0.9 %collective-permute-done.second_ref = bf16[160,256]{1,0:T(8,128)(2,1)S(1)} collective-permute-done((bf16[160,256]{1,0:T(8,128)(2,1)S(1)}, bf16[160,256]{1,0:T(8,128)(2,1)S(1)}, u32[]{:S(2)}, u32[]{:S(2)}) %collective-permute-start) | collective-permute-done | bytes 81952 | tf_op jit(solution)/shard_map/ppermute | solution.py:438
  5.2 0.4 collective-permute-start.2
  5.6 2.7 %collective-permute-start.1 = (bf16[160,256]{1,0:T(8,128)(2,1)S(1)}, bf16[160,256]{1,0:T(8,128)(2,1)S(1)}, u32[]{:S(2)}, u32[]{:S(2)}) collective-permute-start(bf16[160,256]{1,0:T(8,128)(2,1)S(1)} %get-tuple-element.40.after_ref.first_ref), channel_id=1, source_target_pairs={{0,2},{1,3},{2,0},{3,1},{4,6},{5,7},{6,4},{7,5},{8,10},{9,11},{10,... | collective-permute-start | bytes 245768 | tf_op jit(solution)/shard_map/ppermute | solution.py:438
  8.3 0.0 collective-permute-done.2.sum_b
  8.3 0.1 shard_map.80
  8.4 1.5 %collective-permute-start.4 = (bf16[96,256]{1,0:T(8,128)(2,1)S(1)}, bf16[96,256]{1,0:T(8,128)(2,1)S(1)}, u32[]{:S(2)}, u32[]{:S(2)}) collective-permute-start(bf16[96,256]{1,0:T(8,128)(2,1)S(1)} %get-tuple-element.45.refs_0_), channel_id=1, source_target_pairs={{0,2},{1,3},{2,0},{3,1},{4,6},{5,7},{6,4},{7,5},{8,10},{9,11},{10,... | collective-permute-start | bytes 147464 | tf_op jit(solution)/shard_map/ppermute | solution.py:438
  10.0 0.6 %collective-permute-start.5 = (bf16[96,256]{1,0:T(8,128)(2,1)S(1)}, bf16[96,256]{1,0:T(8,128)(2,1)S(1)}, u32[]{:S(2)}, u32[]{:S(2)}) collective-permute-start(bf16[96,256]{1,0:T(8,128)(2,1)S(1)} %get-tuple-element.50), channel_id=1, source_target_pairs={{0,2},{1,3},{2,0},{3,1},{4,6},{5,7},{6,4},{7,5},{8,10},{9,11},{10,... | collective-permute-start | bytes 147464 | tf_op jit(solution)/shard_map/ppermute | solution.py:438
  10.5 0.8 %collective-permute-done.1.second_ref = bf16[160,256]{1,0:T(8,128)(2,1)S(1)} collective-permute-done((bf16[160,256]{1,0:T(8,128)(2,1)S(1)}, bf16[160,256]{1,0:T(8,128)(2,1)S(1)}, u32[]{:S(2)}, u32[]{:S(2)}) %collective-permute-start.1) | collective-permute-done | bytes 81952 | tf_op jit(solution)/shard_map/ppermute | solution.py:438
  11.4 2.1 %collective-permute-start.3 = (bf16[160,256]{1,0:T(8,128)(2,1)S(1)}, bf16[160,256]{1,0:T(8,128)(2,1)S(1)}, u32[]{:S(2)}, u32[]{:S(2)}) collective-permute-start(bf16[160,256]{1,0:T(8,128)(2,1)S(1)} %get-tuple-element.46.first_ref), channel_id=1, source_target_pairs={{0,4},{1,5},{2,6},{3,7},{4,0},{5,1},{6,2},{7,3},{8,12},{9,13},{10,... | collective-permute-start | bytes 245768 | tf_op jit(solution)/shard_map/ppermute | solution.py:438
  13.5 0.0 collective-permute-done.4.refs_1_
  13.5 0.6 %collective-permute-done.5.refs_2_ = bf16[96,256]{1,0:T(8,128)(2,1)S(1)} collective-permute-done((bf16[96,256]{1,0:T(8,128)(2,1)S(1)}, bf16[96,256]{1,0:T(8,128)(2,1)S(1)}, u32[]{:S(2)}, u32[]{:S(2)}) %collective-permute-start.5) | collective-permute-done | bytes 49184 | tf_op jit(solution)/shard_map/ppermute | solution.py:438
  14.1 0.0 copy-start
  14.1 0.0 copy-start.1
  14.1 1.7 %collective-permute-start.7 = (bf16[96,256]{1,0:T(8,128)(2,1)S(1)}, bf16[96,256]{1,0:T(8,128)(2,1)S(1)}, u32[]{:S(2)}, u32[]{:S(2)}) collective-permute-start(bf16[96,256]{1,0:T(8,128)(2,1)S(1)} %get-tuple-element.51.refs_0_), channel_id=1, source_target_pairs={{0,4},{1,5},{2,6},{3,7},{4,0},{5,1},{6,2},{7,3},{8,12},{9,13},{10,... | collective-permute-start | bytes 147464 | tf_op jit(solution)/shard_map/ppermute | solution.py:438
  15.8 0.4 collective-permute-start.8
  16.2 0.0 collective-permute-done.3.second_ref
  16.3 3.3 %collective-permute-start.6 = (bf16[160,256]{1,0:T(8,128)(2,1)S(1)}, bf16[160,256]{1,0:T(8,128)(2,1)S(1)}, u32[]{:S(2)}, u32[]{:S(2)}) collective-permute-start(bf16[160,256]{1,0:T(8,128)(2,1)S(1)} %get-tuple-element.52.first_ref), channel_id=1, source_target_pairs={{0,8},{1,9},{2,10},{3,11},{4,12},{5,13},{6,14},{7,15},{8,0},{9,1},... | collective-permute-start | bytes 245768 | tf_op jit(solution)/shard_map/ppermute | solution.py:438
  19.6 0.0 collective-permute-done.7.refs_2_
  19.6 0.3 collective-permute-done.8.refs_3_
  19.9 2.1 %collective-permute-done.6.second_ref = bf16[160,256]{1,0:T(8,128)(2,1)S(1)} collective-permute-done((bf16[160,256]{1,0:T(8,128)(2,1)S(1)}, bf16[160,256]{1,0:T(8,128)(2,1)S(1)}, u32[]{:S(2)}, u32[]{:S(2)}) %collective-permute-start.6) | collective-permute-done | bytes 81952 | tf_op jit(solution)/shard_map/ppermute | solution.py:438
  22.0 0.1 collective-permute-start.9
  22.1 3.0 %collective-permute-start.10 = (bf16[192,256]{1,0:T(8,128)(2,1)S(1)}, bf16[192,256]{1,0:T(8,128)(2,1)S(1)}, u32[]{:S(2)}, u32[]{:S(2)}) collective-permute-start(bf16[192,256]{1,0:T(8,128)(2,1)S(1)} %shard_map.84.after_ref.sum_a), channel_id=1, source_target_pairs={{0,8},{1,9},{2,10},{3,11},{4,12},{5,13},{6,14},{7,15},{8,0},{9,1},... | collective-permute-start | bytes 294920 | tf_op jit(solution)/shard_map/ppermute | solution.py:438
  25.1 0.0 collective-permute-done.9.other_key_ref
  25.1 0.0 copy-done
  25.1 0.0 copy-done.1
  25.2 2.9 %shard_map.86 = (f32[512,512]{1,0:T(8,128)S(1)}, f32[512,128]{1,0:T(8,128)S(1)}, f32[8,128]{1,0:T(8,128)S(1)}, bf16[512,1024]{1,0:T(8,128)(2,1)S(1)}, bf16[512,1024]{1,0:T(8,128)(2,1)S(1)}) custom-call(s32[16]{0:T(128)S(1)} %copy-done.1, bf16[1024,128]{1,0:T(8,128)(2,1)S(1)} %copy-done, f32[8,256]{1,0:T(8,128)S(1)} %get-tuple-element.56.stat_ref, ...), custom_call_target="tpu_custom_call" | custom-call | flops 1000000000 | bytes 1024 | tf_op jit(solution)/shard_map/pallas_call | solution.py:418
  28.1 2.9 %shard_map.87 = (f32[1,512]{1,0:T(1,128)}, f32[8,512]{1,0:T(8,128)S(1)}, f32[512,512]{1,0:T(8,128)S(1)}) custom-call(f32[512,512]{1,0:T(8,128)S(1)} %get-tuple-element.58.gram_ref, f32[512,128]{1,0:T(8,128)S(1)} %get-tuple-element.59.linear_ref, f32[8,128]{1,0:T(8,128)S(1)} %get-tuple-element.60.norm_ref, bf16[512,1024]{1,0:T(8,128)(2,1)S(1)} %get-tuple-element.61.scaled_hi, ...), custom_call_target="tpu_custom_call" | custom-call | flops 5000000000 | bytes 1024 | tf_op jit(solution)/shard_map/pallas_call | solution.py:418
  31.0 0.0 collective-permute-done.10.sum_b
  31.0 1.6 %collective-permute-start.11 = (bf16[192,256]{1,0:T(8,128)(2,1)S(1)}, bf16[192,256]{1,0:T(8,128)(2,1)S(1)}, u32[]{:S(2)}, u32[]{:S(2)}) collective-permute-start(bf16[192,256]{1,0:T(8,128)(2,1)S(1)} %shard_map.88.after_ref.own_ref), channel_id=1, source_target_pairs={{0,2},{1,3},{2,0},{3,1},{4,6},{5,7},{6,4},{7,5},{8,10},{9,11},{10,... | collective-permute-start | bytes 294920 | tf_op jit(solution)/shard_map/ppermute | solution.py:438
  32.6 3.8 %shard_map.89 = (bf16[2048,512]{1,0:T(8,128)(2,1)S(1)}, bf16[2048,512]{1,0:T(8,128)(2,1)S(1)}, f32[512,512]{1,0:T(8,128)S(1)}) custom-call(f32[512,512]{1,0:T(8,128)S(1)} %get-tuple-element.64.power_in, bf16[192,256]{1,0:T(8,128)(2,1)S(1)} %shard_map.88.after_ref.own_ref), custom_call_target="tpu_custom_call" | custom-call | flops 4000000000 | bytes 1024 | tf_op jit(solution)/shard_map/pallas_call | solution.py:418
  36.3 0.0 collective-permute-done.11.side_ref
  36.4 0.1 collective-permute-start.12
  36.4 1.8 %shard_map.91 = (bf16[1024,512]{1,0:T(8,128)(2,1)S(1)}, bf16[1024,512]{1,0:T(8,128)(2,1)S(1)}, f32[512,512]{1,0:T(8,128)S(1)}) custom-call(f32[512,512]{1,0:T(8,128)S(1)} %get-tuple-element.70.after_ref.power_in, bf16[384,256]{1,0:T(8,128)(2,1)S(1)} %shard_map.90.after_ref.own_ref), custom_call_target="tpu_custom_call" | custom-call | flops 2000000000 | bytes 1024 | tf_op jit(solution)/shard_map/pallas_call | solution.py:418
  38.3 0.0 collective-permute-done.12.half_ref
  38.3 5.6 %shard_map.92 = f32[512,128]{1,0:T(8,128)} custom-call(bf16[2048,512]{1,0:T(8,128)(2,1)S(1)} %get-tuple-element.68.early_hi, bf16[2048,512]{1,0:T(8,128)(2,1)S(1)} %get-tuple-element.69.early_lo, bf16[1024,512]{1,0:T(8,128)(2,1)S(1)} %get-tuple-element.71.late_hi, bf16[1024,512]{1,0:T(8,128)(2,1)S(1)} %get-tuple-element.72.late_lo, ...), custom_call_target="tpu_custom_call" | custom-call | tf_op jit(solution)/shard_map/pallas_call | solution.py:418
  (9 shorter events, 0.3 us)
Async XLA Ops:
  3.7 1.4 %collective-permute-start = (bf16[160,256]{1,0:T(8,128)(2,1)S(1)}, bf16[160,256]{1,0:T(8,128)(2,1)S(1)}, u32[]{:S(2)}, u32[]{:S(2)}) collective-permute-start(bf16[160,256]{1,0:T(8,128)(2,1)S(1)} %get-tuple-element.39), channel_id=1, source_target_pairs={{0,1},{1,0},{2,3},{3,2},{4,5},{5,4},{6,7},{7,6},{8,9},{9,8},{10,11... | collective-permute-start | bytes 245768 | tf_op jit(solution)/shard_map/ppermute | solution.py:438
  5.2 3.1 %collective-permute-start.2 = (bf16[320,512]{1,0:T(8,128)(2,1)S(1)}, bf16[320,512]{1,0:T(8,128)(2,1)S(1)}, u32[]{:S(2)}, u32[]{:S(2)}) collective-permute-start(bf16[320,512]{1,0:T(8,128)(2,1)S(1)} %shard_map.79), channel_id=1, source_target_pairs={{0,1},{1,0},{2,3},{3,2},{4,5},{5,4},{6,7},{7,6},{8,9},{9,8},{10,11... | collective-permute-start | bytes 983048 | tf_op jit(solution)/shard_map/ppermute | solution.py:438
  5.6 5.7 %collective-permute-start.1 = (bf16[160,256]{1,0:T(8,128)(2,1)S(1)}, bf16[160,256]{1,0:T(8,128)(2,1)S(1)}, u32[]{:S(2)}, u32[]{:S(2)}) collective-permute-start(bf16[160,256]{1,0:T(8,128)(2,1)S(1)} %get-tuple-element.40.after_ref.first_ref), channel_id=1, source_target_pairs={{0,2},{1,3},{2,0},{3,1},{4,6},{5,7},{6,4},{7,5},{8,10},{9,11},{10,... | collective-permute-start | bytes 245768 | tf_op jit(solution)/shard_map/ppermute | solution.py:438
  8.4 5.1 %collective-permute-start.4 = (bf16[96,256]{1,0:T(8,128)(2,1)S(1)}, bf16[96,256]{1,0:T(8,128)(2,1)S(1)}, u32[]{:S(2)}, u32[]{:S(2)}) collective-permute-start(bf16[96,256]{1,0:T(8,128)(2,1)S(1)} %get-tuple-element.45.refs_0_), channel_id=1, source_target_pairs={{0,2},{1,3},{2,0},{3,1},{4,6},{5,7},{6,4},{7,5},{8,10},{9,11},{10,... | collective-permute-start | bytes 147464 | tf_op jit(solution)/shard_map/ppermute | solution.py:438
  10.0 4.1 %collective-permute-start.5 = (bf16[96,256]{1,0:T(8,128)(2,1)S(1)}, bf16[96,256]{1,0:T(8,128)(2,1)S(1)}, u32[]{:S(2)}, u32[]{:S(2)}) collective-permute-start(bf16[96,256]{1,0:T(8,128)(2,1)S(1)} %get-tuple-element.50), channel_id=1, source_target_pairs={{0,2},{1,3},{2,0},{3,1},{4,6},{5,7},{6,4},{7,5},{8,10},{9,11},{10,... | collective-permute-start | bytes 147464 | tf_op jit(solution)/shard_map/ppermute | solution.py:438
  11.4 4.9 %collective-permute-start.3 = (bf16[160,256]{1,0:T(8,128)(2,1)S(1)}, bf16[160,256]{1,0:T(8,128)(2,1)S(1)}, u32[]{:S(2)}, u32[]{:S(2)}) collective-permute-start(bf16[160,256]{1,0:T(8,128)(2,1)S(1)} %get-tuple-element.46.first_ref), channel_id=1, source_target_pairs={{0,4},{1,5},{2,6},{3,7},{4,0},{5,1},{6,2},{7,3},{8,12},{9,13},{10,... | collective-permute-start | bytes 245768 | tf_op jit(solution)/shard_map/ppermute | solution.py:438
  14.1 11.0 %copy-start = (bf16[1024,128]{1,0:T(8,128)(2,1)S(1)}, bf16[1024,128]{1,0:T(8,128)(2,1)}, u32[]{:S(2)}) copy-start(bf16[1024,128]{1,0:T(8,128)(2,1)} %query_ref.1) | copy-start | bytes 786436
  14.1 11.0 %copy-start.1 = (s32[16]{0:T(128)S(1)}, s32[16]{0:T(128)}, u32[]{:S(2)}) copy-start(s32[16]{0:T(128)} %len_ref.1) | copy-start | bytes 196
  14.1 5.4 %collective-permute-start.7 = (bf16[96,256]{1,0:T(8,128)(2,1)S(1)}, bf16[96,256]{1,0:T(8,128)(2,1)S(1)}, u32[]{:S(2)}, u32[]{:S(2)}) collective-permute-start(bf16[96,256]{1,0:T(8,128)(2,1)S(1)} %get-tuple-element.51.refs_0_), channel_id=1, source_target_pairs={{0,4},{1,5},{2,6},{3,7},{4,0},{5,1},{6,2},{7,3},{8,12},{9,13},{10,... | collective-permute-start | bytes 147464 | tf_op jit(solution)/shard_map/ppermute | solution.py:438
  15.8 4.1 %collective-permute-start.8 = (bf16[96,256]{1,0:T(8,128)(2,1)S(1)}, bf16[96,256]{1,0:T(8,128)(2,1)S(1)}, u32[]{:S(2)}, u32[]{:S(2)}) collective-permute-start(bf16[96,256]{1,0:T(8,128)(2,1)S(1)} %get-tuple-element.55.refs_1_), channel_id=1, source_target_pairs={{0,4},{1,5},{2,6},{3,7},{4,0},{5,1},{6,2},{7,3},{8,12},{9,13},{10,... | collective-permute-start | bytes 147464 | tf_op jit(solution)/shard_map/ppermute | solution.py:438
  16.3 5.7 %collective-permute-start.6 = (bf16[160,256]{1,0:T(8,128)(2,1)S(1)}, bf16[160,256]{1,0:T(8,128)(2,1)S(1)}, u32[]{:S(2)}, u32[]{:S(2)}) collective-permute-start(bf16[160,256]{1,0:T(8,128)(2,1)S(1)} %get-tuple-element.52.first_ref), channel_id=1, source_target_pairs={{0,8},{1,9},{2,10},{3,11},{4,12},{5,13},{6,14},{7,15},{8,0},{9,1},... | collective-permute-start | bytes 245768 | tf_op jit(solution)/shard_map/ppermute | solution.py:438
  22.0 3.1 %collective-permute-start.9 = (bf16[256,128]{1,0:T(8,128)(2,1)S(1)}, bf16[256,128]{1,0:T(8,128)(2,1)S(1)}, u32[]{:S(2)}, u32[]{:S(2)}) collective-permute-start(bf16[256,128]{1,0:T(8,128)(2,1)S(1)} %get-tuple-element.57.own_key_ref), channel_id=1, source_target_pairs={{0,1},{1,0},{2,3},{3,2},{4,5},{5,4},{6,7},{7,6},{8,9},{9,8},{10,11... | collective-permute-start | bytes 196616 | tf_op jit(solution)/shard_map/ppermute | solution.py:438
  22.1 8.9 %collective-permute-start.10 = (bf16[192,256]{1,0:T(8,128)(2,1)S(1)}, bf16[192,256]{1,0:T(8,128)(2,1)S(1)}, u32[]{:S(2)}, u32[]{:S(2)}) collective-permute-start(bf16[192,256]{1,0:T(8,128)(2,1)S(1)} %shard_map.84.after_ref.sum_a), channel_id=1, source_target_pairs={{0,8},{1,9},{2,10},{3,11},{4,12},{5,13},{6,14},{7,15},{8,0},{9,1},... | collective-permute-start | bytes 294920 | tf_op jit(solution)/shard_map/ppermute | solution.py:438
  31.0 5.3 %collective-permute-start.11 = (bf16[192,256]{1,0:T(8,128)(2,1)S(1)}, bf16[192,256]{1,0:T(8,128)(2,1)S(1)}, u32[]{:S(2)}, u32[]{:S(2)}) collective-permute-start(bf16[192,256]{1,0:T(8,128)(2,1)S(1)} %shard_map.88.after_ref.own_ref), channel_id=1, source_target_pairs={{0,2},{1,3},{2,0},{3,1},{4,6},{5,7},{6,4},{7,5},{8,10},{9,11},{10,... | collective-permute-start | bytes 294920 | tf_op jit(solution)/shard_map/ppermute | solution.py:438
  36.4 1.9 %collective-permute-start.12 = (bf16[384,256]{1,0:T(8,128)(2,1)S(1)}, bf16[384,256]{1,0:T(8,128)(2,1)S(1)}, u32[]{:S(2)}, u32[]{:S(2)}) collective-permute-start(bf16[384,256]{1,0:T(8,128)(2,1)S(1)} %shard_map.90.after_ref.own_ref), channel_id=1, source_target_pairs={{0,1},{1,0},{2,3},{3,2},{4,5},{5,4},{6,7},{7,6},{8,9},{9,8},{10,11... | collective-permute-start | bytes 589832 | tf_op jit(solution)/shard_map/ppermute | solution.py:438
